TPU v7x, 512 devices: a whole 4x8x8 slice. The times are simulated.
512 devices in a mesh: gx: 32 (over z, y_lo), gy: 16 (over x, y_hi, core).
Axes of the slice: x: 4, y: 8 (y_hi: 2, y_lo: 4; y = y_hi * 4 + y_lo), z: 8, core: 2. Of those that a mesh axis runs over, the one named last changes fastest.
Arguments:
- fields: bfloat16 [8, 128, 128, 256], P(None, 'gx', 'gy'), may hold values from -6 to 6
- cotangent: bfloat16 [8, 128, 128, 256], P(None, 'gx', 'gy'), may hold values from -6 to 6
- w_down: bfloat16 [3, 3, 3, 32, 8], replicated, may hold values from -0.4375 to 0.4375
- w_mid: bfloat16 [3, 3, 3, 32, 32], replicated, may hold values from -0.21875 to 0.21875
- w_up: bfloat16 [3, 3, 3, 8, 32], replicated, may hold values from -0.5 to 0.5
Outputs:
- mapped: bfloat16 [8, 128, 128, 256], P(None, 'gx', 'gy')
- grad_fields: bfloat16 [8, 128, 128, 256], P(None, 'gx', 'gy')
- grad_w_down: float32 [3, 3, 3, 32, 8], replicated
- grad_w_mid: float32 [3, 3, 3, 32, 32], replicated
- grad_w_up: float32 [3, 3, 3, 8, 32], replicated
All inputs are finite; a program needn't handle non-finite values.
Results may differ from a plain program's by a relative error of at most 0.0052.
Values may be sent and summed in bfloat16 or wider, within the bound.
No kernel may reach another device: no remote copies, remote signals or barrier semaphores. Data moves between devices by JAX's collectives and lax.ppermute only.
A program may use at most 128 MiB of HBM per device.

v0:
```python
import jax
import jax.numpy as jnp
from jax import lax
from jax.sharding import PartitionSpec as P


def from_behind(x, axis, by):
    devices = lax.axis_size(axis)
    return lax.ppermute(x, axis, [(i, (i + by) % devices) for i in range(devices)])


def padded_2(x, sides, width):
    for axis, dim in sides:
        devices, length = (lax.axis_size(axis), x.shape[dim])
        up = [(i, (i + 1) % devices) for i in range(devices)]
        down = [(j, i) for i, j in up]
        last = lax.slice_in_dim(x, length - width, length, axis=dim)
        initial = lax.slice_in_dim(x, 0, width, axis=dim)
        before = lax.ppermute(last, axis, up)
        after = lax.ppermute(initial, axis, down)
        x = jnp.concatenate([before, x, after], axis=dim)
    return x


def act(v):
    return 0.2 * v + 0.8 * v * jax.nn.sigmoid(v)


def slope(v):
    s = jax.nn.sigmoid(v)
    return 0.2 + 0.8 * (s + v * s * (1.0 - s))


def low_rim(x):
    got = from_behind(x[:, -1:], "gx", 1)
    ext = jnp.concatenate([got, x], 1)
    got = from_behind(ext[:, :, -1:], "gy", 1)
    return jnp.concatenate([got, ext], 2)


def faces(x):
    return padded_2(x, (("gx", 1), ("gy", 2)), 1)


def strided_set(ext):
    chans = ext.shape[0]
    half_x = (ext.shape[1] - 1) // 2
    half_y = (ext.shape[2] - 1) // 2
    half_z = ext.shape[3] // 2
    padded = jnp.pad(ext, ((0, 0), (0, 1), (0, 1), (0, 0)))
    shaped = padded.reshape(chans, half_x + 1, 2, half_y + 1, 2, half_z, 2)
    phases = jnp.transpose(shaped, (6, 2, 4, 0, 1, 3, 5))
    even = phases[0]
    odd = phases[1]
    rolled = jnp.roll(odd, 1, axis=-1)
    return (jnp.stack([rolled, even, odd], 0), half_x, half_y)


def strided_piece(data, a, b, d):
    arr, half_x, half_y = data
    return arr[d, a % 2, b % 2, :, a // 2 : a // 2 + half_x, b // 2 : b // 2 + half_y]


def stencil_set(ext):
    stacked = jnp.stack([jnp.roll(ext, 1, axis=-1), ext, jnp.roll(ext, -1, axis=-1)], 0)
    return (stacked, ext.shape[1] - 2, ext.shape[2] - 2)


def stencil_piece(data, a, b, d):
    arr, inner_x, inner_y = data
    return arr[d, :, a : a + inner_x, b : b + inner_y]


def tap_groups(chans):
    groups = 1 if 27 * chans <= 256 else 3
    per_group = 27 // groups
    result = []
    for g in range(groups):
        result.append(
            [(t // 9, t // 3 % 3, t % 3) for t in range(g * per_group, (g + 1) * per_group)]
        )
    return result


def apply_taps(data, weight, picker):
    chans = weight.shape[4]
    total = None
    for group in tap_groups(chans):
        stacked = jnp.concatenate([picker(data, a, b, d) for a, b, d in group], 0)
        kernel = jnp.concatenate([weight[a, b, d] for a, b, d in group], 1)
        term = jnp.einsum("ok,kxyz->oxyz", kernel, stacked, preferred_element_type=jnp.float32)
        total = term if total is None else total + term
    return total


def tap_grads(data, cot, picker):
    chans = data[0].shape[-4]
    outer = cot.shape[0]
    parts = []
    for group in tap_groups(chans):
        stacked = jnp.concatenate([picker(data, a, b, d) for a, b, d in group], 0)
        block = jnp.einsum("pxyz,kxyz->pk", cot, stacked, preferred_element_type=jnp.float32)
        parts.append(block.reshape(outer, len(group), chans))
    joined = jnp.concatenate(parts, 1)
    return jnp.transpose(joined, (1, 0, 2)).reshape(3, 3, 3, outer, chans)


def spread(source, weight):
    outs = weight.shape[3]
    padded = jnp.pad(source, ((0, 0), (1, 1), (1, 1), (0, 0)))
    rolled = jnp.roll(padded, -1, axis=-1)
    nx, ny, nz = (source.shape[1], source.shape[2], source.shape[3])
    taps = (((0, 1), (2, 0)), ((1, 1),))
    z_taps = (((1, padded),), ((0, rolled), (2, padded)))
    by_p = []
    for p in range(2):
        by_q = []
        for q in range(2):
            by_r = []
            for r in range(2):
                pieces = []
                mats = []
                for a, start_a in taps[p]:
                    for b, start_b in taps[q]:
                        for d, anchor in z_taps[r]:
                            pieces.append(
                                anchor[:, start_a : start_a + nx + 1, start_b : start_b + ny + 1, :]
                            )
                            mats.append(weight[a, b, d])
                stacked = jnp.concatenate(pieces, 0)
                kernel = jnp.concatenate(mats, 1)
                by_r.append(
                    jnp.einsum("ok,kxyz->oxyz", kernel, stacked, preferred_element_type=jnp.float32)
                )
            by_q.append(jnp.stack(by_r, -1))
        by_p.append(jnp.stack(by_q, -2))
    phased = jnp.stack(by_p, -3)
    arranged = jnp.transpose(phased, (0, 1, 4, 2, 5, 3, 6)).reshape(
        outs, 2 * nx + 2, 2 * ny + 2, 2 * nz
    )
    return arranged[:, : 2 * nx + 1, : 2 * ny + 1, :]


def upsample(hidden, weight):
    nx, ny = (hidden.shape[1], hidden.shape[2])
    got = from_behind(hidden[:, :1], "gx", -1)
    ext = jnp.concatenate([hidden, got], 1)
    got = from_behind(ext[:, :, :1], "gy", -1)
    ext = jnp.concatenate([ext, got], 2)
    full = spread(ext, weight)
    return full[:, 1 : 2 * nx + 1, 1 : 2 * ny + 1, :]


def local(fields, cotangent, w_down, w_mid, w_up):
    field_ext = low_rim(fields)
    field_set = strided_set(field_ext)
    h1_pre = apply_taps(field_set, w_down, strided_piece)
    h1 = act(h1_pre).astype(jnp.bfloat16)
    h1_set = stencil_set(faces(h1))
    h2_pre = apply_taps(h1_set, w_mid, stencil_piece)
    h2 = act(h2_pre).astype(jnp.bfloat16)
    lifted = upsample(h2, w_up)
    mapped = (fields.astype(jnp.float32) + lifted).astype(jnp.bfloat16)
    cot_ext = low_rim(cotangent)
    cot_set = strided_set(cot_ext)
    dh2 = apply_taps(cot_set, jnp.swapaxes(w_up, 3, 4), strided_piece)
    dh2_pre = (dh2 * slope(h2_pre)).astype(jnp.bfloat16)
    dh2_set = stencil_set(faces(dh2_pre))
    flipped = jnp.swapaxes(w_mid[::-1, ::-1, ::-1], 3, 4)
    dh1 = apply_taps(dh2_set, flipped, stencil_piece)
    dh1_pre = (dh1 * slope(h1_pre)).astype(jnp.bfloat16)
    back = upsample(dh1_pre, jnp.swapaxes(w_down, 3, 4))
    grad_fields = (cotangent.astype(jnp.float32) + back).astype(jnp.bfloat16)
    local_down = tap_grads(field_set, dh1_pre, strided_piece)
    local_mid = tap_grads(h1_set, dh2_pre, stencil_piece)
    local_up = jnp.swapaxes(tap_grads(cot_set, h2, strided_piece), 3, 4)
    grad_w_down, grad_w_mid, grad_w_up = lax.psum((local_down, local_mid, local_up), ("gx", "gy"))
    return (mapped, grad_fields, grad_w_down, grad_w_mid, grad_w_up)


def solution(mesh):
    in_specs = (P(None, "gx", "gy", None), P(None, "gx", "gy", None), P(), P(), P())
    out_specs = (P(None, "gx", "gy", None), P(None, "gx", "gy", None), P(), P(), P())
    return jax.shard_map(local, mesh=mesh, in_specs=in_specs, out_specs=out_specs, check_vma=False)
```

profile of v0, /device:TPU:1, one launch (start us, length us, event | category | flops | bytes accessed | tf_op | source)
XLA Modules:
  0.0 395.7 jit_solution(6905506190882616361)
XLA Ops:
  8.0 4.0 %collective-permute-start.8 = (bf16[8,1,8,256]{3,2,1,0:T(8,128)(2,1)S(1)}, bf16[8,1,8,256]{3,2,1,0:T(8,128)(2,1)S(1)}, u32[]{:S(2)}, u32[]{:S(2)}) collective-permute-start(bf16[8,1,8,256]{3,2,1,0:T(8,128)(2,1)S(1)} %slice.1336), channel_id=1, source_target_pairs={{0,16},{16,32},{32,48},{48,64},{64,80},{80,96},{96,112},{112,128},... | collective-permute-start | bytes 98312 | tf_op jit(solution)/shard_map/ppermute | solution.py:9
  12.8 3.2 collective-permute-start
  24.1 2.4 copy.78
  26.5 2.4 copy.72
  36.7 6.8 %collective-permute-start.9 = (bf16[8,5,1,256]{3,2,1,0:T(2,128)(2,1)S(1)}, bf16[8,5,1,256]{3,2,1,0:T(2,128)(2,1)S(1)}, u32[]{:S(2)}, u32[]{:S(2)}) collective-permute-start(bf16[8,5,1,256]{3,2,1,0:T(2,128)(2,1)S(1)} %slice.1569), channel_id=1, source_target_pairs={{0,1},{1,2},{2,3},{3,4},{4,5},{5,6},{6,7},{7,8},{8,9},{9,10},{10,1... | collective-permute-start | bytes 61448 | tf_op jit(solution)/shard_map/ppermute | solution.py:9
  43.6 1.9 collective-permute-start.1
  45.7 2.1 copy.149
  47.8 3.0 pad.16.clone
  50.8 7.2 %copy.76 = bf16[8,3,2,5,2,128,2]{5,0,3,1,4,2,6:T(8,128)(2,1)S(1)} copy(bf16[8,3,2,5,2,128,2]{0,6,5,4,3,2,1:T(2,128)(2,1)} %bitcast.1000) | data formatting | bytes 491520 | tf_op jit(solution)/shard_map/reshape | solution.py:51
  60.2 2.1 copy.148
  62.3 3.0 pad.14.clone
  65.3 7.2 %copy.70 = bf16[8,3,2,5,2,128,2]{5,0,3,1,4,2,6:T(8,128)(2,1)S(1)} copy(bf16[8,3,2,5,2,128,2]{0,6,5,4,3,2,1:T(2,128)(2,1)} %bitcast.999) | data formatting | bytes 491520 | tf_op jit(solution)/shard_map/reshape | solution.py:51
  73.4 2.3 collective-permute-start.2
  75.8 9.3 %collective-permute-start.3 = (bf16[32,1,4,128]{3,0,2,1:T(8,128)(2,1)S(1)}, bf16[32,1,4,128]{3,0,2,1:T(8,128)(2,1)S(1)}, u32[]{:S(2)}, u32[]{:S(2)}) collective-permute-start(bf16[32,1,4,128]{3,0,2,1:T(8,128)(2,1)S(1)} %get-tuple-element.184), channel_id=1, source_target_pairs={{16,0},{32,16},{48,32},{64,48},{80,64},{96,80},{112,96},{128,112},... | collective-permute-start | bytes 98312 | tf_op jit(solution)/shard_map/ppermute | solution.py:20
  86.1 8.0 %collective-permute-start.4 = (bf16[32,4,1,128]{3,0,2,1:T(8,128)(2,1)S(1)}, bf16[32,4,1,128]{3,0,2,1:T(8,128)(2,1)S(1)}, u32[]{:S(2)}, u32[]{:S(2)}) collective-permute-start(bf16[32,4,1,128]{3,0,2,1:T(8,128)(2,1)S(1)} %get-tuple-element.169), channel_id=1, source_target_pairs={{0,1},{1,2},{2,3},{3,4},{4,5},{5,6},{6,7},{7,8},{8,9},{9,10},{10,1... | collective-permute-start | bytes 98312 | tf_op jit(solution)/shard_map/ppermute | solution.py:19
  94.1 1.9 collective-permute-start.5
  96.0 7.2 %collective-permute-done.5 = bf16[32,4,1,128]{3,0,2,1:T(8,128)(2,1)S(1)} collective-permute-done((bf16[32,4,1,128]{3,0,2,1:T(8,128)(2,1)S(1)}, bf16[32,4,1,128]{3,0,2,1:T(8,128)(2,1)S(1)}, u32[]{:S(2)}, u32[]{:S(2)}) %collective-permute-start.5) | collective-permute-done | bytes 32800 | tf_op jit(solution)/shard_map/ppermute | solution.py:20
  106.7 7.9 %collective-permute-start.6 = (bf16[32,1,4,128]{3,0,2,1:T(8,128)(2,1)S(1)}, bf16[32,1,4,128]{3,0,2,1:T(8,128)(2,1)S(1)}, u32[]{:S(2)}, u32[]{:S(2)}) collective-permute-start(bf16[32,1,4,128]{3,0,2,1:T(8,128)(2,1)S(1)} %slice.1521), channel_id=1, source_target_pairs={{0,496},{16,0},{32,16},{48,32},{64,48},{80,64},{96,80},{112,96},{1... | collective-permute-start | bytes 98312 | tf_op jit(solution)/shard_map/ppermute | solution.py:9
  115.6 1.9 collective-permute-start.10
  117.5 7.3 %collective-permute-start.11 = (bf16[32,1,4,128]{3,0,2,1:T(8,128)(2,1)S(1)}, bf16[32,1,4,128]{3,0,2,1:T(8,128)(2,1)S(1)}, u32[]{:S(2)}, u32[]{:S(2)}) collective-permute-start(bf16[32,1,4,128]{3,0,2,1:T(8,128)(2,1)S(1)} %get-tuple-element.182), channel_id=1, source_target_pairs={{16,0},{32,16},{48,32},{64,48},{80,64},{96,80},{112,96},{128,112},... | collective-permute-start | bytes 98312 | tf_op jit(solution)/shard_map/ppermute | solution.py:20
  124.8 4.2 %collective-permute-start.7 = (bf16[32,3,1,128]{3,0,2,1:T(8,128)(2,1)S(1)}, bf16[32,3,1,128]{3,0,2,1:T(8,128)(2,1)S(1)}, u32[]{:S(2)}, u32[]{:S(2)}) collective-permute-start(bf16[32,3,1,128]{3,0,2,1:T(8,128)(2,1)S(1)} %pad_maximum_fusion.30), channel_id=1, source_target_pairs={{0,15},{1,0},{2,1},{3,2},{4,3},{5,4},{6,5},{7,6},{8,7},{9,8},{10,9... | collective-permute-start | bytes 73736 | tf_op jit(solution)/shard_map/ppermute | solution.py:9
  129.1 5.2 %collective-permute-start.12 = (bf16[32,4,1,128]{3,0,2,1:T(8,128)(2,1)S(1)}, bf16[32,4,1,128]{3,0,2,1:T(8,128)(2,1)S(1)}, u32[]{:S(2)}, u32[]{:S(2)}) collective-permute-start(bf16[32,4,1,128]{3,0,2,1:T(8,128)(2,1)S(1)} %get-tuple-element.167), channel_id=1, source_target_pairs={{0,1},{1,2},{2,3},{3,4},{4,5},{5,6},{6,7},{7,8},{8,9},{9,10},{10,1... | collective-permute-start | bytes 98312 | tf_op jit(solution)/shard_map/ppermute | solution.py:19
  134.3 5.7 %collective-permute-start.13 = (bf16[32,4,1,128]{3,0,2,1:T(8,128)(2,1)S(1)}, bf16[32,4,1,128]{3,0,2,1:T(8,128)(2,1)S(1)}, u32[]{:S(2)}, u32[]{:S(2)}) collective-permute-start(bf16[32,4,1,128]{3,0,2,1:T(8,128)(2,1)S(1)} %get-tuple-element.168), channel_id=1, source_target_pairs={{1,0},{2,1},{3,2},{4,3},{5,4},{6,5},{7,6},{8,7},{9,8},{10,9},{11,1... | collective-permute-start | bytes 98312 | tf_op jit(solution)/shard_map/ppermute | solution.py:20
  145.3 12.5 %copy.71 = f32[8,4,2,6,2,128,2]{0,6,5,4,3,2,1:T(2,128)} copy(f32[8,4,2,6,2,128,2]{5,0,3,1,6,4,2:T(8,128)S(1)} %maximum_bitcast_fusion) | data formatting | bytes 1572864 | tf_op jit(solution)/shard_map/transpose | solution.py:138
  159.8 2.1 collective-permute-start.14
  161.8 2.8 fusion.1
  166.1 9.9 %collective-permute-start.15 = (bf16[32,3,1,128]{3,0,2,1:T(8,128)(2,1)S(1)}, bf16[32,3,1,128]{3,0,2,1:T(8,128)(2,1)S(1)}, u32[]{:S(2)}, u32[]{:S(2)}) collective-permute-start(bf16[32,3,1,128]{3,0,2,1:T(8,128)(2,1)S(1)} %pad_maximum_fusion.29), channel_id=1, source_target_pairs={{0,15},{1,0},{2,1},{3,2},{4,3},{5,4},{6,5},{7,6},{8,7},{9,8},{10,9... | collective-permute-start | bytes 73736 | tf_op jit(solution)/shard_map/ppermute | solution.py:9
  176.3 97.5 %all-reduce.4 = (f32[3,3,3,32,8]{3,4,2,1,0:T(8,128)}, f32[3,3,3,8,32]{4,3,2,1,0:T(8,128)}) all-reduce(f32[3,3,3,32,8]{3,4,2,1,0:T(8,128)S(1)} %bitcast.1048, f32[3,3,3,8,32]{4,3,2,1,0:T(8,128)S(1)} %bitcast.1047), channel_id=1, replica_groups=mesh['gx'=32,'gy'=16] {'gx','gy'}, use_global_device_ids=true, to_apply=%region_0.1 | all-reduce | flops 13824 | bytes 110592 | tf_op jit(solution)/shard_map/psum | solution.py:177
  279.0 12.5 %copy.77 = f32[8,4,2,6,2,128,2]{0,6,5,4,3,2,1:T(2,128)} copy(f32[8,4,2,6,2,128,2]{5,0,3,1,6,4,2:T(8,128)S(1)} %maximum_bitcast_fusion.1) | data formatting | bytes 1572864 | tf_op jit(solution)/shard_map/transpose | solution.py:138
  291.5 4.1 %fusion = bf16[8,4,8,256]{0,3,2,1:T(8,128)(2,1)S(1)} fusion(f32[8,4,8,256]{0,3,2,1:T(8,128)} %copy.78, f32[8,8,12,256]{0,3,2,1:T(8,128)} %bitcast.998), kind=kLoop, calls=%fused_computation.1 | loop fusion | flops 131072 | bytes 655360 | tf_op jit(solution)/shard_map/convert_element_type | solution.py:173
  297.1 89.9 %all-reduce.7.cloned.1.call-done = f32[3,3,3,32,32]{4,3,2,1,0:T(8,128)} async-done(((f32[3,3,3,32,32]{4,3,2,1,0:T(8,128)}), f32[3,3,3,32,32]{4,3,2,1,0:T(8,128)}) %all-reduce.7.cloned.1.call-update) | async-done | bytes 110608 | tf_op jit(solution)/shard_map/psum | solution.py:177
  387.0 1.8 copy.267
  (349 shorter events, 40.8 us)
Async XLA Ops:
  7.2 17.0 %copy-start.1 = (bf16[8,4,8,256]{3,2,1,0:T(8,128)(2,1)S(1)}, bf16[8,4,8,256]{3,2,1,0:T(8,128)(2,1)}, u32[]{:S(2)}) copy-start(bf16[8,4,8,256]{3,2,1,0:T(8,128)(2,1)} %param.6) | copy-start | bytes 393220
  7.2 14.4 %copy-start.7 = (bf16[3,3,3,32,8]{3,4,2,1,0:T(8,128)(2,1)S(1)}, bf16[3,3,3,32,8]{3,4,2,1,0:T(8,128)(2,1)}, u32[]{:S(2)}) copy-start(bf16[3,3,3,32,8]{3,4,2,1,0:T(8,128)(2,1)} %param.7) | copy-start | bytes 41476
  7.2 15.7 %copy-start.8 = (bf16[3,3,3,8,32]{4,3,2,1,0:T(8,128)(2,1)S(1)}, bf16[3,3,3,8,32]{4,3,2,1,0:T(8,128)(2,1)}, u32[]{:S(2)}) copy-start(bf16[3,3,3,8,32]{4,3,2,1,0:T(8,128)(2,1)} %param.9) | copy-start | bytes 41476
  7.2 379.8 %all-reduce.7.cloned.1.call-start = ((), (), s32[]{:S(2)}) async-start(), calls=%async_computation | async-start | bytes 884736 | tf_op jit(solution)/shard_map/psum | solution.py:177
  8.0 28.6 %collective-permute-start.8 = (bf16[8,1,8,256]{3,2,1,0:T(8,128)(2,1)S(1)}, bf16[8,1,8,256]{3,2,1,0:T(8,128)(2,1)S(1)}, u32[]{:S(2)}, u32[]{:S(2)}) collective-permute-start(bf16[8,1,8,256]{3,2,1,0:T(8,128)(2,1)S(1)} %slice.1336), channel_id=1, source_target_pairs={{0,16},{16,32},{32,48},{48,64},{64,80},{80,96},{96,112},{112,128},... | collective-permute-start | bytes 98312 | tf_op jit(solution)/shard_map/ppermute | solution.py:9
  12.8 30.7 %collective-permute-start = (bf16[8,1,8,256]{3,2,1,0:T(8,128)(2,1)S(1)}, bf16[8,1,8,256]{3,2,1,0:T(8,128)(2,1)S(1)}, u32[]{:S(2)}, u32[]{:S(2)}) collective-permute-start(bf16[8,1,8,256]{3,2,1,0:T(8,128)(2,1)S(1)} %slice.1175), channel_id=1, source_target_pairs={{0,16},{16,32},{32,48},{48,64},{64,80},{80,96},{96,112},{112,128},... | collective-permute-start | bytes 98312 | tf_op jit(solution)/shard_map/ppermute | solution.py:9
  24.1 2.4 copy-start.2
  36.7 8.8 %collective-permute-start.9 = (bf16[8,5,1,256]{3,2,1,0:T(2,128)(2,1)S(1)}, bf16[8,5,1,256]{3,2,1,0:T(2,128)(2,1)S(1)}, u32[]{:S(2)}, u32[]{:S(2)}) collective-permute-start(bf16[8,5,1,256]{3,2,1,0:T(2,128)(2,1)S(1)} %slice.1569), channel_id=1, source_target_pairs={{0,1},{1,2},{2,3},{3,4},{4,5},{5,6},{6,7},{7,8},{8,9},{9,10},{10,1... | collective-permute-start | bytes 61448 | tf_op jit(solution)/shard_map/ppermute | solution.py:9
  43.6 2.0 copy-start.5
  43.6 15.7 %collective-permute-start.1 = (bf16[8,5,1,256]{3,2,1,0:T(2,128)(2,1)S(1)}, bf16[8,5,1,256]{3,2,1,0:T(2,128)(2,1)}, u32[]{:S(2)}, u32[]{:S(2)}) collective-permute-start(bf16[8,5,1,256]{3,2,1,0:T(2,128)(2,1)S(1)} %slice.1457), channel_id=1, source_target_pairs={{0,1},{1,2},{2,3},{3,4},{4,5},{5,6},{6,7},{7,8},{8,9},{9,10},{10,1... | collective-permute-start | bytes 61448 | tf_op jit(solution)/shard_map/ppermute | solution.py:9
  58.0 1.4 copy-start.6
  72.5 12.6 %copy-start.4 = (bf16[216,2,4,128]{3,0,2,1:T(8,128)(2,1)S(1)}, bf16[216,2,4,128]{3,0,2,1:T(8,128)(2,1)}, u32[]{:S(2)}) copy-start(bf16[216,2,4,128]{3,0,2,1:T(8,128)(2,1)} %copy-done.3) | copy-start | bytes 1327108
  73.4 11.6 %collective-permute-start.2 = (bf16[32,1,4,128]{3,0,2,1:T(8,128)(2,1)S(1)}, bf16[32,1,4,128]{3,0,2,1:T(8,128)(2,1)S(1)}, u32[]{:S(2)}, u32[]{:S(2)}) collective-permute-start(bf16[32,1,4,128]{3,0,2,1:T(8,128)(2,1)S(1)} %get-tuple-element.183), channel_id=1, source_target_pairs={{0,16},{16,32},{32,48},{48,64},{64,80},{80,96},{96,112},{112,128},... | collective-permute-start | bytes 98312 | tf_op jit(solution)/shard_map/ppermute | solution.py:19
  75.8 10.3 %collective-permute-start.3 = (bf16[32,1,4,128]{3,0,2,1:T(8,128)(2,1)S(1)}, bf16[32,1,4,128]{3,0,2,1:T(8,128)(2,1)S(1)}, u32[]{:S(2)}, u32[]{:S(2)}) collective-permute-start(bf16[32,1,4,128]{3,0,2,1:T(8,128)(2,1)S(1)} %get-tuple-element.184), channel_id=1, source_target_pairs={{16,0},{32,16},{48,32},{64,48},{80,64},{96,80},{112,96},{128,112},... | collective-permute-start | bytes 98312 | tf_op jit(solution)/shard_map/ppermute | solution.py:20
  86.1 10.0 %collective-permute-start.4 = (bf16[32,4,1,128]{3,0,2,1:T(8,128)(2,1)S(1)}, bf16[32,4,1,128]{3,0,2,1:T(8,128)(2,1)S(1)}, u32[]{:S(2)}, u32[]{:S(2)}) collective-permute-start(bf16[32,4,1,128]{3,0,2,1:T(8,128)(2,1)S(1)} %get-tuple-element.169), channel_id=1, source_target_pairs={{0,1},{1,2},{2,3},{3,4},{4,5},{5,6},{6,7},{7,8},{8,9},{9,10},{10,1... | collective-permute-start | bytes 98312 | tf_op jit(solution)/shard_map/ppermute | solution.py:19
  94.1 9.1 %collective-permute-start.5 = (bf16[32,4,1,128]{3,0,2,1:T(8,128)(2,1)S(1)}, bf16[32,4,1,128]{3,0,2,1:T(8,128)(2,1)S(1)}, u32[]{:S(2)}, u32[]{:S(2)}) collective-permute-start(bf16[32,4,1,128]{3,0,2,1:T(8,128)(2,1)S(1)} %get-tuple-element.170), channel_id=1, source_target_pairs={{1,0},{2,1},{3,2},{4,3},{5,4},{6,5},{7,6},{8,7},{9,8},{10,9},{11,1... | collective-permute-start | bytes 98312 | tf_op jit(solution)/shard_map/ppermute | solution.py:20
  104.1 1.0 copy-start.13
  104.2 1.1 copy-start.14
  106.7 18.1 %collective-permute-start.6 = (bf16[32,1,4,128]{3,0,2,1:T(8,128)(2,1)S(1)}, bf16[32,1,4,128]{3,0,2,1:T(8,128)(2,1)S(1)}, u32[]{:S(2)}, u32[]{:S(2)}) collective-permute-start(bf16[32,1,4,128]{3,0,2,1:T(8,128)(2,1)S(1)} %slice.1521), channel_id=1, source_target_pairs={{0,496},{16,0},{32,16},{48,32},{64,48},{80,64},{96,80},{112,96},{1... | collective-permute-start | bytes 98312 | tf_op jit(solution)/shard_map/ppermute | solution.py:9
  115.6 13.5 %collective-permute-start.10 = (bf16[32,1,4,128]{3,0,2,1:T(8,128)(2,1)S(1)}, bf16[32,1,4,128]{3,0,2,1:T(8,128)(2,1)S(1)}, u32[]{:S(2)}, u32[]{:S(2)}) collective-permute-start(bf16[32,1,4,128]{3,0,2,1:T(8,128)(2,1)S(1)} %get-tuple-element.181), channel_id=1, source_target_pairs={{0,16},{16,32},{32,48},{48,64},{64,80},{80,96},{96,112},{112,128},... | collective-permute-start | bytes 98312 | tf_op jit(solution)/shard_map/ppermute | solution.py:19
  117.5 11.6 %collective-permute-start.11 = (bf16[32,1,4,128]{3,0,2,1:T(8,128)(2,1)S(1)}, bf16[32,1,4,128]{3,0,2,1:T(8,128)(2,1)S(1)}, u32[]{:S(2)}, u32[]{:S(2)}) collective-permute-start(bf16[32,1,4,128]{3,0,2,1:T(8,128)(2,1)S(1)} %get-tuple-element.182), channel_id=1, source_target_pairs={{16,0},{32,16},{48,32},{64,48},{80,64},{96,80},{112,96},{128,112},... | collective-permute-start | bytes 98312 | tf_op jit(solution)/shard_map/ppermute | solution.py:20
  124.8 15.2 %collective-permute-start.7 = (bf16[32,3,1,128]{3,0,2,1:T(8,128)(2,1)S(1)}, bf16[32,3,1,128]{3,0,2,1:T(8,128)(2,1)S(1)}, u32[]{:S(2)}, u32[]{:S(2)}) collective-permute-start(bf16[32,3,1,128]{3,0,2,1:T(8,128)(2,1)S(1)} %pad_maximum_fusion.30), channel_id=1, source_target_pairs={{0,15},{1,0},{2,1},{3,2},{4,3},{5,4},{6,5},{7,6},{8,7},{9,8},{10,9... | collective-permute-start | bytes 73736 | tf_op jit(solution)/shard_map/ppermute | solution.py:9
  129.1 28.7 %collective-permute-start.12 = (bf16[32,4,1,128]{3,0,2,1:T(8,128)(2,1)S(1)}, bf16[32,4,1,128]{3,0,2,1:T(8,128)(2,1)S(1)}, u32[]{:S(2)}, u32[]{:S(2)}) collective-permute-start(bf16[32,4,1,128]{3,0,2,1:T(8,128)(2,1)S(1)} %get-tuple-element.167), channel_id=1, source_target_pairs={{0,1},{1,2},{2,3},{3,4},{4,5},{5,6},{6,7},{7,8},{8,9},{9,10},{10,1... | collective-permute-start | bytes 98312 | tf_op jit(solution)/shard_map/ppermute | solution.py:19
  134.3 23.5 %collective-permute-start.13 = (bf16[32,4,1,128]{3,0,2,1:T(8,128)(2,1)S(1)}, bf16[32,4,1,128]{3,0,2,1:T(8,128)(2,1)S(1)}, u32[]{:S(2)}, u32[]{:S(2)}) collective-permute-start(bf16[32,4,1,128]{3,0,2,1:T(8,128)(2,1)S(1)} %get-tuple-element.168), channel_id=1, source_target_pairs={{1,0},{2,1},{3,2},{4,3},{5,4},{6,5},{7,6},{8,7},{9,8},{10,9},{11,1... | collective-permute-start | bytes 98312 | tf_op jit(solution)/shard_map/ppermute | solution.py:20
  142.6 0.9 copy-start.39
  158.7 3.2 copy-start
  159.8 6.3 %collective-permute-start.14 = (bf16[32,1,4,128]{3,0,2,1:T(8,128)(2,1)S(1)}, bf16[32,1,4,128]{3,0,2,1:T(8,128)(2,1)S(1)}, u32[]{:S(2)}, u32[]{:S(2)}) collective-permute-start(bf16[32,1,4,128]{3,0,2,1:T(8,128)(2,1)S(1)} %slice.1651), channel_id=1, source_target_pairs={{0,496},{16,0},{32,16},{48,32},{64,48},{80,64},{96,80},{112,96},{1... | collective-permute-start | bytes 98312 | tf_op jit(solution)/shard_map/ppermute | solution.py:9
  166.1 107.7 %collective-permute-start.15 = (bf16[32,3,1,128]{3,0,2,1:T(8,128)(2,1)S(1)}, bf16[32,3,1,128]{3,0,2,1:T(8,128)(2,1)S(1)}, u32[]{:S(2)}, u32[]{:S(2)}) collective-permute-start(bf16[32,3,1,128]{3,0,2,1:T(8,128)(2,1)S(1)} %pad_maximum_fusion.29), channel_id=1, source_target_pairs={{0,15},{1,0},{2,1},{3,2},{4,3},{5,4},{6,5},{7,6},{8,7},{9,8},{10,9... | collective-permute-start | bytes 73736 | tf_op jit(solution)/shard_map/ppermute | solution.py:9
  276.3 0.9 copy-start.25
  276.3 0.9 copy-start.26
  276.3 0.9 copy-start.27
  276.3 0.9 copy-start.28
  (37 other events, 27.0 us)
Sparse Core Ops, SparseCore 0:
  115.7 271.3 all-reduce.6
where the time goes:
time: 397 us; the launch traced here: 396 us
  waiting for transfers between devices  98.2 us (25%)
  blocking collectives  97.5 us (25%)
  local copies, waits for them, and re-layouts  83.7 us (21%)
  starting transfers between devices  81.7 us (21%)
  between operations  15.7 us (4%)
  other arithmetic  10.6 us (3%)
  matrix products  8.33 us (2%)
    psum x1, blocking collectives, local(): lax.psum((local_down, local_mid, local_up), ('gx', 'gy'))  97.5 us
    psum x1, waiting for transfers between devices, local(): lax.psum((local_down, local_mid, local_up), ('gx', 'gy'))  89.9 us
    ppermute x8, starting transfers between devices, from_behind(): lax.ppermute(x, axis, [(i, (i + by) % devices) for i in range(devices)])  40 us
    transpose x2, local copies, waits for them, and re-layouts, spread(): jnp.transpose(phased, (0, 1, 4, 2, 5, 3, 6))  25 us
    ppermute x4, starting transfers between devices, padded_2(): after = lax.ppermute(initial, axis, down)  24.2 us
    unnamed x212, local copies, waits for them, and re-layouts  18.2 us
    ppermute x4, starting transfers between devices, padded_2(): before = lax.ppermute(last, axis, up)  17.5 us
    reshape x2, local copies, waits for them, and re-layouts, strided_set(): shaped = padded.reshape(chans, half_x + 1, 2, half_y + 1, 2, half_z, 2)  14.3 us
  transfers between devices with their start and end apart: 17, of which 3 were waited for; matrix products, arithmetic and copies ran while one was open for 20% of the time, Pallas kernels for 0%

commit v1 on v0

v1 whole, which is shorter than its diff:
```python
import jax
import jax.numpy as jnp
from jax import lax
from jax.experimental import pallas as pl
from jax.experimental.pallas import tpu as pltpu
from jax.sharding import PartitionSpec as P

BF = jnp.bfloat16
F32 = jnp.float32
LANES = 128
LOCAL = [(i, j) for i in range(2) for j in range(4)]
UPPER = LOCAL + [(0, 4), (1, 4)] + [(2, j) for j in range(5)]
ROWS = 384


def shift(x, axis, by):
    devices = lax.axis_size(axis)
    return lax.ppermute(x, axis, [(i, (i + by) % devices) for i in range(devices)])


def call(body, outs, args, scratch=(), flops=10**8):
    moved = 2 * 10**6
    return pl.pallas_call(
        body,
        out_shape=[jax.ShapeDtypeStruct(s, d) for s, d in outs],
        in_specs=[pl.BlockSpec(memory_space=pltpu.VMEM)] * len(args),
        out_specs=[pl.BlockSpec(memory_space=pltpu.VMEM)] * len(outs),
        scratch_shapes=[pltpu.VMEM(s, d) for s, d in scratch],
        compiler_params=pltpu.CompilerParams(vmem_limit_bytes=32 * 2**20),
        cost_estimate=pl.CostEstimate(flops=flops, bytes_accessed=moved, transcendentals=0),
    )(*args)


def dot(a, b):
    return lax.dot_general(a, b, (((1,), (0,)), ((), ())), preferred_element_type=F32)


def dot_nt(a, b):
    return lax.dot_general(a, b, (((1,), (1,)), ((), ())), preferred_element_type=F32)


def split_z():
    z = lax.broadcasted_iota(jnp.int32, (256, 256), 0)
    k = lax.broadcasted_iota(jnp.int32, (256, 256), 1)
    return (z == 2 * (k & 127) + (k >> 7)).astype(F32).astype(BF)


def join_z():
    k = lax.broadcasted_iota(jnp.int32, (256, 256), 0)
    z = lax.broadcasted_iota(jnp.int32, (256, 256), 1)
    return (z == 2 * (k & 127) + (k >> 7)).astype(F32).astype(BF)


def slab_order(dim):
    r = lax.broadcasted_iota(jnp.int32, (512, 512), dim)
    s = lax.broadcasted_iota(jnp.int32, (512, 512), 1 - dim)
    source = ((r >> 3) & 1) * 256 + (r & 7) * 32 + (r >> 7) * 8 + ((r >> 4) & 7)
    return (s == source).astype(F32).astype(BF)


def to_slabs_kernel(f_ref, g_ref, f_out, g_out, up_out, down_out):
    halves = split_z()
    order = slab_order(0)
    for ref, out in ((f_ref, f_out), (g_ref, g_out)):
        z = dot(ref[...], halves).astype(BF)
        z = jnp.concatenate([z[:, :LANES], z[:, LANES:]], 0)
        out[...] = dot(order, z).astype(BF).reshape(4, 8, 16, LANES)
    up_out[:, 0:3] = f_out[:, 5:8]
    up_out[:, 3:4] = g_out[:, 7:8]
    down_out[...] = f_out[:, 0:2]


def rolled_odd(slab):
    return pltpu.roll(slab.astype(F32)[8:], 1, 1)


def act_and_slope(v):
    s = jax.nn.sigmoid(v)
    return 0.2 * v + 0.8 * v * s, 0.2 + 0.8 * (s + v * s * (1.0 - s))


def three(v):
    return jnp.concatenate([pltpu.roll(v, 1, 1), v, pltpu.roll(v, LANES - 1, 1)], 0).astype(BF)


def fill_columns(out, n, slab, pair, i, j):
    for a in range(3):
        x = 2 * i + a - 1
        tiles = [slab(x, 2 * j - 1), slab(x, 2 * j), slab(x, 2 * j + 1), pair(x, j - 1), pair(x, j)]
        for t, tile in enumerate(tiles):
            row = 80 * a + 16 * t
            out[row : row + 16, n * LANES : (n + 1) * LANES] = tile


def grad_block(cols, h, rows, step):
    n = h.shape[1]
    total = None
    for k in range(4):
        size = min(step, rows - step * k)
        padded = jnp.concatenate(
            [jnp.zeros((32 * k, n), BF)] * (k > 0) + [h] + [jnp.zeros((96 - 32 * k, n), BF)] * (k < 3), 0
        )
        term = dot_nt(cols[step * k : step * k + size, :n], padded)
        if size < step:
            term = jnp.concatenate([term, jnp.zeros((step - size, LANES), F32)], 0)
        total = term if total is None else total + term
    return total


def forward_kernel(
    f_ref, g_ref, ylo, yhi, xlo, xhi, wd, wm, wg,
    slope_out, h1_out, h2_out, d2_out, fcol_out, gup_out, up_out, down_out,
    fpair, gpair, h1_three, xcol, mcol, gcol,
):
    def f(x, y):
        if x < 0:
            return xlo[(x + 3) * 13 + y + 3]
        if x > 3:
            return xhi[(x - 4) * 13 + y + 3]
        return ylo[x, y + 3] if y < 0 else yhi[x, y - 8] if y > 7 else f_ref[x, y]

    def g(x, y):
        if x < 0:
            return xlo[39 + y + 1]
        return ylo[x, 3] if y < 0 else g_ref[x, y]

    zero = jnp.zeros((8, LANES), F32)
    for x in range(-3, 6):
        for j in range(-2, 5):
            first = zero if j == -2 else rolled_odd(f(x, 2 * j))
            fpair[x + 3, j + 2] = jnp.concatenate([first, rolled_odd(f(x, 2 * j + 1))], 0).astype(BF)
    for x in range(-1, 4):
        for j in range(-1, 4):
            first = zero if j == -1 else rolled_odd(g(x, 2 * j))
            gpair[x + 1, j + 1] = jnp.concatenate([first, rolled_odd(g(x, 2 * j + 1))], 0).astype(BF)

    def f_pair(x, j):
        return fpair[x + 3, j + 2]

    def g_pair(x, j):
        return gpair[x + 1, j + 1]

    for n, (i, j) in enumerate(LOCAL):
        fill_columns(fcol_out, n, f, f_pair, i, j)
        fill_columns(gcol, n, g, g_pair, i, j)
    rest = [(i, j) for i in range(-1, 3) for j in range(-1, 5) if (i, j) not in LOCAL]
    for n, (i, j) in enumerate(rest):
        fill_columns(xcol, n, f, f_pair, i, j)

    def put_h1(cells, columns):
        wide = len(cells) * LANES
        v, s = act_and_slope(dot(wd[...], columns))
        for n, (i, j) in enumerate(cells):
            lanes = slice(n * LANES, (n + 1) * LANES)
            h1_three[i + 1, j + 1] = three(v[:, lanes])
            if i >= 0 and j >= 0:
                slope_out[i * 5 + j] = s[:, lanes]
            if (i, j) in LOCAL:
                h1_out[:, LOCAL.index((i, j)) * LANES : (LOCAL.index((i, j)) + 1) * LANES] = v[:, lanes].astype(BF)

    for start in range(0, 8, 4):
        put_h1(LOCAL[start : start + 4], fcol_out[:, start * LANES : (start + 4) * LANES])
    for start in range(0, 16, 4):
        put_h1(rest[start : start + 4], xcol[:, start * LANES : (start + 4) * LANES])

    for n, (i, j) in enumerate(LOCAL):
        for a in range(3):
            for b in range(3):
                row = 96 * (3 * a + b)
                mcol[row : row + 96, n * LANES : (n + 1) * LANES] = h1_three[i + a, j + b]

    for start in range(0, 8, 4):
        lanes = slice(start * LANES, (start + 4) * LANES)
        v, s = act_and_slope(dot(wm[...], mcol[:, lanes]))
        h2_out[:, lanes] = v.astype(BF)
        d2_out[:, lanes] = (dot(wg[...], gcol[:, lanes]) * s).astype(BF)

    gup_out[...] = grad_block(gcol, h2_out[...], 240, 64)
    for i in range(2):
        at = 4 * i * LANES
        up_out[i] = d2_out[:, at + 3 * LANES : at + 4 * LANES]
        down_out[i] = d2_out[:, at : at + LANES]
        down_out[2 + i] = d2_out[:, at + LANES : at + 2 * LANES]
        down_out[4 + i] = h2_out[:, at : at + LANES]


def backward_kernel(
    d2, ylo, yhi, xlo, xhi, slope, h1, fcol, gup, wb, grads_out, d1_out, d2_three, mcol,
):
    def d(i, j):
        if i < 0:
            return xlo[j + 1]
        if i > 1:
            return xhi[(i - 2) * 7 + j + 1]
        if j < 0:
            return ylo[i]
        if j > 3:
            return yhi[2 * (j - 4) + i]
        at = (4 * i + j) * LANES
        return d2[:, at : at + LANES]

    for i in range(-1, 4):
        for j in range(-1, 6):
            d2_three[i + 1, j + 1] = three(d(i, j).astype(F32))
    for n, (i, j) in enumerate(UPPER):
        for a in range(3):
            for b in range(3):
                row = 96 * (3 * a + b)
                mcol[row : row + 96, n * LANES : (n + 1) * LANES] = d2_three[i + a, j + b]
    for start in range(0, 15, 4):
        cells = UPPER[start : start + 4]
        v = dot(wb[...], mcol[:, start * LANES : (start + len(cells)) * LANES])
        for n, (i, j) in enumerate(cells):
            at = (start + n) * LANES
            d1_out[:, at : at + LANES] = (v[:, n * LANES : (n + 1) * LANES] * slope[i * 5 + j]).astype(BF)
    grads_out[0:224] = grad_block(mcol, h1[...], 864, 224)
    grads_out[224:288] = grad_block(fcol, d1_out[:, : 8 * LANES], 240, 64)
    grads_out[288:352] = gup[...]
    grads_out[352:ROWS] = jnp.zeros((ROWS - 352, LANES), F32)


def outputs_kernel(f_ref, g_ref, h2, yhi, xhi, d1, wu, wv, mapped_out, grad_out, ucol, slabs):
    def h(i, j):
        if i > 1:
            return xhi[14 + j]
        if j > 3:
            return yhi[4 + i]
        at = (4 * i + j) * LANES
        return h2[:, at : at + LANES]

    def p(i, j):
        at = UPPER.index((i, j)) * LANES
        return d1[:, at : at + LANES]

    joined = join_z()
    order = slab_order(1)
    for cell, w, base, out in ((h, wu, f_ref, mapped_out), (p, wv, g_ref, grad_out)):
        two = {}
        for i, j in UPPER:
            v = cell(i, j).astype(F32)
            two[i, j] = jnp.concatenate([v, pltpu.roll(v, LANES - 1, 1)], 0).astype(BF)
        for n, (i, j) in enumerate(LOCAL):
            for k in range(4):
                ucol[64 * k : 64 * k + 64, n * LANES : (n + 1) * LANES] = two[i + k // 2, j + k % 2]
        for start in range(0, 8, 2):
            up = dot(w[...], ucol[:, start * LANES : (start + 2) * LANES])
            for n in range(2):
                i, j = LOCAL[start + n]
                for k in range(4):
                    x, y = 2 * i + k // 2, 2 * j + k % 2
                    row = 16 * (8 * x + y)
                    added = base[x, y].astype(F32) + up[16 * k : 16 * k + 16, n * LANES : (n + 1) * LANES]
                    slabs[row : row + 16] = added.astype(BF)
        z = dot(order, slabs[...]).astype(BF)
        out[...] = dot(jnp.concatenate([z[:256], z[256:]], 1), joined).astype(BF)


def tap_rows(rows):
    order = [(0, 1), (0, 2), (1, 1), (1, 2), (2, 1), (2, 2), None, (0, 0), (1, 0), (2, 0)]
    for a in range(3):
        for m, tap in enumerate(order):
            if tap is not None:
                yield 10 * a + m, 9 * a + 3 * tap[0] + tap[1]


def unpack_kernel(total, down_out, mid_out, up_out):
    for k in range(4):
        part = total[0:224]
        part = pltpu.roll(part, LANES - 32 * k, 1) if k else part
        for s in range(min(7, 27 - 7 * k)):
            mid_out[26 - (7 * k + s)] = part[32 * s : 32 * s + 32, :32]
    flipped = total[224:288].T
    for block, tap in tap_rows(240):
        k, m = block // 8, block % 8
        rows = flipped[32 * k : 32 * k + 32]
        rows = jnp.concatenate([rows, jnp.zeros((32, 64), F32)], 1)
        rows = pltpu.roll(rows, LANES - 8 * m, 1) if m else rows
        down_out[tap] = rows[:, :8]
    for k in range(4):
        part = total[288:352]
        part = pltpu.roll(part, LANES - 32 * k, 1) if k else part
        for block, tap in tap_rows(240):
            if block // 8 == k:
                m = block % 8
                up_out[tap] = part[8 * m : 8 * m + 8, :32]


def down_weights(w):
    none = jnp.zeros_like(w[:, 0, 0])
    blocks = [w[:, 0, 1], w[:, 0, 2], w[:, 1, 1], w[:, 1, 2], w[:, 2, 1], w[:, 2, 2], none, w[:, 0, 0], w[:, 1, 0], w[:, 2, 0]]
    return jnp.transpose(jnp.stack(blocks, 1), (2, 0, 1, 3)).reshape(32, 240)


def up_weights(w):
    none = jnp.zeros_like(w[0, 0, 0])
    pick = ((1, None), (2, 0))
    rows = []
    for p in range(2):
        for q in range(2):
            for r in range(2):
                row = []
                for k in range(8):
                    a, b, d = pick[p][k // 4], pick[q][k // 2 % 2], pick[r][k % 2]
                    row.append(none if None in (a, b, d) else w[a, b, d])
                rows.append(jnp.concatenate(row, 1))
    return jnp.concatenate(rows, 0)


def all_sum(x):
    gx, gy = lax.axis_size("gx"), lax.axis_size("gy")
    part = x.reshape(gx, ROWS // gx, LANES)
    part = lax.all_to_all(part, "gx", 0, 0, tiled=True).sum(0)
    part = jnp.broadcast_to(part[None], (gy,) + part.shape)
    part = lax.all_to_all(part, "gy", 0, 0, tiled=True).sum(0)
    part = jnp.broadcast_to(part[None], (gx,) + part.shape)
    return lax.all_to_all(part, "gx", 0, 0, tiled=True).reshape(ROWS, LANES)


def local(fields, cotangent, w_down, w_mid, w_up):
    wd = down_weights(w_down)
    wg = down_weights(jnp.swapaxes(w_up, 3, 4))
    wm = jnp.transpose(w_mid, (3, 0, 1, 2, 4)).reshape(32, 864)
    wb = jnp.transpose(w_mid[::-1, ::-1, ::-1], (4, 0, 1, 2, 3)).reshape(32, 864)
    wu = up_weights(w_up)
    wv = up_weights(jnp.swapaxes(w_down, 3, 4))

    f, g, up, down = call(
        to_slabs_kernel,
        [((4, 8, 16, LANES), BF)] * 2 + [((4, 4, 16, LANES), BF), ((4, 2, 16, LANES), BF)],
        [fields.reshape(256, 256), cotangent.reshape(256, 256)],
    )
    ylo, yhi = shift(up, "gy", 1), shift(down, "gy", -1)
    f_ext = jnp.concatenate([ylo[:, :3], f, yhi], 1)
    last = jnp.concatenate([f_ext[1:].reshape(39, 16, LANES), ylo[3, 3:4], g[3]], 0)
    xlo = shift(last, "gx", 1)
    xhi = shift(f_ext[:2].reshape(26, 16, LANES), "gx", -1)

    slope, h1, h2, d2, fcol, gup, up, down = call(
        forward_kernel,
        [((15, 32, LANES), F32), ((32, 8 * LANES), BF), ((32, 8 * LANES), BF), ((32, 8 * LANES), BF),
         ((240, 8 * LANES), BF), ((64, LANES), F32), ((2, 32, LANES), BF), ((6, 32, LANES), BF)],
        [f, g, ylo, yhi, xlo, xhi, wd, wm, wg],
        [((9, 7, 16, LANES), BF), ((5, 5, 16, LANES), BF), ((4, 6, 96, LANES), BF),
         ((240, 16 * LANES), BF), ((864, 8 * LANES), BF), ((240, 8 * LANES), BF)],
    )
    ylo, yhi = shift(up, "gy", 1), shift(down, "gy", -1)
    cells = jnp.transpose(d2.reshape(32, 8, LANES), (1, 0, 2))
    last = jnp.concatenate([ylo[1:2], cells[4:8], yhi[1:2], yhi[3:4]], 0)
    first = jnp.concatenate(
        [ylo[0:1], cells[0:4], yhi[0:1], yhi[2:3], last]
        + [h2[None, :, j * LANES : (j + 1) * LANES] for j in range(4)] + [yhi[4:5]], 0
    )
    xlo = shift(last, "gx", 1)
    xhi = shift(first, "gx", -1)

    grads, d1 = call(
        backward_kernel,
        [((ROWS, LANES), F32), ((32, 15 * LANES), BF)],
        [d2, ylo, yhi, xlo, xhi, slope, h1, fcol, gup, wb],
        [((5, 7, 96, LANES), BF), ((864, 15 * LANES), BF)],
    )
    mapped, grad_fields = call(
        outputs_kernel,
        [((256, 256), BF)] * 2,
        [f, g, h2, yhi, xhi, d1, wu, wv],
        [((256, 8 * LANES), BF), ((512, LANES), BF)],
    )
    grad_down, grad_mid, grad_up = call(
        unpack_kernel,
        [((27, 32, 8), F32), ((27, 32, 32), F32), ((27, 8, 32), F32)],
        [all_sum(grads)],
    )
    return (
        mapped.reshape(fields.shape),
        grad_fields.reshape(fields.shape),
        grad_down.reshape(w_down.shape),
        grad_mid.reshape(w_mid.shape),
        grad_up.reshape(w_up.shape),
    )


def solution(mesh):
    in_specs = (P(None, "gx", "gy", None), P(None, "gx", "gy", None), P(), P(), P())
    out_specs = (P(None, "gx", "gy", None), P(None, "gx", "gy", None), P(), P(), P())
    return jax.shard_map(local, mesh=mesh, in_specs=in_specs, out_specs=out_specs, check_vma=False)
```

time: 397 us -> 126 us (0.32)
  blocking collectives: 97.5 us -> 0 us
  local copies, waits for them, and re-layouts: 83.7 us -> 6.73 us
  waiting for transfers between devices: 98.2 us -> 48.6 us
  starting transfers between devices: 81.7 us -> 62 us
  between operations: 15.7 us -> 1.1 us
  other arithmetic: 10.6 us -> 0.37 us
  matrix products: 8.33 us -> 0 us
  Pallas kernels: 0 us -> 6.67 us
    psum x1 -> x0, blocking collectives: 97.5 us -> none  [local(): lax.psum((local_down, local_mid, local_up), ('gx', 'gy'))]
    psum x1 -> x0, waiting for transfers between devices: 89.9 us -> none  [local(): lax.psum((local_down, local_mid, local_up), ('gx', 'gy'))]
    ppermute x16 -> x8, starting transfers between devices: 81.7 us -> 38.2 us  [shift(): lax.ppermute(x, axis, [(i, (i + by) % devices) for i in range(devices)])]
    all_to_all x0 -> x3, waiting for transfers between devices: none -> 30.6 us  [the longest x1 11.2 us: all_sum(): part = lax.all_to_all(part, 'gx', 0, 0, tiled=True).sum(0)]
    transpose x3 -> x4, local copies, waits for them, and re-layouts: 25 us -> 0.21 us  [the longest x1 0.16 us: local(): wm = jnp.transpose(w_mid, (3, 0, 1, 2, 4)).reshape(32, 864)]
    all_to_all x0 -> x3, starting transfers between devices: none -> 23.8 us  [the longest x1 11.5 us: all_sum(): part = lax.all_to_all(part, 'gx', 0, 0, tiled=True).sum(0)]
    unnamed x212 -> x45, local copies, waits for them, and re-layouts: 18.2 us -> 2.89 us
    reshape x3 -> x6, local copies, waits for them, and re-layouts: 15.3 us -> 1.2 us  [the longest x1 0.72 us: all_sum(): part = x.reshape(gx, ROWS // gx, LANES)]
  transfers between devices with their start and end apart: 17 -> 11, of which waited for: 3 -> 7; matrix products, arithmetic and copies ran while one was open for 20% -> 2% of each run, Pallas kernels for 0% -> 1%
where the time goes in v1:
time: 126 us; the launch traced here: 125 us
  starting transfers between devices  62 us (49%)
  waiting for transfers between devices  48.6 us (39%)
  local copies, waits for them, and re-layouts  6.73 us (5%)
  Pallas kernels  6.67 us (5%)
    ppermute x8, starting transfers between devices, shift(): lax.ppermute(x, axis, [(i, (i + by) % devices) for i in range(devices)])  38.2 us
    ppermute x8, waiting for transfers between devices, shift(): lax.ppermute(x, axis, [(i, (i + by) % devices) for i in range(devices)])  18.1 us
    all_to_all x1, starting transfers between devices, all_sum(): part = lax.all_to_all(part, 'gx', 0, 0, tiled=True).sum(0)  11.5 us
    all_to_all x1, waiting for transfers between devices, all_sum(): part = lax.all_to_all(part, 'gx', 0, 0, tiled=True).sum(0)  11.2 us
    all_to_all x1, waiting for transfers between devices, all_sum(): part = lax.all_to_all(part, 'gy', 0, 0, tiled=True).sum(0)  10 us
    all_to_all x1, waiting for transfers between devices, all_sum(): return lax.all_to_all(part, 'gx', 0, 0, tiled=True).reshape(ROWS, LANES)  9.3 us
    all_to_all x1, starting transfers between devices, all_sum(): part = lax.all_to_all(part, 'gy', 0, 0, tiled=True).sum(0)  8.27 us
    pallas_call x5, Pallas kernels, call(): pl.pallas_call(body, out_shape=[jax.ShapeDtypeStruct(s, d) for s, d in ou...  6.67 us
  transfers between devices with their start and end apart: 11, of which 7 were waited for; matrix products, arithmetic and copies ran while one was open for 2% of the time, Pallas kernels for 1%

profile of v1, /device:TPU:1, one launch (start us, length us, event | category | flops | bytes accessed | tf_op | source)
XLA Modules:
  0.0 125.5 jit_solution(9854705051511208779)
XLA Ops:
  0.6 0.9 copy-done
  1.5 0.9 copy-done.1
  2.4 0.7 shard_map.92
  3.1 8.8 %collective-permute-start = (bf16[4,4,16,128]{3,2,1,0:T(8,128)(2,1)S(1)}, bf16[4,4,16,128]{3,2,1,0:T(8,128)(2,1)S(1)}, u32[]{:S(2)}, u32[]{:S(2)}) collective-permute-start(bf16[4,4,16,128]{3,2,1,0:T(8,128)(2,1)S(1)} %get-tuple-element.26), channel_id=1, source_target_pairs={{0,1},{1,2},{2,3},{3,4},{4,5},{5,6},{6,7},{7,8},{8,9},{9,10},{10,1... | collective-permute-start | bytes 196616 | tf_op jit(solution)/shard_map/ppermute | solution.py:18
  12.0 2.1 %collective-permute-start.1 = (bf16[4,2,16,128]{3,2,1,0:T(8,128)(2,1)S(1)}, bf16[4,2,16,128]{3,2,1,0:T(8,128)(2,1)S(1)}, u32[]{:S(2)}, u32[]{:S(2)}) collective-permute-start(bf16[4,2,16,128]{3,2,1,0:T(8,128)(2,1)S(1)} %get-tuple-element.27), channel_id=1, source_target_pairs={{0,15},{1,0},{2,1},{3,2},{4,3},{5,4},{6,5},{7,6},{8,7},{9,8},{10,9... | collective-permute-start | bytes 98312 | tf_op jit(solution)/shard_map/ppermute | solution.py:18
  14.4 6.9 %collective-permute-done.1.yhi = bf16[4,2,16,128]{3,2,1,0:T(8,128)(2,1)S(1)} collective-permute-done((bf16[4,2,16,128]{3,2,1,0:T(8,128)(2,1)S(1)}, bf16[4,2,16,128]{3,2,1,0:T(8,128)(2,1)S(1)}, u32[]{:S(2)}, u32[]{:S(2)}) %collective-permute-start.1) | collective-permute-done | bytes 32800 | tf_op jit(solution)/shard_map/ppermute | solution.py:18
  21.4 2.8 %collective-permute-start.2 = (bf16[48,16,128]{2,1,0:T(8,128)(2,1)S(1)}, bf16[48,16,128]{2,1,0:T(8,128)(2,1)S(1)}, u32[]{:S(2)}, u32[]{:S(2)}) collective-permute-start(bf16[48,16,128]{2,1,0:T(8,128)(2,1)S(1)} %pad_maximum_fusion.1), channel_id=1, source_target_pairs={{0,16},{16,32},{32,48},{48,64},{64,80},{80,96},{96,112},{112,128},... | collective-permute-start | bytes 589832 | tf_op jit(solution)/shard_map/ppermute | solution.py:18
  24.4 0.2 copy.92
  24.6 0.2 reshape.65.wm
  24.9 10.4 %collective-permute-start.3 = (bf16[26,16,128]{2,1,0:T(8,128)(2,1)S(1)}, bf16[26,16,128]{2,1,0:T(8,128)(2,1)S(1)}, u32[]{:S(2)}, u32[]{:S(2)}) collective-permute-start(bf16[26,16,128]{2,1,0:T(8,128)(2,1)S(1)} %bitcast.253), channel_id=1, source_target_pairs={{0,496},{16,0},{32,16},{48,32},{64,48},{80,64},{96,80},{112,96},{1... | collective-permute-start | bytes 319496 | tf_op jit(solution)/shard_map/ppermute | solution.py:18
  35.3 2.5 %collective-permute-done.3.xhi = bf16[26,16,128]{2,1,0:T(8,128)(2,1)S(1)} collective-permute-done((bf16[26,16,128]{2,1,0:T(8,128)(2,1)S(1)}, bf16[26,16,128]{2,1,0:T(8,128)(2,1)S(1)}, u32[]{:S(2)}, u32[]{:S(2)}) %collective-permute-start.3) | collective-permute-done | bytes 106528 | tf_op jit(solution)/shard_map/ppermute | solution.py:18
  37.8 1.7 %shard_map.93 = (f32[15,32,128]{2,1,0:T(8,128)S(1)}, bf16[32,1024]{1,0:T(8,128)(2,1)S(1)}, bf16[32,1024]{1,0:T(8,128)(2,1)S(1)}, bf16[32,1024]{1,0:T(8,128)(2,1)...) custom-call(bf16[4,8,16,128]{3,2,1,0:T(8,128)(2,1)S(1)} %get-tuple-e, ...), custom_call_target="tpu_custom_call" | custom-call | flops 100000000 | bytes 2000000 | tf_op jit(solution)/shard_map/pallas_call | solution.py:23
  39.5 1.9 %collective-permute-start.5 = (bf16[2,32,128]{2,1,0:T(8,128)(2,1)S(1)}, bf16[2,32,128]{2,1,0:T(8,128)(2,1)S(1)}, u32[]{:S(2)}, u32[]{:S(2)}) collective-permute-start(bf16[2,32,128]{2,1,0:T(8,128)(2,1)S(1)} %get-tuple-element.30), channel_id=1, source_target_pairs={{0,1},{1,2},{2,3},{3,4},{4,5},{5,6},{6,7},{7,8},{8,9},{9,10},{10,1... | collective-permute-start | bytes 49160 | tf_op jit(solution)/shard_map/ppermute | solution.py:18
  41.4 2.4 %collective-permute-start.4 = (bf16[6,32,128]{2,1,0:T(8,128)(2,1)S(1)}, bf16[6,32,128]{2,1,0:T(8,128)(2,1)S(1)}, u32[]{:S(2)}, u32[]{:S(2)}) collective-permute-start(bf16[6,32,128]{2,1,0:T(8,128)(2,1)S(1)} %get-tuple-element.29), channel_id=1, source_target_pairs={{0,15},{1,0},{2,1},{3,2},{4,3},{5,4},{6,5},{7,6},{8,7},{9,8},{10,9... | collective-permute-start | bytes 147464 | tf_op jit(solution)/shard_map/ppermute | solution.py:18
  43.9 6.9 %collective-permute-done.4.yhi = bf16[6,32,128]{2,1,0:T(8,128)(2,1)S(1)} collective-permute-done((bf16[6,32,128]{2,1,0:T(8,128)(2,1)S(1)}, bf16[6,32,128]{2,1,0:T(8,128)(2,1)S(1)}, u32[]{:S(2)}, u32[]{:S(2)}) %collective-permute-start.4) | collective-permute-done | bytes 49184 | tf_op jit(solution)/shard_map/ppermute | solution.py:18
  50.8 1.9 %collective-permute-start.7 = (bf16[7,32,128]{2,1,0:T(8,128)(2,1)S(1)}, bf16[7,32,128]{2,1,0:T(8,128)(2,1)S(1)}, u32[]{:S(2)}, u32[]{:S(2)}) collective-permute-start(bf16[7,32,128]{2,1,0:T(8,128)(2,1)S(1)} %pad_maximum_fusion.2), channel_id=1, source_target_pairs={{0,16},{16,32},{32,48},{48,64},{64,80},{80,96},{96,112},{112,128},... | collective-permute-start | bytes 172040 | tf_op jit(solution)/shard_map/ppermute | solution.py:18
  52.8 7.9 %collective-permute-start.6 = (bf16[19,32,128]{2,1,0:T(8,128)(2,1)S(1)}, bf16[19,32,128]{2,1,0:T(8,128)(2,1)S(1)}, u32[]{:S(2)}, u32[]{:S(2)}) collective-permute-start(bf16[19,32,128]{2,1,0:T(8,128)(2,1)S(1)} %constant_dynamic-update-slice_fusion.20), channel_id=1, source_target_pairs={{0,496},{16,0},{32,16},{48,32},{64,48},{80,64},{96,80},{112,96},{1... | collective-permute-start | bytes 466952 | tf_op jit(solution)/shard_map/ppermute | solution.py:18
  60.8 0.1 copy.108.wb
  61.1 1.8 %collective-permute-done.6.xhi = bf16[19,32,128]{2,1,0:T(8,128)(2,1)S(1)} collective-permute-done((bf16[19,32,128]{2,1,0:T(8,128)(2,1)S(1)}, bf16[19,32,128]{2,1,0:T(8,128)(2,1)S(1)}, u32[]{:S(2)}, u32[]{:S(2)}) %collective-permute-start.6) | collective-permute-done | bytes 155680 | tf_op jit(solution)/shard_map/ppermute | solution.py:18
  62.9 1.6 %shard_map.94 = (f32[384,128]{1,0:T(8,128)S(1)}, bf16[32,1920]{1,0:T(8,128)(2,1)S(1)}) custom-call(bf16[32,1024]{1,0:T(8,128)(2,1)S(1)} %get-tuple-element.31.d2, bf16[2,32,128]{2,1,0:T(8,128)(2,1)S(1)} %collective-permute-done.5.ylo, bf16[6,32,128]{2,1,0:T(8,128)(2,1)S(1)} %collective-permute-done.4.yhi, ...), custom_call_target="tpu_custom_call" | custom-call | flops 100000000 | bytes 2000000 | tf_op jit(solution)/shard_map/pallas_call | solution.py:23
  64.5 0.7 reshape.71
  65.2 11.5 %all-to-all-start = ((f32[32,12,128]{2,1,0:T(8,128)}), f32[32,12,128]{2,1,0:T(8,128)S(1)}, u32[]{:S(2)}, u32[]{:S(2)}) async-start(f32[32,12,128]{2,1,0:T(8,128)} %reshape.71), calls=%async_computation | async-start | bytes 524288 | tf_op jit(solution)/shard_map/all_to_all | solution.py:312
  77.4 11.2 %all-to-all-done = f32[32,12,128]{2,1,0:T(8,128)S(1)} async-done(((f32[32,12,128]{2,1,0:T(8,128)}), f32[32,12,128]{2,1,0:T(8,128)S(1)}, u32[]{:S(2)}, u32[]{:S(2)}) %all-to-all-start) | async-done | bytes 196640 | tf_op jit(solution)/shard_map/all_to_all | solution.py:312
  88.6 0.7 broadcast_in_dim.28
  89.3 8.3 %all-to-all-start.1 = ((f32[16,12,128]{2,1,0:T(8,128)}), f32[16,12,128]{2,1,0:T(8,128)S(1)}, u32[]{:S(2)}, u32[]{:S(2)}) async-start(f32[16,12,128]{2,1,0:T(8,128)} %broadcast_in_dim.28), calls=%async_computation.1 | async-start | bytes 262144 | tf_op jit(solution)/shard_map/all_to_all | solution.py:314
  97.6 10.0 %all-to-all-done.1 = f32[16,12,128]{2,1,0:T(8,128)S(1)} async-done(((f32[16,12,128]{2,1,0:T(8,128)}), f32[16,12,128]{2,1,0:T(8,128)S(1)}, u32[]{:S(2)}, u32[]{:S(2)}) %all-to-all-start.1) | async-done | bytes 98336 | tf_op jit(solution)/shard_map/all_to_all | solution.py:314
  107.6 0.7 broadcast_in_dim.29
  108.4 4.0 %all-to-all-start.2 = ((f32[32,12,128]{2,1,0:T(8,128)}), f32[32,12,128]{2,1,0:T(8,128)S(1)}, u32[]{:S(2)}, u32[]{:S(2)}) async-start(f32[32,12,128]{2,1,0:T(8,128)} %broadcast_in_dim.29), calls=%async_computation.2 | async-start | bytes 524288 | tf_op jit(solution)/shard_map/all_to_all | solution.py:316
  112.7 1.6 %shard_map.95 = (bf16[256,256]{1,0:T(8,128)(2,1)}, bf16[256,256]{1,0:T(8,128)(2,1)}) custom-call(bf16[4,8,16,128]{3,2,1,0:T(8,128)(2,1)S(1)} %get-tuple-element.24.f_ref, bf16[4,8,16,128]{3,2,1,0:T(8,128)(2,1)S(1)} %get-tuple-element.25.g_ref, bf16[32,1024]{1,0:T(8,128)(2,1)S(1)} %get-tuple-element.28.h2, ...), custom_call_target="tpu_custom_call" | custom-call | flops 100000000 | bytes 2000000 | tf_op jit(solution)/shard_map/pallas_call | solution.py:23
  114.3 9.3 %all-to-all-done.2 = f32[32,12,128]{2,1,0:T(8,128)S(1)} async-done(((f32[32,12,128]{2,1,0:T(8,128)}), f32[32,12,128]{2,1,0:T(8,128)S(1)}, u32[]{:S(2)}, u32[]{:S(2)}) %all-to-all-start.2) | async-done | bytes 196640 | tf_op jit(solution)/shard_map/all_to_all | solution.py:316
  123.6 1.0 shard_map.96
  124.7 0.8 copy.107
  (94 shorter events, 1.9 us)
Async XLA Ops:
  0.6 0.9 copy-start
  1.5 0.9 copy-start.1
  2.4 11.6 %copy-start.3 = (bf16[3,3,3,8,32]{4,3,2,1,0:T(8,128)(2,1)S(1)}, bf16[3,3,3,8,32]{4,3,2,1,0:T(8,128)(2,1)}, u32[]{:S(2)}) copy-start(bf16[3,3,3,8,32]{4,3,2,1,0:T(8,128)(2,1)} %param.9) | copy-start | bytes 41476
  3.1 11.3 %collective-permute-start = (bf16[4,4,16,128]{3,2,1,0:T(8,128)(2,1)S(1)}, bf16[4,4,16,128]{3,2,1,0:T(8,128)(2,1)S(1)}, u32[]{:S(2)}, u32[]{:S(2)}) collective-permute-start(bf16[4,4,16,128]{3,2,1,0:T(8,128)(2,1)S(1)} %get-tuple-element.26), channel_id=1, source_target_pairs={{0,1},{1,2},{2,3},{3,4},{4,5},{5,6},{6,7},{7,8},{8,9},{9,10},{10,1... | collective-permute-start | bytes 196616 | tf_op jit(solution)/shard_map/ppermute | solution.py:18
  12.0 2.1 %copy-start.4 = (bf16[3,3,3,32,8]{3,4,2,1,0:T(8,128)(2,1)S(1)}, bf16[3,3,3,32,8]{3,4,2,1,0:T(8,128)(2,1)}, u32[]{:S(2)}) copy-start(bf16[3,3,3,32,8]{3,4,2,1,0:T(8,128)(2,1)} %param.7) | copy-start | bytes 41476
  12.0 9.3 %collective-permute-start.1 = (bf16[4,2,16,128]{3,2,1,0:T(8,128)(2,1)S(1)}, bf16[4,2,16,128]{3,2,1,0:T(8,128)(2,1)S(1)}, u32[]{:S(2)}, u32[]{:S(2)}) collective-permute-start(bf16[4,2,16,128]{3,2,1,0:T(8,128)(2,1)S(1)} %get-tuple-element.27), channel_id=1, source_target_pairs={{0,15},{1,0},{2,1},{3,2},{4,3},{5,4},{6,5},{7,6},{8,7},{9,8},{10,9... | collective-permute-start | bytes 98312 | tf_op jit(solution)/shard_map/ppermute | solution.py:18
  21.4 3.0 %copy-start.2 = (bf16[3,3,3,32,32]{4,3,2,1,0:T(8,128)(2,1)S(1)}, bf16[3,3,3,32,32]{4,3,2,1,0:T(8,128)(2,1)}, u32[]{:S(2)}) copy-start(bf16[3,3,3,32,32]{4,3,2,1,0:T(8,128)(2,1)} %param.8) | copy-start | bytes 165892
  21.4 16.4 %collective-permute-start.2 = (bf16[48,16,128]{2,1,0:T(8,128)(2,1)S(1)}, bf16[48,16,128]{2,1,0:T(8,128)(2,1)S(1)}, u32[]{:S(2)}, u32[]{:S(2)}) collective-permute-start(bf16[48,16,128]{2,1,0:T(8,128)(2,1)S(1)} %pad_maximum_fusion.1), channel_id=1, source_target_pairs={{0,16},{16,32},{32,48},{48,64},{64,80},{80,96},{96,112},{112,128},... | collective-permute-start | bytes 589832 | tf_op jit(solution)/shard_map/ppermute | solution.py:18
  24.9 12.9 %collective-permute-start.3 = (bf16[26,16,128]{2,1,0:T(8,128)(2,1)S(1)}, bf16[26,16,128]{2,1,0:T(8,128)(2,1)S(1)}, u32[]{:S(2)}, u32[]{:S(2)}) collective-permute-start(bf16[26,16,128]{2,1,0:T(8,128)(2,1)S(1)} %bitcast.253), channel_id=1, source_target_pairs={{0,496},{16,0},{32,16},{48,32},{64,48},{80,64},{96,80},{112,96},{1... | collective-permute-start | bytes 319496 | tf_op jit(solution)/shard_map/ppermute | solution.py:18
  39.5 4.4 %collective-permute-start.5 = (bf16[2,32,128]{2,1,0:T(8,128)(2,1)S(1)}, bf16[2,32,128]{2,1,0:T(8,128)(2,1)S(1)}, u32[]{:S(2)}, u32[]{:S(2)}) collective-permute-start(bf16[2,32,128]{2,1,0:T(8,128)(2,1)S(1)} %get-tuple-element.30), channel_id=1, source_target_pairs={{0,1},{1,2},{2,3},{3,4},{4,5},{5,6},{6,7},{7,8},{8,9},{9,10},{10,1... | collective-permute-start | bytes 49160 | tf_op jit(solution)/shard_map/ppermute | solution.py:18
  41.4 9.3 %collective-permute-start.4 = (bf16[6,32,128]{2,1,0:T(8,128)(2,1)S(1)}, bf16[6,32,128]{2,1,0:T(8,128)(2,1)S(1)}, u32[]{:S(2)}, u32[]{:S(2)}) collective-permute-start(bf16[6,32,128]{2,1,0:T(8,128)(2,1)S(1)} %get-tuple-element.29), channel_id=1, source_target_pairs={{0,15},{1,0},{2,1},{3,2},{4,3},{5,4},{6,5},{7,6},{8,7},{9,8},{10,9... | collective-permute-start | bytes 147464 | tf_op jit(solution)/shard_map/ppermute | solution.py:18
  50.8 10.2 %collective-permute-start.7 = (bf16[7,32,128]{2,1,0:T(8,128)(2,1)S(1)}, bf16[7,32,128]{2,1,0:T(8,128)(2,1)S(1)}, u32[]{:S(2)}, u32[]{:S(2)}) collective-permute-start(bf16[7,32,128]{2,1,0:T(8,128)(2,1)S(1)} %pad_maximum_fusion.2), channel_id=1, source_target_pairs={{0,16},{16,32},{32,48},{48,64},{64,80},{80,96},{96,112},{112,128},... | collective-permute-start | bytes 172040 | tf_op jit(solution)/shard_map/ppermute | solution.py:18
  52.8 10.0 %collective-permute-start.6 = (bf16[19,32,128]{2,1,0:T(8,128)(2,1)S(1)}, bf16[19,32,128]{2,1,0:T(8,128)(2,1)S(1)}, u32[]{:S(2)}, u32[]{:S(2)}) collective-permute-start(bf16[19,32,128]{2,1,0:T(8,128)(2,1)S(1)} %constant_dynamic-update-slice_fusion.20), channel_id=1, source_target_pairs={{0,496},{16,0},{32,16},{48,32},{64,48},{80,64},{96,80},{112,96},{1... | collective-permute-start | bytes 466952 | tf_op jit(solution)/shard_map/ppermute | solution.py:18
  65.2 23.4 %all-to-all-start = ((f32[32,12,128]{2,1,0:T(8,128)}), f32[32,12,128]{2,1,0:T(8,128)S(1)}, u32[]{:S(2)}, u32[]{:S(2)}) async-start(f32[32,12,128]{2,1,0:T(8,128)} %reshape.71), calls=%async_computation | async-start | bytes 524288 | tf_op jit(solution)/shard_map/all_to_all | solution.py:312
  89.3 18.3 %all-to-all-start.1 = ((f32[16,12,128]{2,1,0:T(8,128)}), f32[16,12,128]{2,1,0:T(8,128)S(1)}, u32[]{:S(2)}, u32[]{:S(2)}) async-start(f32[16,12,128]{2,1,0:T(8,128)} %broadcast_in_dim.28), calls=%async_computation.1 | async-start | bytes 262144 | tf_op jit(solution)/shard_map/all_to_all | solution.py:314
  108.4 15.2 %all-to-all-start.2 = ((f32[32,12,128]{2,1,0:T(8,128)}), f32[32,12,128]{2,1,0:T(8,128)S(1)}, u32[]{:S(2)}, u32[]{:S(2)}) async-start(f32[32,12,128]{2,1,0:T(8,128)} %broadcast_in_dim.29), calls=%async_computation.2 | async-start | bytes 524288 | tf_op jit(solution)/shard_map/all_to_all | solution.py:316

commit v2 on v1

v2 whole, which is shorter than its diff:
```python
import jax
import jax.numpy as jnp
from jax import lax
from jax.experimental import pallas as pl
from jax.experimental.pallas import tpu as pltpu
from jax.sharding import Mesh
from jax.sharding import PartitionSpec as P

BF = jnp.bfloat16
F32 = jnp.float32
LANES = 128
LOCAL = [(i, j) for i in range(2) for j in range(4)]
UPPER = LOCAL + [(0, 4), (1, 4)] + [(2, j) for j in range(5)]
AROUND = [(i, j) for i in range(-1, 3) for j in range(-1, 5)]
ROW = 6 * LANES
ROWS = 384
GX = ("z", "yl")
GY = ("x", "yh", "core")


def shift(x, axis, by):
    devices = lax.axis_size(axis)
    return lax.ppermute(x, axis, [(i, (i + by) % devices) for i in range(devices)])


def call(body, outs, args, scratch=(), flops=10**8, space=pltpu.VMEM):
    moved = 2 * 10**6
    return pl.pallas_call(
        body,
        out_shape=[jax.ShapeDtypeStruct(s, d) for s, d in outs],
        in_specs=[pl.BlockSpec(memory_space=space)] * len(args),
        out_specs=[pl.BlockSpec(memory_space=pltpu.VMEM)] * len(outs),
        scratch_shapes=[pltpu.VMEM(*s) if isinstance(s, tuple) else s for s in scratch],
        compiler_params=pltpu.CompilerParams(vmem_limit_bytes=32 * 2**20),
        cost_estimate=pl.CostEstimate(flops=flops, bytes_accessed=moved, transcendentals=0),
    )(*args)


def dot(a, b):
    return lax.dot_general(a, b, (((1,), (0,)), ((), ())), preferred_element_type=F32)


def dot_nt(a, b):
    return lax.dot_general(a, b, (((1,), (1,)), ((), ())), preferred_element_type=F32)


def split_z():
    z = lax.broadcasted_iota(jnp.int32, (256, 256), 0)
    k = lax.broadcasted_iota(jnp.int32, (256, 256), 1)
    return (z == 2 * (k & 127) + (k >> 7)).astype(F32).astype(BF)


def join_z():
    k = lax.broadcasted_iota(jnp.int32, (256, 256), 0)
    z = lax.broadcasted_iota(jnp.int32, (256, 256), 1)
    return (z == 2 * (k & 127) + (k >> 7)).astype(F32).astype(BF)


def slab_order(dim):
    r = lax.broadcasted_iota(jnp.int32, (512, 512), dim)
    s = lax.broadcasted_iota(jnp.int32, (512, 512), 1 - dim)
    source = ((r >> 3) & 1) * 256 + (r & 7) * 32 + (r >> 7) * 8 + ((r >> 4) & 7)
    return (s == source).astype(F32).astype(BF)


def to_slabs_kernel(f_any, g_any, f_out, g_out, up_out, down_out, raw, sems):
    copies = [pltpu.make_async_copy(ref, raw.at[k], sems.at[k]) for k, ref in enumerate((f_any, g_any))]
    for copy in copies:
        copy.start()
    halves = split_z()
    order = slab_order(0)
    for k, out in enumerate((f_out, g_out)):
        copies[k].wait()
        z = dot(raw[k], halves).astype(BF)
        z = jnp.concatenate([z[:, :LANES], z[:, LANES:]], 0)
        out[...] = dot(order, z).astype(BF).reshape(4, 8, 16, LANES)
    up_out[:, 0:3] = f_out[:, 5:8]
    up_out[:, 3:4] = g_out[:, 7:8]
    down_out[...] = f_out[:, 0:2]


def rolled_odd(slab):
    return pltpu.roll(slab.astype(F32)[8:], 1, 1)


def act_and_slope(v):
    s = jax.nn.sigmoid(v)
    return 0.2 * v + 0.8 * v * s, 0.2 + 0.8 * (s + v * s * (1.0 - s))


def three(v):
    return jnp.concatenate([pltpu.roll(v, 1, 1), v, pltpu.roll(v, LANES - 1, 1)], 0).astype(BF)


def fill_columns(out, n, slab, pair, i, j):
    for a in range(3):
        x = 2 * i + a - 1
        tiles = [slab(x, 2 * j - 1), slab(x, 2 * j), slab(x, 2 * j + 1), pair(x, j - 1), pair(x, j)]
        for t, tile in enumerate(tiles):
            row = 80 * a + 16 * t
            out[row : row + 16, n * LANES : (n + 1) * LANES] = tile


def packed(v, step):
    total = None
    for k in range(4):
        part = v[step * k : step * (k + 1)]
        part = jnp.concatenate([part, jnp.zeros((part.shape[0], 96), F32)], 1)
        if part.shape[0] < step:
            part = jnp.concatenate([part, jnp.zeros((step - part.shape[0], LANES), F32)], 0)
        part = pltpu.roll(part, 32 * k, 1) if k else part
        total = part if total is None else total + part
    return total


def forward_kernel(
    f_ref, g_ref, ylo, yhi, xlo, xhi, wd, wm, wg, wb,
    grads_out, slope_out, h2_out, d2_out, up_out, down_out,
    fpair, gpair, h1_three, d2_three, slope, xcol, mcol, gcol, zcol,
):
    def f(x, y):
        if x < 0:
            return xlo[(x + 3) * 13 + y + 3]
        if x > 3:
            return xhi[(x - 4) * 13 + y + 3]
        return ylo[x, y + 3] if y < 0 else yhi[x, y - 8] if y > 7 else f_ref[x, y]

    def g(x, y):
        if x < 0:
            return xlo[39 + y + 1]
        return ylo[x, 3] if y < 0 else g_ref[x, y]

    zero = jnp.zeros((8, LANES), F32)
    for x in range(-3, 6):
        for j in range(-2, 5):
            first = zero if j == -2 else rolled_odd(f(x, 2 * j))
            fpair[x + 3, j + 2] = jnp.concatenate([first, rolled_odd(f(x, 2 * j + 1))], 0).astype(BF)
    for x in range(-1, 4):
        for j in range(-1, 4):
            first = zero if j == -1 else rolled_odd(g(x, 2 * j))
            gpair[x + 1, j + 1] = jnp.concatenate([first, rolled_odd(g(x, 2 * j + 1))], 0).astype(BF)

    def f_pair(x, j):
        return fpair[x + 3, j + 2]

    def g_pair(x, j):
        return gpair[x + 1, j + 1]

    for n, (i, j) in enumerate(LOCAL):
        fill_columns(gcol, n, g, g_pair, i, j)
    for n, (i, j) in enumerate(AROUND):
        fill_columns(xcol, n, f, f_pair, i, j)

    for i in range(-1, 3):
        start = (i + 1) * ROW
        v, s = act_and_slope(dot(wd[...], xcol[:, start : start + ROW]))
        slope[:, start : start + ROW] = s
        for j in range(-1, 5):
            lanes = slice((j + 1) * LANES, (j + 2) * LANES)
            h1_three[i + 1, j + 1] = three(v[:, lanes])
            if i >= 0 and j >= 0:
                slope_out[i * 5 + j] = s[:, lanes]

    for n, (i, j) in enumerate(LOCAL):
        for a in range(3):
            for b in range(3):
                row = 96 * (3 * a + b)
                mcol[row : row + 96, n * LANES : (n + 1) * LANES] = h1_three[i + a, j + b]

    for start in range(0, 8, 4):
        lanes = slice(start * LANES, (start + 4) * LANES)
        v, s = act_and_slope(dot(wm[...], mcol[:, lanes]))
        h2_out[:, lanes] = v.astype(BF)
        d2_out[:, lanes] = (dot(wg[...], gcol[:, lanes]) * s).astype(BF)
    for i in range(2):
        at = 4 * i * LANES
        up_out[i] = d2_out[:, at + 3 * LANES : at + 4 * LANES]
        down_out[i] = d2_out[:, at : at + LANES]
        down_out[2 + i] = d2_out[:, at + LANES : at + 2 * LANES]
        down_out[4 + i] = h2_out[:, at : at + LANES]
    for n, (i, j) in enumerate(LOCAL):
        d2_three[i, j] = three(d2_out[:, n * LANES : (n + 1) * LANES].astype(F32))

    down = jnp.zeros((240, 64), F32)
    for i in range(-1, 3):
        inside = [a for a in range(3) if 0 <= i + a - 1 <= 1]
        depth = 288 * len(inside)
        for m, a in enumerate(inside):
            for b in range(3):
                row = 288 * m + 96 * b
                for j in range(-1, 5):
                    lanes = slice((j + 1) * LANES, (j + 2) * LANES)
                    near = 0 <= j + b - 1 <= 3
                    zcol[row : row + 96, lanes] = d2_three[i + a - 1, j + b - 1] if near else jnp.zeros((96, LANES), BF)
        start = (i + 1) * ROW
        part = dot(wb[i + 1, :, :depth], zcol[:depth]) * slope[:, start : start + ROW]
        high = part.astype(BF)
        low = (part - high.astype(F32)).astype(BF)
        down += dot_nt(xcol[:, start : start + ROW], jnp.concatenate([high, low], 0))
    rows = jnp.concatenate(
        [
            packed(dot_nt(mcol[...], d2_out[...]), 224),
            packed(down[:, :32] + down[:, 32:], 64),
            packed(dot_nt(gcol[...], h2_out[...]), 64),
            jnp.zeros((ROWS - 352, LANES), F32),
        ],
        0,
    )
    grads_out[...] = rows.reshape(grads_out.shape)


def outputs_kernel(
    f_ref, g_ref, h2, d2, ylo, yhi, xlo, xhi, slope, wb, wu, wv,
    mapped_out, grad_out, d2_three, mcol, d1, ucol, slabs,
):
    def d(i, j):
        if i < 0:
            return xlo[j + 1]
        if i > 1:
            return xhi[(i - 2) * 7 + j + 1]
        if j < 0:
            return ylo[i]
        if j > 3:
            return yhi[2 * (j - 4) + i]
        at = (4 * i + j) * LANES
        return d2[:, at : at + LANES]

    for i in range(-1, 4):
        for j in range(-1, 6):
            d2_three[i + 1, j + 1] = three(d(i, j).astype(F32))
    for n, (i, j) in enumerate(UPPER):
        for a in range(3):
            for b in range(3):
                row = 96 * (3 * a + b)
                mcol[row : row + 96, n * LANES : (n + 1) * LANES] = d2_three[i + a, j + b]
    for start in range(0, 15, 4):
        cells = UPPER[start : start + 4]
        v = dot(wb[...], mcol[:, start * LANES : (start + len(cells)) * LANES])
        for n, (i, j) in enumerate(cells):
            at = (start + n) * LANES
            d1[:, at : at + LANES] = (v[:, n * LANES : (n + 1) * LANES] * slope[i * 5 + j]).astype(BF)

    def h(i, j):
        if i > 1:
            return xhi[14 + j]
        if j > 3:
            return yhi[4 + i]
        at = (4 * i + j) * LANES
        return h2[:, at : at + LANES]

    def p(i, j):
        at = UPPER.index((i, j)) * LANES
        return d1[:, at : at + LANES]

    joined = join_z()
    order = slab_order(1)
    for cell, w, base, out in ((h, wu, f_ref, mapped_out), (p, wv, g_ref, grad_out)):
        two = {}
        for i, j in UPPER:
            v = cell(i, j).astype(F32)
            two[i, j] = jnp.concatenate([v, pltpu.roll(v, LANES - 1, 1)], 0).astype(BF)
        for n, (i, j) in enumerate(LOCAL):
            for k in range(4):
                ucol[64 * k : 64 * k + 64, n * LANES : (n + 1) * LANES] = two[i + k // 2, j + k % 2]
        for start in range(0, 8, 2):
            up = dot(w[...], ucol[:, start * LANES : (start + 2) * LANES])
            for n in range(2):
                i, j = LOCAL[start + n]
                for k in range(4):
                    x, y = 2 * i + k // 2, 2 * j + k % 2
                    row = 16 * (8 * x + y)
                    added = base[x, y].astype(F32) + up[16 * k : 16 * k + 16, n * LANES : (n + 1) * LANES]
                    slabs[row : row + 16] = added.astype(BF)
        z = dot(order, slabs[...]).astype(BF)
        out[...] = dot(jnp.concatenate([z[:256], z[256:]], 1), joined).astype(BF)


def tap_rows(rows):
    order = [(0, 1), (0, 2), (1, 1), (1, 2), (2, 1), (2, 2), None, (0, 0), (1, 0), (2, 0)]
    for a in range(3):
        for m, tap in enumerate(order):
            if tap is not None:
                yield 10 * a + m, 9 * a + 3 * tap[0] + tap[1]


def unpack_kernel(total, down_out, mid_out, up_out):
    total = total[...].reshape(ROWS, LANES)
    flipped = jnp.concatenate([total[0:224], jnp.zeros((32, LANES), F32)], 0).T
    for tap in range(27):
        k, m = tap // 7, tap % 7
        rows = flipped[32 * k : 32 * k + 32, LANES * (m // 4) : LANES * (m // 4 + 1)]
        rows = pltpu.roll(rows, LANES - 32 * (m % 4), 1) if m % 4 else rows
        mid_out[tap] = rows[:, :32]
    for k in range(4):
        parts = total[224:352]
        parts = pltpu.roll(parts, LANES - 32 * k, 1) if k else parts
        for block, tap in tap_rows(240):
            if block // 8 == k:
                row = 8 * (block % 8)
                down_out[tap] = parts[row : row + 8, :32]
                up_out[tap] = parts[64 + row : 64 + row + 8, :32]


def down_weights(w):
    none = jnp.zeros_like(w[:, 0, 0])
    blocks = [w[:, 0, 1], w[:, 0, 2], w[:, 1, 1], w[:, 1, 2], w[:, 2, 1], w[:, 2, 2], none, w[:, 0, 0], w[:, 1, 0], w[:, 2, 0]]
    return jnp.transpose(jnp.stack(blocks, 1), (2, 0, 1, 3)).reshape(32, 240)


def up_weights(w):
    none = jnp.zeros_like(w[0, 0, 0])
    pick = ((1, None), (2, 0))
    rows = []
    for p in range(2):
        for q in range(2):
            for r in range(2):
                row = []
                for k in range(8):
                    a, b, d = pick[p][k // 4], pick[q][k // 2 % 2], pick[r][k % 2]
                    row.append(none if None in (a, b, d) else w[a, b, d])
                rows.append(jnp.concatenate(row, 1))
    return jnp.concatenate(rows, 0)


def all_sum(part):
    def spread(x, axes):
        return jnp.broadcast_to(x[None], (lax.axis_size(axes),) + x.shape)

    part = lax.all_to_all(part, ("x", "core"), 0, 0, tiled=True).sum(0)
    for axes in (("z",), ("yl", "yh")):
        part = lax.all_to_all(spread(part, axes), axes, 0, 0, tiled=True).sum(0)
    return lax.all_to_all(spread(part, ("x", "core")), ("x", "core"), 0, 0, tiled=True)


def local(fields, cotangent, w_down, w_mid, w_up):
    w_down_swapped = jnp.swapaxes(w_down, 3, 4)
    wd = down_weights(w_down)
    wg = down_weights(jnp.swapaxes(w_up, 3, 4))
    wm = jnp.transpose(w_mid, (3, 0, 1, 2, 4)).reshape(32, 864)
    wb = jnp.transpose(w_mid[::-1, ::-1, ::-1], (4, 0, 1, 2, 3)).reshape(32, 864)
    none = jnp.zeros((32, 288), BF)
    wb_rows = jnp.stack([jnp.concatenate([wb[:, 576:], none], 1), wb[:, 288:], wb[:, :576], jnp.concatenate([wb[:, :288], none], 1)], 0)
    wu = up_weights(w_up)
    wv = up_weights(w_down_swapped)

    f, g, up, down = call(
        to_slabs_kernel,
        [((4, 8, 16, LANES), BF)] * 2 + [((4, 4, 16, LANES), BF), ((4, 2, 16, LANES), BF)],
        [fields.reshape(256, 256), cotangent.reshape(256, 256)],
        [((2, 256, 256), BF), pltpu.SemaphoreType.DMA((2,))],
        space=pl.ANY,
    )
    ylo, yhi = shift(up, GY, 1), shift(down, GY, -1)
    f_ext = jnp.concatenate([ylo[:, :3], f, yhi], 1)
    last = jnp.concatenate([f_ext[1:].reshape(39, 16, LANES), ylo[3, 3:4], g[3]], 0)
    xlo = shift(last, GX, 1)
    xhi = shift(f_ext[:2].reshape(26, 16, LANES), GX, -1)

    parts = lax.axis_size(("x", "core"))
    grads, slope, h2, d2, up, down = call(
        forward_kernel,
        [((parts, ROWS // parts, LANES), F32), ((15, 32, LANES), F32), ((32, 8 * LANES), BF), ((32, 8 * LANES), BF),
         ((2, 32, LANES), BF), ((6, 32, LANES), BF)],
        [f, g, ylo, yhi, xlo, xhi, wd, wm, wg, wb_rows],
        [((9, 7, 16, LANES), BF), ((5, 5, 16, LANES), BF), ((4, 6, 96, LANES), BF), ((2, 4, 96, LANES), BF),
         ((32, 4 * ROW), F32), ((240, 4 * ROW), BF), ((864, 8 * LANES), BF), ((240, 8 * LANES), BF), ((576, ROW), BF)],
    )
    ylo, yhi = shift(up, GY, 1), shift(down, GY, -1)
    cells = jnp.transpose(d2.reshape(32, 8, LANES), (1, 0, 2))
    last = jnp.concatenate([ylo[1:2], cells[4:8], yhi[1:2], yhi[3:4]], 0)
    first = jnp.concatenate(
        [ylo[0:1], cells[0:4], yhi[0:1], yhi[2:3], last]
        + [h2[None, :, j * LANES : (j + 1) * LANES] for j in range(4)] + [yhi[4:5]], 0
    )
    xlo = shift(last, GX, 1)
    xhi = shift(first, GX, -1)

    mapped, grad_fields = call(
        outputs_kernel,
        [((256, 256), BF)] * 2,
        [f, g, h2, d2, ylo, yhi, xlo, xhi, slope, wb, wu, wv],
        [((5, 7, 96, LANES), BF), ((864, 15 * LANES), BF), ((32, 15 * LANES), BF), ((256, 8 * LANES), BF), ((512, LANES), BF)],
    )
    grad_down, grad_mid, grad_up = call(
        unpack_kernel,
        [((27, 8, 32), F32), ((27, 32, 32), F32), ((27, 8, 32), F32)],
        [all_sum(grads)],
    )
    return (
        mapped.reshape(fields.shape),
        grad_fields.reshape(fields.shape),
        jnp.swapaxes(grad_down.reshape(w_down_swapped.shape), 3, 4),
        grad_mid.reshape(w_mid.shape),
        grad_up.reshape(w_up.shape),
    )


def solution(mesh):
    nx, ny = mesh.devices.shape
    fine = Mesh(mesh.devices.reshape(nx // 4, 4, ny // 4, 2, 2), GX + GY)
    block = P(None, GX, GY, None)
    specs = (block, block, P(), P(), P())
    return jax.shard_map(local, mesh=fine, in_specs=specs, out_specs=specs, check_vma=False)
```

time: 126 us -> 113 us (0.90)
  waiting for transfers between devices: 48.6 us -> 29.3 us
  starting transfers between devices: 62 us -> 65.8 us
  Pallas kernels: 6.67 us -> 9.22 us
    all_to_all x3 -> x4, waiting for transfers between devices: 30.6 us -> 16.8 us  [the longest x2 11 us: all_sum(): part = lax.all_to_all(spread(part, axes), axes, 0, 0, tiled=True).sum(0)]
    ppermute x8, waiting for transfers between devices: 18.1 us -> 12.5 us  [shift(): lax.ppermute(x, axis, [(i, (i + by) % devices) for i in range(devices)])]
    all_to_all x3 -> x4, starting transfers between devices: 23.8 us -> 28.2 us  [the longest x1 11.1 us: all_sum(): part = lax.all_to_all(part, ('x', 'core'), 0, 0, tiled=True).sum(0)]
    pallas_call x5 -> x4, Pallas kernels: 6.67 us -> 9.22 us  [call(): pl.pallas_call(body, out_shape=[jax.ShapeDtypeStruct(s, d) for s, d in ou...]
    unnamed x45 -> x49, local copies, waits for them, and re-layouts: 2.89 us -> 2.71 us
  transfers between devices with their start and end apart: 11 -> 12, of which waited for: 7 -> 7; matrix products, arithmetic and copies ran while one was open for 2% -> 3% of each run, Pallas kernels for 1% -> 2%
where the time goes in v2:
time: 113 us; the launch traced here: 112 us
  starting transfers between devices  65.8 us (58%)
  waiting for transfers between devices  29.3 us (26%)
  Pallas kernels  9.22 us (8%)
  local copies, waits for them, and re-layouts  6.56 us (6%)
    ppermute x8, starting transfers between devices, shift(): lax.ppermute(x, axis, [(i, (i + by) % devices) for i in range(devices)])  37.6 us
    ppermute x8, waiting for transfers between devices, shift(): lax.ppermute(x, axis, [(i, (i + by) % devices) for i in range(devices)])  12.5 us
    all_to_all x1, starting transfers between devices, all_sum(): part = lax.all_to_all(part, ('x', 'core'), 0, 0, tiled=True).sum(0)  11.1 us
    all_to_all x2, waiting for transfers between devices, all_sum(): part = lax.all_to_all(spread(part, axes), axes, 0, 0, tiled=True).sum(0)  11 us
    pallas_call x4, Pallas kernels, call(): pl.pallas_call(body, out_shape=[jax.ShapeDtypeStruct(s, d) for s, d in ou...  9.22 us
    all_to_all x1, starting transfers between devices, all_sum(): lax.all_to_all(spread(part, ('x', 'core')), ('x', 'core'), 0, 0, tiled=True)  8.62 us
    all_to_all x2, starting transfers between devices, all_sum(): part = lax.all_to_all(spread(part, axes), axes, 0, 0, tiled=True).sum(0)  8.53 us
    all_to_all x1, waiting for transfers between devices, all_sum(): part = lax.all_to_all(part, ('x', 'core'), 0, 0, tiled=True).sum(0)  5.78 us
  transfers between devices with their start and end apart: 12, of which 7 were waited for; matrix products, arithmetic and copies ran while one was open for 3% of the time, Pallas kernels for 2%

profile of v2, /device:TPU:1, one launch (start us, length us, event | category | flops | bytes accessed | tf_op | source)
XLA Modules:
  0.0 112.4 jit_solution(11284060514252929607)
XLA Ops:
  0.6 0.9 copy-done
  1.5 0.9 copy-done.1
  2.4 1.8 %shard_map.92 = (bf16[4,8,16,128]{3,2,1,0:T(8,128)(2,1)S(1)}, bf16[4,8,16,128]{3,2,1,0:T(8,128)(2,1)S(1)}, bf16[4,4,16,128]{3,2,1,0:T(8,128)(2,1)S(1)}, bf16[4,2,16,128]{3,2,1,0:T(8,128)(2,1)S(1)}) custom-call(bf16[256,256]{1,0:T(8,128)(2,1)S(1)} %bitcast.244, bf16[256,256]{1,0:T(8,128)(2,1)S(1)} %bitcast.245), custom_call_target="tpu_custom_call" | custom-call | flops 100000000 | bytes 2000000 | tf_op jit(solution)/shard_map/pallas_call | solution.py:28
  4.3 9.0 %collective-permute-start = (bf16[4,4,16,128]{3,2,1,0:T(8,128)(2,1)S(1)}, bf16[4,4,16,128]{3,2,1,0:T(8,128)(2,1)S(1)}, u32[]{:S(2)}, u32[]{:S(2)}) collective-permute-start(bf16[4,4,16,128]{3,2,1,0:T(8,128)(2,1)S(1)} %get-tuple-element.22), channel_id=1, source_target_pairs={{0,1},{1,2},{2,3},{3,4},{4,5},{5,6},{6,7},{7,8},{8,9},{9,10},{10,1... | collective-permute-start | bytes 196616 | tf_op jit(solution)/shard_map/ppermute | solution.py:23
  13.3 1.9 %collective-permute-start.1 = (bf16[4,2,16,128]{3,2,1,0:T(8,128)(2,1)S(1)}, bf16[4,2,16,128]{3,2,1,0:T(8,128)(2,1)S(1)}, u32[]{:S(2)}, u32[]{:S(2)}) collective-permute-start(bf16[4,2,16,128]{3,2,1,0:T(8,128)(2,1)S(1)} %get-tuple-element.23), channel_id=1, source_target_pairs={{0,15},{1,0},{2,1},{3,2},{4,3},{5,4},{6,5},{7,6},{8,7},{9,8},{10,9... | collective-permute-start | bytes 98312 | tf_op jit(solution)/shard_map/ppermute | solution.py:23
  15.5 0.1 copy.79.wb
  15.7 0.6 copy-done.5
  17.6 0.2 copy.65
  17.8 0.2 reshape.60.wm
  18.3 4.2 %collective-permute-done.1.yhi = bf16[4,2,16,128]{3,2,1,0:T(8,128)(2,1)S(1)} collective-permute-done((bf16[4,2,16,128]{3,2,1,0:T(8,128)(2,1)S(1)}, bf16[4,2,16,128]{3,2,1,0:T(8,128)(2,1)S(1)}, u32[]{:S(2)}, u32[]{:S(2)}) %collective-permute-start.1) | collective-permute-done | bytes 32800 | tf_op jit(solution)/shard_map/ppermute | solution.py:23
  22.6 2.6 %collective-permute-start.2 = (bf16[48,16,128]{2,1,0:T(8,128)(2,1)S(1)}, bf16[48,16,128]{2,1,0:T(8,128)(2,1)S(1)}, u32[]{:S(2)}, u32[]{:S(2)}) collective-permute-start(bf16[48,16,128]{2,1,0:T(8,128)(2,1)S(1)} %pad_maximum_fusion.1), channel_id=1, source_target_pairs={{0,16},{16,32},{32,48},{48,64},{64,80},{80,96},{96,112},{112,128},... | collective-permute-start | bytes 589832 | tf_op jit(solution)/shard_map/ppermute | solution.py:23
  25.2 10.4 %collective-permute-start.3 = (bf16[26,16,128]{2,1,0:T(8,128)(2,1)S(1)}, bf16[26,16,128]{2,1,0:T(8,128)(2,1)S(1)}, u32[]{:S(2)}, u32[]{:S(2)}) collective-permute-start(bf16[26,16,128]{2,1,0:T(8,128)(2,1)S(1)} %bitcast.262), channel_id=1, source_target_pairs={{0,496},{16,0},{32,16},{48,32},{64,48},{80,64},{96,80},{112,96},{1... | collective-permute-start | bytes 319496 | tf_op jit(solution)/shard_map/ppermute | solution.py:23
  35.6 1.7 %collective-permute-done.3.xhi = bf16[26,16,128]{2,1,0:T(8,128)(2,1)S(1)} collective-permute-done((bf16[26,16,128]{2,1,0:T(8,128)(2,1)S(1)}, bf16[26,16,128]{2,1,0:T(8,128)(2,1)S(1)}, u32[]{:S(2)}, u32[]{:S(2)}) %collective-permute-start.3) | collective-permute-done | bytes 106528 | tf_op jit(solution)/shard_map/ppermute | solution.py:23
  37.3 0.8 collective-permute-done.2.xlo
  38.1 3.6 %shard_map.93 = (f32[8,48,128]{2,1,0:T(8,128)}, f32[15,32,128]{2,1,0:T(8,128)S(1)}, bf16[32,1024]{1,0:T(8,128)(2,1)S(1)}, bf16[32,1024]{1,0:T(8,128)(2,1)S(1)}, ...) custom-call(bf16[4,8,16,128]{3,2,1,0:T(8,128)(2,1)S(1)} %get-tuple-element.20.f_ref, ...), custom_call_target="tpu_custom_call" | custom-call | flops 100000000 | bytes 2000000 | tf_op jit(solution)/shard_map/pallas_call | solution.py:28
  41.7 3.4 %collective-permute-start.4 = (bf16[2,32,128]{2,1,0:T(8,128)(2,1)S(1)}, bf16[2,32,128]{2,1,0:T(8,128)(2,1)S(1)}, u32[]{:S(2)}, u32[]{:S(2)}) collective-permute-start(bf16[2,32,128]{2,1,0:T(8,128)(2,1)S(1)} %get-tuple-element.26), channel_id=1, source_target_pairs={{0,1},{1,2},{2,3},{3,4},{4,5},{5,6},{6,7},{7,8},{8,9},{9,10},{10,1... | collective-permute-start | bytes 49160 | tf_op jit(solution)/shard_map/ppermute | solution.py:23
  45.1 2.6 %collective-permute-start.5 = (bf16[6,32,128]{2,1,0:T(8,128)(2,1)S(1)}, bf16[6,32,128]{2,1,0:T(8,128)(2,1)S(1)}, u32[]{:S(2)}, u32[]{:S(2)}) collective-permute-start(bf16[6,32,128]{2,1,0:T(8,128)(2,1)S(1)} %get-tuple-element.27), channel_id=1, source_target_pairs={{0,15},{1,0},{2,1},{3,2},{4,3},{5,4},{6,5},{7,6},{8,7},{9,8},{10,9... | collective-permute-start | bytes 147464 | tf_op jit(solution)/shard_map/ppermute | solution.py:23
  47.7 11.1 %all-to-all-start = ((f32[8,48,128]{2,1,0:T(8,128)}), f32[8,48,128]{2,1,0:T(8,128)S(1)}, u32[]{:S(2)}, u32[]{:S(2)}) async-start(f32[8,48,128]{2,1,0:T(8,128)} %get-tuple-element.31), calls=%async_computation | async-start | bytes 393216 | tf_op jit(solution)/shard_map/all_to_all | solution.py:329
  58.8 5.8 %all-to-all-done = f32[8,48,128]{2,1,0:T(8,128)S(1)} async-done(((f32[8,48,128]{2,1,0:T(8,128)}), f32[8,48,128]{2,1,0:T(8,128)S(1)}, u32[]{:S(2)}, u32[]{:S(2)}) %all-to-all-start) | async-done | bytes 196640 | tf_op jit(solution)/shard_map/all_to_all | solution.py:329
  64.6 0.7 broadcast_in_dim.35
  65.3 5.1 %all-to-all-start.1 = ((f32[8,48,128]{2,1,0:T(8,128)}), f32[8,48,128]{2,1,0:T(8,128)S(1)}, u32[]{:S(2)}, u32[]{:S(2)}) async-start(f32[8,48,128]{2,1,0:T(8,128)} %broadcast_in_dim.35), calls=%async_computation.1 | async-start | bytes 393216 | tf_op jit(solution)/shard_map/all_to_all | solution.py:331
  70.5 8.5 %all-to-all-done.1 = f32[8,48,128]{2,1,0:T(8,128)S(1)} async-done(((f32[8,48,128]{2,1,0:T(8,128)}), f32[8,48,128]{2,1,0:T(8,128)S(1)}, u32[]{:S(2)}, u32[]{:S(2)}) %all-to-all-start.1) | async-done | bytes 196640 | tf_op jit(solution)/shard_map/all_to_all | solution.py:331
  79.0 0.7 broadcast_in_dim.36
  79.7 3.4 %all-to-all-start.2 = ((f32[8,48,128]{2,1,0:T(8,128)}), f32[8,48,128]{2,1,0:T(8,128)S(1)}, u32[]{:S(2)}, u32[]{:S(2)}) async-start(f32[8,48,128]{2,1,0:T(8,128)} %broadcast_in_dim.36), calls=%async_computation.2 | async-start | bytes 393216 | tf_op jit(solution)/shard_map/all_to_all | solution.py:331
  83.1 4.3 %collective-permute-start.7 = (bf16[19,32,128]{2,1,0:T(8,128)(2,1)S(1)}, bf16[19,32,128]{2,1,0:T(8,128)(2,1)S(1)}, u32[]{:S(2)}, u32[]{:S(2)}) collective-permute-start(bf16[19,32,128]{2,1,0:T(8,128)(2,1)S(1)} %get-tuple-element.94), channel_id=1, source_target_pairs={{0,496},{16,0},{32,16},{48,32},{64,48},{80,64},{96,80},{112,96},{1... | collective-permute-start | bytes 466952 | tf_op jit(solution)/shard_map/ppermute | solution.py:23
  87.4 2.5 %all-to-all-done.2 = f32[8,48,128]{2,1,0:T(8,128)S(1)} async-done(((f32[8,48,128]{2,1,0:T(8,128)}), f32[8,48,128]{2,1,0:T(8,128)S(1)}, u32[]{:S(2)}, u32[]{:S(2)}) %all-to-all-start.2) | async-done | bytes 196640 | tf_op jit(solution)/shard_map/all_to_all | solution.py:331
  89.9 0.7 broadcast_in_dim.37
  90.6 8.6 %all-to-all-start.3 = ((f32[8,48,128]{2,1,0:T(8,128)}), f32[8,48,128]{2,1,0:T(8,128)S(1)}, u32[]{:S(2)}, u32[]{:S(2)}) async-start(f32[8,48,128]{2,1,0:T(8,128)} %broadcast_in_dim.37), calls=%async_computation.3 | async-start | bytes 393216 | tf_op jit(solution)/shard_map/all_to_all | solution.py:332
  99.3 3.5 %collective-permute-start.6 = (bf16[7,32,128]{2,1,0:T(8,128)(2,1)S(1)}, bf16[7,32,128]{2,1,0:T(8,128)(2,1)S(1)}, u32[]{:S(2)}, u32[]{:S(2)}) collective-permute-start(bf16[7,32,128]{2,1,0:T(8,128)(2,1)S(1)} %pad_maximum_fusion.3), channel_id=1, source_target_pairs={{0,16},{16,32},{32,48},{48,64},{64,80},{80,96},{96,112},{112,128},... | collective-permute-start | bytes 172040 | tf_op jit(solution)/shard_map/ppermute | solution.py:23
  102.8 5.8 %collective-permute-done.6.xlo = bf16[7,32,128]{2,1,0:T(8,128)(2,1)S(1)} collective-permute-done((bf16[7,32,128]{2,1,0:T(8,128)(2,1)S(1)}, bf16[7,32,128]{2,1,0:T(8,128)(2,1)S(1)}, u32[]{:S(2)}, u32[]{:S(2)}) %collective-permute-start.6) | collective-permute-done | bytes 57376 | tf_op jit(solution)/shard_map/ppermute | solution.py:23
  108.6 2.8 %shard_map.94 = (bf16[256,256]{1,0:T(8,128)(2,1)}, bf16[256,256]{1,0:T(8,128)(2,1)}) custom-call(bf16[4,8,16,128]{3,2,1,0:T(8,128)(2,1)S(1)} %get-tuple-element.20.f_ref, bf16[4,8,16,128]{3,2,1,0:T(8,128)(2,1)S(1)} %get-tuple-element.21.g_ref, bf16[32,1024]{1,0:T(8,128)(2,1)S(1)} %get-tuple-element.24.h2, bf16[32,1024]{1,0:T(8,128)(2,1)S(1)} %get-tuple-element.25.d2, ...), custom_call_target="tpu_custom_call" | custom-call | flops 100000000 | bytes 2000000 | tf_op jit(solution)/shard_map/pallas_call | solution.py:28
  111.3 1.0 shard_map.95
  (100 shorter events, 2.1 us)
Async XLA Ops:
  0.6 0.9 copy-start
  1.5 0.9 copy-start.1
  2.4 12.7 %copy-start.3 = (bf16[3,3,3,8,32]{4,3,2,1,0:T(8,128)(2,1)S(1)}, bf16[3,3,3,8,32]{4,3,2,1,0:T(8,128)(2,1)}, u32[]{:S(2)}) copy-start(bf16[3,3,3,8,32]{4,3,2,1,0:T(8,128)(2,1)} %param.9) | copy-start | bytes 41476
  2.4 12.8 %copy-start.4 = (bf16[3,3,3,32,8]{3,4,2,1,0:T(8,128)(2,1)S(1)}, bf16[3,3,3,32,8]{3,4,2,1,0:T(8,128)(2,1)}, u32[]{:S(2)}) copy-start(bf16[3,3,3,32,8]{3,4,2,1,0:T(8,128)(2,1)} %param.7) | copy-start | bytes 41476
  4.3 11.2 %copy-start.2 = (bf16[3,3,3,32,32]{4,3,2,1,0:T(8,128)(2,1)S(1)}, bf16[3,3,3,32,32]{4,3,2,1,0:T(8,128)(2,1)}, u32[]{:S(2)}) copy-start(bf16[3,3,3,32,32]{4,3,2,1,0:T(8,128)(2,1)} %param.8) | copy-start | bytes 165892
  4.3 14.0 %collective-permute-start = (bf16[4,4,16,128]{3,2,1,0:T(8,128)(2,1)S(1)}, bf16[4,4,16,128]{3,2,1,0:T(8,128)(2,1)S(1)}, u32[]{:S(2)}, u32[]{:S(2)}) collective-permute-start(bf16[4,4,16,128]{3,2,1,0:T(8,128)(2,1)S(1)} %get-tuple-element.22), channel_id=1, source_target_pairs={{0,1},{1,2},{2,3},{3,4},{4,5},{5,6},{6,7},{7,8},{8,9},{9,10},{10,1... | collective-permute-start | bytes 196616 | tf_op jit(solution)/shard_map/ppermute | solution.py:23
  13.3 9.2 %collective-permute-start.1 = (bf16[4,2,16,128]{3,2,1,0:T(8,128)(2,1)S(1)}, bf16[4,2,16,128]{3,2,1,0:T(8,128)(2,1)S(1)}, u32[]{:S(2)}, u32[]{:S(2)}) collective-permute-start(bf16[4,2,16,128]{3,2,1,0:T(8,128)(2,1)S(1)} %get-tuple-element.23), channel_id=1, source_target_pairs={{0,15},{1,0},{2,1},{3,2},{4,3},{5,4},{6,5},{7,6},{8,7},{9,8},{10,9... | collective-permute-start | bytes 98312 | tf_op jit(solution)/shard_map/ppermute | solution.py:23
  15.6 0.7 copy-start.5
  22.6 15.5 %collective-permute-start.2 = (bf16[48,16,128]{2,1,0:T(8,128)(2,1)S(1)}, bf16[48,16,128]{2,1,0:T(8,128)(2,1)S(1)}, u32[]{:S(2)}, u32[]{:S(2)}) collective-permute-start(bf16[48,16,128]{2,1,0:T(8,128)(2,1)S(1)} %pad_maximum_fusion.1), channel_id=1, source_target_pairs={{0,16},{16,32},{32,48},{48,64},{64,80},{80,96},{96,112},{112,128},... | collective-permute-start | bytes 589832 | tf_op jit(solution)/shard_map/ppermute | solution.py:23
  25.2 12.1 %collective-permute-start.3 = (bf16[26,16,128]{2,1,0:T(8,128)(2,1)S(1)}, bf16[26,16,128]{2,1,0:T(8,128)(2,1)S(1)}, u32[]{:S(2)}, u32[]{:S(2)}) collective-permute-start(bf16[26,16,128]{2,1,0:T(8,128)(2,1)S(1)} %bitcast.262), channel_id=1, source_target_pairs={{0,496},{16,0},{32,16},{48,32},{64,48},{80,64},{96,80},{112,96},{1... | collective-permute-start | bytes 319496 | tf_op jit(solution)/shard_map/ppermute | solution.py:23
  41.7 17.0 %collective-permute-start.4 = (bf16[2,32,128]{2,1,0:T(8,128)(2,1)S(1)}, bf16[2,32,128]{2,1,0:T(8,128)(2,1)S(1)}, u32[]{:S(2)}, u32[]{:S(2)}) collective-permute-start(bf16[2,32,128]{2,1,0:T(8,128)(2,1)S(1)} %get-tuple-element.26), channel_id=1, source_target_pairs={{0,1},{1,2},{2,3},{3,4},{4,5},{5,6},{6,7},{7,8},{8,9},{9,10},{10,1... | collective-permute-start | bytes 49160 | tf_op jit(solution)/shard_map/ppermute | solution.py:23
  45.1 13.7 %collective-permute-start.5 = (bf16[6,32,128]{2,1,0:T(8,128)(2,1)S(1)}, bf16[6,32,128]{2,1,0:T(8,128)(2,1)S(1)}, u32[]{:S(2)}, u32[]{:S(2)}) collective-permute-start(bf16[6,32,128]{2,1,0:T(8,128)(2,1)S(1)} %get-tuple-element.27), channel_id=1, source_target_pairs={{0,15},{1,0},{2,1},{3,2},{4,3},{5,4},{6,5},{7,6},{8,7},{9,8},{10,9... | collective-permute-start | bytes 147464 | tf_op jit(solution)/shard_map/ppermute | solution.py:23
  47.7 17.0 %all-to-all-start = ((f32[8,48,128]{2,1,0:T(8,128)}), f32[8,48,128]{2,1,0:T(8,128)S(1)}, u32[]{:S(2)}, u32[]{:S(2)}) async-start(f32[8,48,128]{2,1,0:T(8,128)} %get-tuple-element.31), calls=%async_computation | async-start | bytes 393216 | tf_op jit(solution)/shard_map/all_to_all | solution.py:329
  65.3 13.7 %all-to-all-start.1 = ((f32[8,48,128]{2,1,0:T(8,128)}), f32[8,48,128]{2,1,0:T(8,128)S(1)}, u32[]{:S(2)}, u32[]{:S(2)}) async-start(f32[8,48,128]{2,1,0:T(8,128)} %broadcast_in_dim.35), calls=%async_computation.1 | async-start | bytes 393216 | tf_op jit(solution)/shard_map/all_to_all | solution.py:331
  79.7 10.2 %all-to-all-start.2 = ((f32[8,48,128]{2,1,0:T(8,128)}), f32[8,48,128]{2,1,0:T(8,128)S(1)}, u32[]{:S(2)}, u32[]{:S(2)}) async-start(f32[8,48,128]{2,1,0:T(8,128)} %broadcast_in_dim.36), calls=%async_computation.2 | async-start | bytes 393216 | tf_op jit(solution)/shard_map/all_to_all | solution.py:331
  83.1 25.4 %collective-permute-start.7 = (bf16[19,32,128]{2,1,0:T(8,128)(2,1)S(1)}, bf16[19,32,128]{2,1,0:T(8,128)(2,1)S(1)}, u32[]{:S(2)}, u32[]{:S(2)}) collective-permute-start(bf16[19,32,128]{2,1,0:T(8,128)(2,1)S(1)} %get-tuple-element.94), channel_id=1, source_target_pairs={{0,496},{16,0},{32,16},{48,32},{64,48},{80,64},{96,80},{112,96},{1... | collective-permute-start | bytes 466952 | tf_op jit(solution)/shard_map/ppermute | solution.py:23
  90.6 20.7 %all-to-all-start.3 = ((f32[8,48,128]{2,1,0:T(8,128)}), f32[8,48,128]{2,1,0:T(8,128)S(1)}, u32[]{:S(2)}, u32[]{:S(2)}) async-start(f32[8,48,128]{2,1,0:T(8,128)} %broadcast_in_dim.37), calls=%async_computation.3 | async-start | bytes 393216 | tf_op jit(solution)/shard_map/all_to_all | solution.py:332
  99.3 9.3 %collective-permute-start.6 = (bf16[7,32,128]{2,1,0:T(8,128)(2,1)S(1)}, bf16[7,32,128]{2,1,0:T(8,128)(2,1)S(1)}, u32[]{:S(2)}, u32[]{:S(2)}) collective-permute-start(bf16[7,32,128]{2,1,0:T(8,128)(2,1)S(1)} %pad_maximum_fusion.3), channel_id=1, source_target_pairs={{0,16},{16,32},{32,48},{48,64},{64,80},{80,96},{96,112},{112,128},... | collective-permute-start | bytes 172040 | tf_op jit(solution)/shard_map/ppermute | solution.py:23

commit v3 on v2

--- a/solution.py
+++ b/solution.py
@@ -11,11 +11,13 @@
 LANES = 128
 LOCAL = [(i, j) for i in range(2) for j in range(4)]
 UPPER = LOCAL + [(0, 4), (1, 4)] + [(2, j) for j in range(5)]
-AROUND = [(i, j) for i in range(-1, 3) for j in range(-1, 5)]
-ROW = 6 * LANES
+WIDE = LOCAL + [(i, j) for j in (-1, 4, 5) for i in range(2)]
+AROUND = [(i, j) for i in range(-1, 3) for j in range(-2, 7)]
+ROW = 9 * LANES
 ROWS = 384
 GX = ("z", "yl")
 GY = ("x", "yh", "core")
+XC, Y, Z = ("x", "core"), ("yl", "yh"), ("z",)
 
 
 def shift(x, axis, by):
@@ -23,17 +25,18 @@
     return lax.ppermute(x, axis, [(i, (i + by) % devices) for i in range(devices)])
 
 
-def call(body, outs, args, scratch=(), flops=10**8, space=pltpu.VMEM):
+def call(body, outs, args, scratch=(), after=()):
     moved = 2 * 10**6
+    flops = 10**8
     return pl.pallas_call(
         body,
         out_shape=[jax.ShapeDtypeStruct(s, d) for s, d in outs],
-        in_specs=[pl.BlockSpec(memory_space=space)] * len(args),
+        in_specs=[pl.BlockSpec(memory_space=pltpu.VMEM)] * len(args) + [pl.BlockSpec(memory_space=pl.ANY)] * len(after),
         out_specs=[pl.BlockSpec(memory_space=pltpu.VMEM)] * len(outs),
-        scratch_shapes=[pltpu.VMEM(*s) if isinstance(s, tuple) else s for s in scratch],
+        scratch_shapes=[pltpu.VMEM(*s) for s in scratch],
         compiler_params=pltpu.CompilerParams(vmem_limit_bytes=32 * 2**20),
         cost_estimate=pl.CostEstimate(flops=flops, bytes_accessed=moved, transcendentals=0),
-    )(*args)
+    )(*args, *after)
 
 
 def dot(a, b):
@@ -63,20 +66,17 @@
     return (s == source).astype(F32).astype(BF)
 
 
-def to_slabs_kernel(f_any, g_any, f_out, g_out, up_out, down_out, raw, sems):
-    copies = [pltpu.make_async_copy(ref, raw.at[k], sems.at[k]) for k, ref in enumerate((f_any, g_any))]
-    for copy in copies:
-        copy.start()
+def to_slabs_kernel(f_ref, g_ref, f_out, g_out, up_out, down_out):
     halves = split_z()
     order = slab_order(0)
-    for k, out in enumerate((f_out, g_out)):
-        copies[k].wait()
-        z = dot(raw[k], halves).astype(BF)
+    for ref, out in ((f_ref, f_out), (g_ref, g_out)):
+        z = dot(ref[...], halves).astype(BF)
         z = jnp.concatenate([z[:, :LANES], z[:, LANES:]], 0)
         out[...] = dot(order, z).astype(BF).reshape(4, 8, 16, LANES)
-    up_out[:, 0:3] = f_out[:, 5:8]
-    up_out[:, 3:4] = g_out[:, 7:8]
-    down_out[...] = f_out[:, 0:2]
+    up_out[:, 0:5] = f_out[:, 3:8]
+    up_out[:, 5:8] = g_out[:, 5:8]
+    down_out[:, 0:6] = f_out[:, 0:6]
+    down_out[:, 6:10] = g_out[:, 0:4]
 
 
 def rolled_odd(slab):
@@ -115,38 +115,38 @@
 
 def forward_kernel(
     f_ref, g_ref, ylo, yhi, xlo, xhi, wd, wm, wg, wb,
-    grads_out, slope_out, h2_out, d2_out, up_out, down_out,
+    grads_out, slope_out, h2_out, d2_out,
     fpair, gpair, h1_three, d2_three, slope, xcol, mcol, gcol, zcol,
 ):
     def f(x, y):
         if x < 0:
-            return xlo[(x + 3) * 13 + y + 3]
+            return xlo[(x + 3) * 19 + y + 5]
         if x > 3:
-            return xhi[(x - 4) * 13 + y + 3]
-        return ylo[x, y + 3] if y < 0 else yhi[x, y - 8] if y > 7 else f_ref[x, y]
+            return xhi[(x - 4) * 19 + y + 5]
+        return ylo[x, y + 5] if y < 0 else yhi[x, y - 8] if y > 7 else f_ref[x, y]
 
     def g(x, y):
         if x < 0:
-            return xlo[39 + y + 1]
-        return ylo[x, 3] if y < 0 else g_ref[x, y]
+            return xlo[57 + y + 3]
+        return ylo[x, 5 + y + 3] if y < 0 else yhi[x, 6 + y - 8] if y > 7 else g_ref[x, y]
 
     zero = jnp.zeros((8, LANES), F32)
     for x in range(-3, 6):
-        for j in range(-2, 5):
-            first = zero if j == -2 else rolled_odd(f(x, 2 * j))
-            fpair[x + 3, j + 2] = jnp.concatenate([first, rolled_odd(f(x, 2 * j + 1))], 0).astype(BF)
+        for j in range(-3, 7):
+            first = zero if j == -3 else rolled_odd(f(x, 2 * j))
+            fpair[x + 3, j + 3] = jnp.concatenate([first, rolled_odd(f(x, 2 * j + 1))], 0).astype(BF)
     for x in range(-1, 4):
-        for j in range(-1, 4):
-            first = zero if j == -1 else rolled_odd(g(x, 2 * j))
-            gpair[x + 1, j + 1] = jnp.concatenate([first, rolled_odd(g(x, 2 * j + 1))], 0).astype(BF)
+        for j in range(-2, 6):
+            first = zero if j == -2 else rolled_odd(g(x, 2 * j))
+            gpair[x + 1, j + 2] = jnp.concatenate([first, rolled_odd(g(x, 2 * j + 1))], 0).astype(BF)
 
     def f_pair(x, j):
-        return fpair[x + 3, j + 2]
+        return fpair[x + 3, j + 3]
 
     def g_pair(x, j):
-        return gpair[x + 1, j + 1]
-
-    for n, (i, j) in enumerate(LOCAL):
+        return gpair[x + 1, j + 2]
+
+    for n, (i, j) in enumerate(WIDE):
         fill_columns(gcol, n, g, g_pair, i, j)
     for n, (i, j) in enumerate(AROUND):
         fill_columns(xcol, n, f, f_pair, i, j)
@@ -155,29 +155,23 @@
         start = (i + 1) * ROW
         v, s = act_and_slope(dot(wd[...], xcol[:, start : start + ROW]))
         slope[:, start : start + ROW] = s
-        for j in range(-1, 5):
-            lanes = slice((j + 1) * LANES, (j + 2) * LANES)
-            h1_three[i + 1, j + 1] = three(v[:, lanes])
-            if i >= 0 and j >= 0:
+        for j in range(-2, 7):
+            lanes = slice((j + 2) * LANES, (j + 3) * LANES)
+            h1_three[i + 1, j + 2] = three(v[:, lanes])
+            if i >= 0 and 0 <= j <= 4:
                 slope_out[i * 5 + j] = s[:, lanes]
 
-    for n, (i, j) in enumerate(LOCAL):
+    for n, (i, j) in enumerate(WIDE):
         for a in range(3):
             for b in range(3):
                 row = 96 * (3 * a + b)
-                mcol[row : row + 96, n * LANES : (n + 1) * LANES] = h1_three[i + a, j + b]
-
-    for start in range(0, 8, 4):
-        lanes = slice(start * LANES, (start + 4) * LANES)
+                mcol[row : row + 96, n * LANES : (n + 1) * LANES] = h1_three[i + a, j + b + 1]
+
+    for start in range(0, 14, 7):
+        lanes = slice(start * LANES, (start + 7) * LANES)
         v, s = act_and_slope(dot(wm[...], mcol[:, lanes]))
         h2_out[:, lanes] = v.astype(BF)
         d2_out[:, lanes] = (dot(wg[...], gcol[:, lanes]) * s).astype(BF)
-    for i in range(2):
-        at = 4 * i * LANES
-        up_out[i] = d2_out[:, at + 3 * LANES : at + 4 * LANES]
-        down_out[i] = d2_out[:, at : at + LANES]
-        down_out[2 + i] = d2_out[:, at + LANES : at + 2 * LANES]
-        down_out[4 + i] = h2_out[:, at : at + LANES]
     for n, (i, j) in enumerate(LOCAL):
         d2_three[i, j] = three(d2_out[:, n * LANES : (n + 1) * LANES].astype(F32))
 
@@ -192,16 +186,16 @@
                     lanes = slice((j + 1) * LANES, (j + 2) * LANES)
                     near = 0 <= j + b - 1 <= 3
                     zcol[row : row + 96, lanes] = d2_three[i + a - 1, j + b - 1] if near else jnp.zeros((96, LANES), BF)
-        start = (i + 1) * ROW
-        part = dot(wb[i + 1, :, :depth], zcol[:depth]) * slope[:, start : start + ROW]
+        start = (i + 1) * ROW + LANES
+        part = dot(wb[i + 1, :, :depth], zcol[:depth]) * slope[:, start : start + 6 * LANES]
         high = part.astype(BF)
         low = (part - high.astype(F32)).astype(BF)
-        down += dot_nt(xcol[:, start : start + ROW], jnp.concatenate([high, low], 0))
+        down += dot_nt(xcol[:, start : start + 6 * LANES], jnp.concatenate([high, low], 0))
     rows = jnp.concatenate(
         [
-            packed(dot_nt(mcol[...], d2_out[...]), 224),
+            packed(dot_nt(mcol[:, : 8 * LANES], d2_out[:, : 8 * LANES]), 224),
             packed(down[:, :32] + down[:, 32:], 64),
-            packed(dot_nt(gcol[...], h2_out[...]), 64),
+            packed(dot_nt(gcol[:, : 8 * LANES], h2_out[:, : 8 * LANES]), 64),
             jnp.zeros((ROWS - 352, LANES), F32),
         ],
         0,
@@ -209,8 +203,22 @@
     grads_out[...] = rows.reshape(grads_out.shape)
 
 
+def cell_of(ref, i, j):
+    at = WIDE.index((i, j)) * LANES
+    return ref[:, at : at + LANES]
+
+
+def x_rows_kernel(h2, d2, after, up_out, down_out):
+    for j in range(7):
+        up_out[j] = cell_of(d2, 1, j - 1)
+        down_out[j] = cell_of(d2, 0, j - 1)
+        down_out[7 + j] = cell_of(d2, 1, j - 1)
+    for j in range(5):
+        down_out[14 + j] = cell_of(h2, 0, j)
+
+
 def outputs_kernel(
-    f_ref, g_ref, h2, d2, ylo, yhi, xlo, xhi, slope, wb, wu, wv,
+    f_ref, g_ref, h2, d2, xlo, xhi, slope, wb, wu, wv, after,
     mapped_out, grad_out, d2_three, mcol, d1, ucol, slabs,
 ):
     def d(i, j):
@@ -218,12 +226,7 @@
             return xlo[j + 1]
         if i > 1:
             return xhi[(i - 2) * 7 + j + 1]
-        if j < 0:
-            return ylo[i]
-        if j > 3:
-            return yhi[2 * (j - 4) + i]
-        at = (4 * i + j) * LANES
-        return d2[:, at : at + LANES]
+        return cell_of(d2, i, j)
 
     for i in range(-1, 4):
         for j in range(-1, 6):
@@ -243,10 +246,7 @@
     def h(i, j):
         if i > 1:
             return xhi[14 + j]
-        if j > 3:
-            return yhi[4 + i]
-        at = (4 * i + j) * LANES
-        return h2[:, at : at + LANES]
+        return cell_of(h2, i, j)
 
     def p(i, j):
         at = UPPER.index((i, j)) * LANES
@@ -322,14 +322,16 @@
     return jnp.concatenate(rows, 0)
 
 
-def all_sum(part):
-    def spread(x, axes):
-        return jnp.broadcast_to(x[None], (lax.axis_size(axes),) + x.shape)
-
-    part = lax.all_to_all(part, ("x", "core"), 0, 0, tiled=True).sum(0)
-    for axes in (("z",), ("yl", "yh")):
-        part = lax.all_to_all(spread(part, axes), axes, 0, 0, tiled=True).sum(0)
-    return lax.all_to_all(spread(part, ("x", "core")), ("x", "core"), 0, 0, tiled=True)
+def exchange(part, axes):
+    return lax.all_to_all(part, axes, 0, 0, tiled=True)
+
+
+def sum_kernel(got, *refs):
+    refs[-1][...] = jnp.broadcast_to(jnp.sum(got[...], 0, keepdims=True), refs[-1].shape)
+
+
+def sum_spread(got, axes, after=()):
+    return call(sum_kernel, [((lax.axis_size(axes),) + got.shape[1:], F32)], [got], after=after)[0]
 
 
 def local(fields, cotangent, w_down, w_mid, w_up):
@@ -345,46 +347,41 @@
 
     f, g, up, down = call(
         to_slabs_kernel,
-        [((4, 8, 16, LANES), BF)] * 2 + [((4, 4, 16, LANES), BF), ((4, 2, 16, LANES), BF)],
+        [((4, 8, 16, LANES), BF)] * 2 + [((4, 8, 16, LANES), BF), ((4, 10, 16, LANES), BF)],
         [fields.reshape(256, 256), cotangent.reshape(256, 256)],
-        [((2, 256, 256), BF), pltpu.SemaphoreType.DMA((2,))],
-        space=pl.ANY,
     )
     ylo, yhi = shift(up, GY, 1), shift(down, GY, -1)
-    f_ext = jnp.concatenate([ylo[:, :3], f, yhi], 1)
-    last = jnp.concatenate([f_ext[1:].reshape(39, 16, LANES), ylo[3, 3:4], g[3]], 0)
+    f_ext = jnp.concatenate([ylo[:, :5], f, yhi[:, :6]], 1)
+    last = jnp.concatenate([f_ext[1:].reshape(57, 16, LANES), ylo[3, 5:], g[3], yhi[3, 6:]], 0)
     xlo = shift(last, GX, 1)
-    xhi = shift(f_ext[:2].reshape(26, 16, LANES), GX, -1)
-
-    parts = lax.axis_size(("x", "core"))
-    grads, slope, h2, d2, up, down = call(
+    xhi = shift(f_ext[:2].reshape(38, 16, LANES), GX, -1)
+
+    parts = lax.axis_size(XC)
+    grads, slope, h2, d2 = call(
         forward_kernel,
-        [((parts, ROWS // parts, LANES), F32), ((15, 32, LANES), F32), ((32, 8 * LANES), BF), ((32, 8 * LANES), BF),
-         ((2, 32, LANES), BF), ((6, 32, LANES), BF)],
+        [((parts, ROWS // parts, LANES), F32), ((15, 32, LANES), F32), ((32, 14 * LANES), BF), ((32, 14 * LANES), BF)],
         [f, g, ylo, yhi, xlo, xhi, wd, wm, wg, wb_rows],
-        [((9, 7, 16, LANES), BF), ((5, 5, 16, LANES), BF), ((4, 6, 96, LANES), BF), ((2, 4, 96, LANES), BF),
-         ((32, 4 * ROW), F32), ((240, 4 * ROW), BF), ((864, 8 * LANES), BF), ((240, 8 * LANES), BF), ((576, ROW), BF)],
-    )
-    ylo, yhi = shift(up, GY, 1), shift(down, GY, -1)
-    cells = jnp.transpose(d2.reshape(32, 8, LANES), (1, 0, 2))
-    last = jnp.concatenate([ylo[1:2], cells[4:8], yhi[1:2], yhi[3:4]], 0)
-    first = jnp.concatenate(
-        [ylo[0:1], cells[0:4], yhi[0:1], yhi[2:3], last]
-        + [h2[None, :, j * LANES : (j + 1) * LANES] for j in range(4)] + [yhi[4:5]], 0
-    )
-    xlo = shift(last, GX, 1)
-    xhi = shift(first, GX, -1)
-
+        [((9, 10, 16, LANES), BF), ((5, 8, 16, LANES), BF), ((4, 9, 96, LANES), BF), ((2, 4, 96, LANES), BF),
+         ((32, 4 * ROW), F32), ((240, 4 * ROW), BF), ((864, 14 * LANES), BF), ((240, 14 * LANES), BF),
+         ((576, 6 * LANES), BF)],
+    )
+
+    got = exchange(grads, XC)
+    last, first = call(x_rows_kernel, [((7, 32, LANES), BF), ((19, 32, LANES), BF)], [h2, d2], after=[got])
+    xlo, xhi = shift(last, GX, 1), shift(first, GX, -1)
+    got = exchange(sum_spread(got, Z), Z)
+    got = exchange(sum_spread(got, Y, after=[xlo, xhi]), Y)
     mapped, grad_fields = call(
         outputs_kernel,
         [((256, 256), BF)] * 2,
-        [f, g, h2, d2, ylo, yhi, xlo, xhi, slope, wb, wu, wv],
+        [f, g, h2, d2, xlo, xhi, slope, wb, wu, wv],
         [((5, 7, 96, LANES), BF), ((864, 15 * LANES), BF), ((32, 15 * LANES), BF), ((256, 8 * LANES), BF), ((512, LANES), BF)],
+        after=[got],
     )
     grad_down, grad_mid, grad_up = call(
         unpack_kernel,
         [((27, 8, 32), F32), ((27, 32, 32), F32), ((27, 8, 32), F32)],
-        [all_sum(grads)],
+        [exchange(sum_spread(got, XC), XC)],
     )
     return (
         mapped.reshape(fields.shape),

time: 113 us -> 105 us (0.929)
  starting transfers between devices: 65.8 us -> 53.4 us
  waiting for transfers between devices: 29.3 us -> 32.8 us
  Pallas kernels: 9.22 us -> 10.9 us
    all_to_all x4, starting transfers between devices: 28.2 us -> 21.9 us  [exchange(): return lax.all_to_all(part, axes, 0, 0, tiled=True)]
    ppermute x8 -> x6, starting transfers between devices: 37.6 us -> 31.4 us  [shift(): lax.ppermute(x, axis, [(i, (i + by) % devices) for i in range(devices)])]
    ppermute x8 -> x6, waiting for transfers between devices: 12.5 us -> 17.5 us  [shift(): lax.ppermute(x, axis, [(i, (i + by) % devices) for i in range(devices)])]
    broadcast_in_dim x3 -> x0, local copies, waits for them, and re-layouts: 2.07 us -> none  [spread(): return jnp.broadcast_to(x[None], (lax.axis_size(axes),) + x.shape)]
    pallas_call x4 -> x8, Pallas kernels: 9.22 us -> 10.9 us  [call(): pl.pallas_call(body, out_shape=[jax.ShapeDtypeStruct(s, d) for s, d in ou...]
    all_to_all x4, waiting for transfers between devices: 16.8 us -> 15.3 us  [exchange(): return lax.all_to_all(part, axes, 0, 0, tiled=True)]
    unnamed x49 -> x41, local copies, waits for them, and re-layouts: 2.71 us -> 3.93 us
  transfers between devices with their start and end apart: 12 -> 10, of which waited for: 7 -> 7; matrix products, arithmetic and copies ran while one was open for 3% -> 2% of each run, Pallas kernels for 2% -> 3%
where the time goes in v3:
time: 105 us; the launch traced here: 104 us
  starting transfers between devices  53.4 us (51%)
  waiting for transfers between devices  32.8 us (31%)
  Pallas kernels  10.9 us (10%)
  local copies, waits for them, and re-layouts  5.69 us (5%)
    ppermute x6, starting transfers between devices, shift(): lax.ppermute(x, axis, [(i, (i + by) % devices) for i in range(devices)])  31.4 us
    all_to_all x4, starting transfers between devices, exchange(): return lax.all_to_all(part, axes, 0, 0, tiled=True)  21.9 us
    ppermute x6, waiting for transfers between devices, shift(): lax.ppermute(x, axis, [(i, (i + by) % devices) for i in range(devices)])  17.5 us
    all_to_all x4, waiting for transfers between devices, exchange(): return lax.all_to_all(part, axes, 0, 0, tiled=True)  15.3 us
    pallas_call x8, Pallas kernels, call(): pl.pallas_call(body, out_shape=[jax.ShapeDtypeStruct(s, d) for s, d in ou...  10.9 us
    unnamed x41, local copies, waits for them, and re-layouts  3.93 us
  transfers between devices with their start and end apart: 10, of which 7 were waited for; matrix products, arithmetic and copies ran while one was open for 2% of the time, Pallas kernels for 3%

profile of v3, /device:TPU:1, one launch (start us, length us, event | category | flops | bytes accessed | tf_op | source)
XLA Modules:
  0.0 104.2 jit_solution(10269560090306144378)
XLA Ops:
  0.6 0.9 copy-done.2
  1.5 0.9 copy-done.3
  2.4 0.7 shard_map.92
  3.2 8.8 %collective-permute-start = (bf16[4,8,16,128]{3,2,1,0:T(8,128)(2,1)S(1)}, bf16[4,8,16,128]{3,2,1,0:T(8,128)(2,1)S(1)}, u32[]{:S(2)}, u32[]{:S(2)}) collective-permute-start(bf16[4,8,16,128]{3,2,1,0:T(8,128)(2,1)S(1)} %get-tuple-element.22), channel_id=1, source_target_pairs={{0,1},{1,2},{2,3},{3,4},{4,5},{5,6},{6,7},{7,8},{8,9},{9,10},{10,1... | collective-permute-start | bytes 393224 | tf_op jit(solution)/shard_map/ppermute | solution.py:25
  12.0 1.9 %collective-permute-start.1 = (bf16[4,10,16,128]{3,2,1,0:T(8,128)(2,1)S(1)}, bf16[4,10,16,128]{3,2,1,0:T(8,128)(2,1)S(1)}, u32[]{:S(2)}, u32[]{:S(2)}) collective-permute-start(bf16[4,10,16,128]{3,2,1,0:T(8,128)(2,1)S(1)} %get-tuple-element.23), channel_id=1, source_target_pairs={{0,15},{1,0},{2,1},{3,2},{4,3},{5,4},{6,5},{7,6},{8,7},{9,8},{10,9... | collective-permute-start | bytes 491528 | tf_op jit(solution)/shard_map/ppermute | solution.py:25
  14.0 0.8 copy-done.6
  15.1 0.1 copy.54.wb
  15.2 0.5 copy-done.7
  15.9 0.6 copy-done
  16.6 6.1 %collective-permute-done.1.yhi = bf16[4,10,16,128]{3,2,1,0:T(8,128)(2,1)S(1)} collective-permute-done((bf16[4,10,16,128]{3,2,1,0:T(8,128)(2,1)S(1)}, bf16[4,10,16,128]{3,2,1,0:T(8,128)(2,1)S(1)}, u32[]{:S(2)}, u32[]{:S(2)}) %collective-permute-start.1) | collective-permute-done | bytes 163872 | tf_op jit(solution)/shard_map/ppermute | solution.py:25
  22.8 4.0 %collective-permute-start.2 = (bf16[72,16,128]{2,1,0:T(8,128)(2,1)S(1)}, bf16[72,16,128]{2,1,0:T(8,128)(2,1)S(1)}, u32[]{:S(2)}, u32[]{:S(2)}) collective-permute-start(bf16[72,16,128]{2,1,0:T(8,128)(2,1)S(1)} %pad_maximum_fusion.1), channel_id=1, source_target_pairs={{0,16},{16,32},{32,48},{48,64},{64,80},{80,96},{96,112},{112,128},... | collective-permute-start | bytes 884744 | tf_op jit(solution)/shard_map/ppermute | solution.py:25
  27.0 9.0 %collective-permute-start.3 = (bf16[38,16,128]{2,1,0:T(8,128)(2,1)S(1)}, bf16[38,16,128]{2,1,0:T(8,128)(2,1)S(1)}, u32[]{:S(2)}, u32[]{:S(2)}) collective-permute-start(bf16[38,16,128]{2,1,0:T(8,128)(2,1)S(1)} %bitcast.249), channel_id=1, source_target_pairs={{0,496},{16,0},{32,16},{48,32},{64,48},{80,64},{96,80},{112,96},{1... | collective-permute-start | bytes 466952 | tf_op jit(solution)/shard_map/ppermute | solution.py:25
  36.0 0.2 copy.41
  36.2 0.2 reshape.54.wm
  36.8 2.7 %collective-permute-done.3.xhi = bf16[38,16,128]{2,1,0:T(8,128)(2,1)S(1)} collective-permute-done((bf16[38,16,128]{2,1,0:T(8,128)(2,1)S(1)}, bf16[38,16,128]{2,1,0:T(8,128)(2,1)S(1)}, u32[]{:S(2)}, u32[]{:S(2)}) %collective-permute-start.3) | collective-permute-done | bytes 155680 | tf_op jit(solution)/shard_map/ppermute | solution.py:25
  39.5 1.9 %collective-permute-done.2.xlo = bf16[72,16,128]{2,1,0:T(8,128)(2,1)S(1)} collective-permute-done((bf16[72,16,128]{2,1,0:T(8,128)(2,1)S(1)}, bf16[72,16,128]{2,1,0:T(8,128)(2,1)S(1)}, u32[]{:S(2)}, u32[]{:S(2)}) %collective-permute-start.2) | collective-permute-done | bytes 294944 | tf_op jit(solution)/shard_map/ppermute | solution.py:25
  41.4 4.3 %shard_map.93 = (f32[8,48,128]{2,1,0:T(8,128)}, f32[15,32,128]{2,1,0:T(8,128)S(1)}, bf16[32,1792]{1,0:T(8,128)(2,1)S(1)}, bf16[32,1792]{1,0:T(8,128)(2,1)S(1)}) custom-call(bf16[4,8,16,128]{3,2,1,0:T(8,128)(2,1)S(1)} %get-tuple-element.20.f_ref, bf16[4,8,16,128]{3,2,1,0:T(8,128)(2,1)S(1)} %get-tuple-element.21.g_ref, bf16[4,8,16,128]{3,2,1,0:T(8,128)(2,1)S(1)} %copy-done.1, ...), custom_call_target="tpu_custom_call" | custom-call | flops 100000000 | bytes 2000000 | tf_op jit(solution)/shard_map/pallas_call | solution.py:31
  45.7 4.6 %all-to-all-start = ((f32[8,48,128]{2,1,0:T(8,128)}), f32[8,48,128]{2,1,0:T(8,128)S(1)}, u32[]{:S(2)}, u32[]{:S(2)}) async-start(f32[8,48,128]{2,1,0:T(8,128)} %get-tuple-element.26), calls=%async_computation | async-start | bytes 393216 | tf_op jit(solution)/shard_map/all_to_all | solution.py:326
  50.4 5.8 %all-to-all-done.after.got = f32[8,48,128]{2,1,0:T(8,128)S(1)} async-done(((f32[8,48,128]{2,1,0:T(8,128)}), f32[8,48,128]{2,1,0:T(8,128)S(1)}, u32[]{:S(2)}, u32[]{:S(2)}) %all-to-all-start) | async-done | bytes 196640 | tf_op jit(solution)/shard_map/all_to_all | solution.py:326
  56.2 0.7 shard_map.95
  56.9 4.9 %all-to-all-start.1 = ((f32[8,48,128]{2,1,0:T(8,128)}), f32[8,48,128]{2,1,0:T(8,128)S(1)}, u32[]{:S(2)}, u32[]{:S(2)}) async-start(f32[8,48,128]{2,1,0:T(8,128)} %shard_map.95), calls=%async_computation.1 | async-start | bytes 393216 | tf_op jit(solution)/shard_map/all_to_all | solution.py:326
  61.9 5.8 %collective-permute-start.5 = (bf16[19,32,128]{2,1,0:T(8,128)(2,1)S(1)}, bf16[19,32,128]{2,1,0:T(8,128)(2,1)S(1)}, u32[]{:S(2)}, u32[]{:S(2)}) collective-permute-start(bf16[19,32,128]{2,1,0:T(8,128)(2,1)S(1)} %get-tuple-element.28), channel_id=1, source_target_pairs={{0,496},{16,0},{32,16},{48,32},{64,48},{80,64},{96,80},{112,96},{1... | collective-permute-start | bytes 466952 | tf_op jit(solution)/shard_map/ppermute | solution.py:25
  67.8 1.9 %collective-permute-start.4 = (bf16[7,32,128]{2,1,0:T(8,128)(2,1)S(1)}, bf16[7,32,128]{2,1,0:T(8,128)(2,1)S(1)}, u32[]{:S(2)}, u32[]{:S(2)}) collective-permute-start(bf16[7,32,128]{2,1,0:T(8,128)(2,1)S(1)} %get-tuple-element.27), channel_id=1, source_target_pairs={{0,16},{16,32},{32,48},{48,64},{64,80},{80,96},{96,112},{112,128},... | collective-permute-start | bytes 172040 | tf_op jit(solution)/shard_map/ppermute | solution.py:25
  69.8 6.8 %collective-permute-done.4.refs_0_.xlo = bf16[7,32,128]{2,1,0:T(8,128)(2,1)S(1)} collective-permute-done((bf16[7,32,128]{2,1,0:T(8,128)(2,1)S(1)}, bf16[7,32,128]{2,1,0:T(8,128)(2,1)S(1)}, u32[]{:S(2)}, u32[]{:S(2)}) %collective-permute-start.4) | collective-permute-done | bytes 57376 | tf_op jit(solution)/shard_map/ppermute | solution.py:25
  76.7 0.7 shard_map.96
  77.4 4.7 %all-to-all-start.2 = ((f32[8,48,128]{2,1,0:T(8,128)}), f32[8,48,128]{2,1,0:T(8,128)S(1)}, u32[]{:S(2)}, u32[]{:S(2)}) async-start(f32[8,48,128]{2,1,0:T(8,128)} %shard_map.96), calls=%async_computation.2 | async-start | bytes 393216 | tf_op jit(solution)/shard_map/all_to_all | solution.py:326
  82.5 6.5 %all-to-all-done.2.after.got = f32[8,48,128]{2,1,0:T(8,128)S(1)} async-done(((f32[8,48,128]{2,1,0:T(8,128)}), f32[8,48,128]{2,1,0:T(8,128)S(1)}, u32[]{:S(2)}, u32[]{:S(2)}) %all-to-all-start.2) | async-done | bytes 196640 | tf_op jit(solution)/shard_map/all_to_all | solution.py:326
  88.9 0.7 shard_map.98
  89.6 7.7 %all-to-all-start.3 = ((f32[8,48,128]{2,1,0:T(8,128)}), f32[8,48,128]{2,1,0:T(8,128)S(1)}, u32[]{:S(2)}, u32[]{:S(2)}) async-start(f32[8,48,128]{2,1,0:T(8,128)} %shard_map.98), calls=%async_computation.3 | async-start | bytes 393216 | tf_op jit(solution)/shard_map/all_to_all | solution.py:326
  97.4 2.8 %shard_map.97 = (bf16[256,256]{1,0:T(8,128)(2,1)}, bf16[256,256]{1,0:T(8,128)(2,1)}) custom-call(bf16[4,8,16,128]{3,2,1,0:T(8,128)(2,1)S(1)} %get-tuple-element.20.f_ref, bf16[4,8,16,128]{3,2,1,0:T(8,128)(2,1)S(1)} %get-tuple-element.21.g_ref, bf16[32,1792]{1,0:T(8,128)(2,1)S(1)} %get-tuple-element.24.h2, bf16[32,1792]{1,0:T(8,128)(2,1)S(1)} %get-tuple-element.25.d2, ...), custom_call_target="tpu_custom_call" | custom-call | flops 100000000 | bytes 2000000 | tf_op jit(solution)/shard_map/pallas_call | solution.py:31
  100.1 3.0 %all-to-all-done.3.total = f32[8,48,128]{2,1,0:T(8,128)S(1)} async-done(((f32[8,48,128]{2,1,0:T(8,128)}), f32[8,48,128]{2,1,0:T(8,128)S(1)}, u32[]{:S(2)}, u32[]{:S(2)}) %all-to-all-start.3) | async-done | bytes 196640 | tf_op jit(solution)/shard_map/all_to_all | solution.py:326
  103.2 1.0 %shard_map.99 = (f32[27,8,32]{2,1,0:T(8,128)}, f32[27,32,32]{2,1,0:T(8,128)}, f32[27,8,32]{2,1,0:T(8,128)}) custom-call(f32[8,48,128]{2,1,0:T(8,128)S(1)} %all-to-all-done.3.total), custom_call_target="tpu_custom_call" | custom-call | flops 100000000 | bytes 2000000 | tf_op jit(solution)/shard_map/pallas_call | solution.py:31
  (86 shorter events, 2.0 us)
Async XLA Ops:
  0.6 0.9 copy-start.2
  1.5 0.9 copy-start.3
  2.4 11.5 %copy-start.5 = (bf16[3,3,3,32,8]{3,4,2,1,0:T(8,128)(2,1)S(1)}, bf16[3,3,3,32,8]{3,4,2,1,0:T(8,128)(2,1)}, u32[]{:S(2)}) copy-start(bf16[3,3,3,32,8]{3,4,2,1,0:T(8,128)(2,1)} %param.7) | copy-start | bytes 41476
  3.2 12.8 %collective-permute-start = (bf16[4,8,16,128]{3,2,1,0:T(8,128)(2,1)S(1)}, bf16[4,8,16,128]{3,2,1,0:T(8,128)(2,1)S(1)}, u32[]{:S(2)}, u32[]{:S(2)}) collective-permute-start(bf16[4,8,16,128]{3,2,1,0:T(8,128)(2,1)S(1)} %get-tuple-element.22), channel_id=1, source_target_pairs={{0,1},{1,2},{2,3},{3,4},{4,5},{5,6},{6,7},{7,8},{8,9},{9,10},{10,1... | collective-permute-start | bytes 393224 | tf_op jit(solution)/shard_map/ppermute | solution.py:25
  12.0 10.6 %collective-permute-start.1 = (bf16[4,10,16,128]{3,2,1,0:T(8,128)(2,1)S(1)}, bf16[4,10,16,128]{3,2,1,0:T(8,128)(2,1)S(1)}, u32[]{:S(2)}, u32[]{:S(2)}) collective-permute-start(bf16[4,10,16,128]{3,2,1,0:T(8,128)(2,1)S(1)} %get-tuple-element.23), channel_id=1, source_target_pairs={{0,15},{1,0},{2,1},{3,2},{4,3},{5,4},{6,5},{7,6},{8,7},{9,8},{10,9... | collective-permute-start | bytes 491528 | tf_op jit(solution)/shard_map/ppermute | solution.py:25
  14.0 0.8 copy-start.6
  14.0 1.0 copy-start.4
  15.1 0.7 copy-start.7
  15.9 0.7 copy-start
  16.6 6.1 %slice-start = ((bf16[4,8,16,128]{3,2,1,0:T(8,128)(2,1)}), bf16[4,5,16,128]{3,2,1,0:T(8,128)(2,1)S(1)}, s32[]{:S(2)}) async-start(bf16[4,8,16,128]{3,2,1,0:T(8,128)(2,1)} %copy-done), calls=%async_computation.4 | async-start | bytes 163840 | tf_op jit(solution)/shard_map/slice | solution.py:354
  22.8 18.6 %collective-permute-start.2 = (bf16[72,16,128]{2,1,0:T(8,128)(2,1)S(1)}, bf16[72,16,128]{2,1,0:T(8,128)(2,1)S(1)}, u32[]{:S(2)}, u32[]{:S(2)}) collective-permute-start(bf16[72,16,128]{2,1,0:T(8,128)(2,1)S(1)} %pad_maximum_fusion.1), channel_id=1, source_target_pairs={{0,16},{16,32},{32,48},{48,64},{64,80},{80,96},{96,112},{112,128},... | collective-permute-start | bytes 884744 | tf_op jit(solution)/shard_map/ppermute | solution.py:25
  27.0 12.5 %collective-permute-start.3 = (bf16[38,16,128]{2,1,0:T(8,128)(2,1)S(1)}, bf16[38,16,128]{2,1,0:T(8,128)(2,1)S(1)}, u32[]{:S(2)}, u32[]{:S(2)}) collective-permute-start(bf16[38,16,128]{2,1,0:T(8,128)(2,1)S(1)} %bitcast.249), channel_id=1, source_target_pairs={{0,496},{16,0},{32,16},{48,32},{64,48},{80,64},{96,80},{112,96},{1... | collective-permute-start | bytes 466952 | tf_op jit(solution)/shard_map/ppermute | solution.py:25
  36.8 4.6 %copy-start.1 = (bf16[4,8,16,128]{3,2,1,0:T(8,128)(2,1)S(1)}, bf16[4,8,16,128]{3,2,1,0:T(8,128)(2,1)}, u32[]{:S(2)}) copy-start(bf16[4,8,16,128]{3,2,1,0:T(8,128)(2,1)} %copy-done) | copy-start | bytes 393220
  45.7 10.5 %all-to-all-start = ((f32[8,48,128]{2,1,0:T(8,128)}), f32[8,48,128]{2,1,0:T(8,128)S(1)}, u32[]{:S(2)}, u32[]{:S(2)}) async-start(f32[8,48,128]{2,1,0:T(8,128)} %get-tuple-element.26), calls=%async_computation | async-start | bytes 393216 | tf_op jit(solution)/shard_map/all_to_all | solution.py:326
  56.9 19.8 %all-to-all-start.1 = ((f32[8,48,128]{2,1,0:T(8,128)}), f32[8,48,128]{2,1,0:T(8,128)S(1)}, u32[]{:S(2)}, u32[]{:S(2)}) async-start(f32[8,48,128]{2,1,0:T(8,128)} %shard_map.95), calls=%async_computation.1 | async-start | bytes 393216 | tf_op jit(solution)/shard_map/all_to_all | solution.py:326
  61.9 14.8 %collective-permute-start.5 = (bf16[19,32,128]{2,1,0:T(8,128)(2,1)S(1)}, bf16[19,32,128]{2,1,0:T(8,128)(2,1)S(1)}, u32[]{:S(2)}, u32[]{:S(2)}) collective-permute-start(bf16[19,32,128]{2,1,0:T(8,128)(2,1)S(1)} %get-tuple-element.28), channel_id=1, source_target_pairs={{0,496},{16,0},{32,16},{48,32},{64,48},{80,64},{96,80},{112,96},{1... | collective-permute-start | bytes 466952 | tf_op jit(solution)/shard_map/ppermute | solution.py:25
  67.8 8.8 %collective-permute-start.4 = (bf16[7,32,128]{2,1,0:T(8,128)(2,1)S(1)}, bf16[7,32,128]{2,1,0:T(8,128)(2,1)S(1)}, u32[]{:S(2)}, u32[]{:S(2)}) collective-permute-start(bf16[7,32,128]{2,1,0:T(8,128)(2,1)S(1)} %get-tuple-element.27), channel_id=1, source_target_pairs={{0,16},{16,32},{32,48},{48,64},{64,80},{80,96},{96,112},{112,128},... | collective-permute-start | bytes 172040 | tf_op jit(solution)/shard_map/ppermute | solution.py:25
  77.4 11.6 %all-to-all-start.2 = ((f32[8,48,128]{2,1,0:T(8,128)}), f32[8,48,128]{2,1,0:T(8,128)S(1)}, u32[]{:S(2)}, u32[]{:S(2)}) async-start(f32[8,48,128]{2,1,0:T(8,128)} %shard_map.96), calls=%async_computation.2 | async-start | bytes 393216 | tf_op jit(solution)/shard_map/all_to_all | solution.py:326
  89.6 13.6 %all-to-all-start.3 = ((f32[8,48,128]{2,1,0:T(8,128)}), f32[8,48,128]{2,1,0:T(8,128)S(1)}, u32[]{:S(2)}, u32[]{:S(2)}) async-start(f32[8,48,128]{2,1,0:T(8,128)} %shard_map.98), calls=%async_computation.3 | async-start | bytes 393216 | tf_op jit(solution)/shard_map/all_to_all | solution.py:326

commit v4 on v3

--- a/solution.py
+++ b/solution.py
@@ -25,9 +25,8 @@
     return lax.ppermute(x, axis, [(i, (i + by) % devices) for i in range(devices)])
 
 
-def call(body, outs, args, scratch=(), after=()):
+def call(body, outs, args, scratch=(), after=(), flops=10**8):
     moved = 2 * 10**6
-    flops = 10**8
     return pl.pallas_call(
         body,
         out_shape=[jax.ShapeDtypeStruct(s, d) for s, d in outs],
@@ -218,7 +217,7 @@
 
 
 def outputs_kernel(
-    f_ref, g_ref, h2, d2, xlo, xhi, slope, wb, wu, wv, after,
+    f_ref, g_ref, h2, d2, xlo, xhi, slope, wb, wu, wv,
     mapped_out, grad_out, d2_three, mcol, d1, ucol, slabs,
 ):
     def d(i, j):
@@ -284,7 +283,7 @@
 
 
 def unpack_kernel(total, down_out, mid_out, up_out):
-    total = total[...].reshape(ROWS, LANES)
+    total = total[...].astype(F32).reshape(ROWS, LANES)
     flipped = jnp.concatenate([total[0:224], jnp.zeros((32, LANES), F32)], 0).T
     for tap in range(27):
         k, m = tap // 7, tap % 7
@@ -327,11 +326,12 @@
 
 
 def sum_kernel(got, *refs):
-    refs[-1][...] = jnp.broadcast_to(jnp.sum(got[...], 0, keepdims=True), refs[-1].shape)
-
-
-def sum_spread(got, axes, after=()):
-    return call(sum_kernel, [((lax.axis_size(axes),) + got.shape[1:], F32)], [got], after=after)[0]
+    total = jnp.sum(got[...], 0, keepdims=True).astype(refs[-1].dtype)
+    refs[-1][...] = jnp.broadcast_to(total, refs[-1].shape)
+
+
+def sum_spread(got, axes, after=(), dtype=F32):
+    return call(sum_kernel, [((lax.axis_size(axes),) + got.shape[1:], dtype)], [got], after=after)[0]
 
 
 def local(fields, cotangent, w_down, w_mid, w_up):
@@ -370,18 +370,18 @@
     last, first = call(x_rows_kernel, [((7, 32, LANES), BF), ((19, 32, LANES), BF)], [h2, d2], after=[got])
     xlo, xhi = shift(last, GX, 1), shift(first, GX, -1)
     got = exchange(sum_spread(got, Z), Z)
-    got = exchange(sum_spread(got, Y, after=[xlo, xhi]), Y)
+    got = exchange(sum_spread(got, Y), Y)
     mapped, grad_fields = call(
         outputs_kernel,
         [((256, 256), BF)] * 2,
         [f, g, h2, d2, xlo, xhi, slope, wb, wu, wv],
         [((5, 7, 96, LANES), BF), ((864, 15 * LANES), BF), ((32, 15 * LANES), BF), ((256, 8 * LANES), BF), ((512, LANES), BF)],
-        after=[got],
+        flops=10**10,
     )
     grad_down, grad_mid, grad_up = call(
         unpack_kernel,
         [((27, 8, 32), F32), ((27, 32, 32), F32), ((27, 8, 32), F32)],
-        [exchange(sum_spread(got, XC), XC)],
+        [exchange(sum_spread(got, XC, dtype=BF), XC)],
     )
     return (
         mapped.reshape(fields.shape),

time: 105 us -> 103 us (0.981)
  waiting for transfers between devices: 32.8 us -> 22.7 us
  starting transfers between devices: 53.4 us -> 61.3 us
    ppermute x6, waiting for transfers between devices: 17.5 us -> 6.17 us  [shift(): lax.ppermute(x, axis, [(i, (i + by) % devices) for i in range(devices)])]
    all_to_all x4, starting transfers between devices: 21.9 us -> 31.8 us  [exchange(): return lax.all_to_all(part, axes, 0, 0, tiled=True)]
    ppermute x6, starting transfers between devices: 31.4 us -> 29.6 us  [shift(): lax.ppermute(x, axis, [(i, (i + by) % devices) for i in range(devices)])]
    all_to_all x4, waiting for transfers between devices: 15.3 us -> 16.5 us  [exchange(): return lax.all_to_all(part, axes, 0, 0, tiled=True)]
  transfers between devices with their start and end apart: 10 -> 10, of which waited for: 7 -> 6; matrix products, arithmetic and copies ran while one was open for 2% -> 2% of each run, Pallas kernels for 3% -> 3%
where the time goes in v4:
time: 103 us; the launch traced here: 102 us
  starting transfers between devices  61.3 us (60%)
  waiting for transfers between devices  22.7 us (22%)
  Pallas kernels  10.9 us (11%)
  local copies, waits for them, and re-layouts  5.88 us (6%)
    all_to_all x4, starting transfers between devices, exchange(): return lax.all_to_all(part, axes, 0, 0, tiled=True)  31.8 us
    ppermute x6, starting transfers between devices, shift(): lax.ppermute(x, axis, [(i, (i + by) % devices) for i in range(devices)])  29.6 us
    all_to_all x4, waiting for transfers between devices, exchange(): return lax.all_to_all(part, axes, 0, 0, tiled=True)  16.5 us
    pallas_call x8, Pallas kernels, call(): pl.pallas_call(body, out_shape=[jax.ShapeDtypeStruct(s, d) for s, d in ou...  10.9 us
    ppermute x6, waiting for transfers between devices, shift(): lax.ppermute(x, axis, [(i, (i + by) % devices) for i in range(devices)])  6.17 us
    unnamed x41, local copies, waits for them, and re-layouts  3.24 us
  transfers between devices with their start and end apart: 10, of which 6 were waited for; matrix products, arithmetic and copies ran while one was open for 2% of the time, Pallas kernels for 3%

profile of v4, /device:TPU:1, one launch (start us, length us, event | category | flops | bytes accessed | tf_op | source)
XLA Modules:
  0.0 102.2 jit_solution(1037972241182799697)
XLA Ops:
  0.6 0.9 copy-done.2
  1.5 0.9 copy-done.3
  2.4 0.7 shard_map.92
  3.2 8.9 %collective-permute-start.1 = (bf16[4,10,16,128]{3,2,1,0:T(8,128)(2,1)S(1)}, bf16[4,10,16,128]{3,2,1,0:T(8,128)(2,1)S(1)}, u32[]{:S(2)}, u32[]{:S(2)}) collective-permute-start(bf16[4,10,16,128]{3,2,1,0:T(8,128)(2,1)S(1)} %get-tuple-element.23), channel_id=1, source_target_pairs={{0,15},{1,0},{2,1},{3,2},{4,3},{5,4},{6,5},{7,6},{8,7},{9,8},{10,9... | collective-permute-start | bytes 491528 | tf_op jit(solution)/shard_map/ppermute | solution.py:25
  12.1 2.0 %collective-permute-start = (bf16[4,8,16,128]{3,2,1,0:T(8,128)(2,1)S(1)}, bf16[4,8,16,128]{3,2,1,0:T(8,128)(2,1)S(1)}, u32[]{:S(2)}, u32[]{:S(2)}) collective-permute-start(bf16[4,8,16,128]{3,2,1,0:T(8,128)(2,1)S(1)} %get-tuple-element.22), channel_id=1, source_target_pairs={{0,1},{1,2},{2,3},{3,4},{4,5},{5,6},{6,7},{7,8},{8,9},{9,10},{10,1... | collective-permute-start | bytes 393224 | tf_op jit(solution)/shard_map/ppermute | solution.py:25
  14.3 0.1 copy.54.wb
  14.8 0.6 copy-done.7
  15.5 3.2 %collective-permute-done.ylo = bf16[4,8,16,128]{3,2,1,0:T(8,128)(2,1)S(1)} collective-permute-done((bf16[4,8,16,128]{3,2,1,0:T(8,128)(2,1)S(1)}, bf16[4,8,16,128]{3,2,1,0:T(8,128)(2,1)S(1)}, u32[]{:S(2)}, u32[]{:S(2)}) %collective-permute-start) | collective-permute-done | bytes 131104 | tf_op jit(solution)/shard_map/ppermute | solution.py:25
  18.7 0.7 copy-done
  19.4 0.9 slice-done
  20.4 4.6 %collective-permute-start.2 = (bf16[72,16,128]{2,1,0:T(8,128)(2,1)S(1)}, bf16[72,16,128]{2,1,0:T(8,128)(2,1)S(1)}, u32[]{:S(2)}, u32[]{:S(2)}) collective-permute-start(bf16[72,16,128]{2,1,0:T(8,128)(2,1)S(1)} %pad_maximum_fusion.1), channel_id=1, source_target_pairs={{0,16},{16,32},{32,48},{48,64},{64,80},{80,96},{96,112},{112,128},... | collective-permute-start | bytes 884744 | tf_op jit(solution)/shard_map/ppermute | solution.py:25
  25.2 7.9 %collective-permute-start.3 = (bf16[38,16,128]{2,1,0:T(8,128)(2,1)S(1)}, bf16[38,16,128]{2,1,0:T(8,128)(2,1)S(1)}, u32[]{:S(2)}, u32[]{:S(2)}) collective-permute-start(bf16[38,16,128]{2,1,0:T(8,128)(2,1)S(1)} %bitcast.249), channel_id=1, source_target_pairs={{0,496},{16,0},{32,16},{48,32},{64,48},{80,64},{96,80},{112,96},{1... | collective-permute-start | bytes 466952 | tf_op jit(solution)/shard_map/ppermute | solution.py:25
  33.3 0.2 copy.41
  33.4 0.2 reshape.54.wm
  33.9 3.0 %collective-permute-done.3.xhi = bf16[38,16,128]{2,1,0:T(8,128)(2,1)S(1)} collective-permute-done((bf16[38,16,128]{2,1,0:T(8,128)(2,1)S(1)}, bf16[38,16,128]{2,1,0:T(8,128)(2,1)S(1)}, u32[]{:S(2)}, u32[]{:S(2)}) %collective-permute-start.3) | collective-permute-done | bytes 155680 | tf_op jit(solution)/shard_map/ppermute | solution.py:25
  36.8 4.3 %shard_map.93 = (f32[8,48,128]{2,1,0:T(8,128)}, f32[15,32,128]{2,1,0:T(8,128)S(1)}, bf16[32,1792]{1,0:T(8,128)(2,1)S(1)}, bf16[32,1792]{1,0:T(8,128)(2,1)S(1)}) custom-call(bf16[4,8,16,128]{3,2,1,0:T(8,128)(2,1)S(1)} %get-tuple-element.20.f_ref, bf16[4,8,16,128]{3,2,1,0:T(8,128)(2,1)S(1)} %get-tuple-element.21.g_ref, bf16[4,8,16,128]{3,2,1,0:T(8,128)(2,1)S(1)} %copy-done.1, ...), custom_call_target="tpu_custom_call" | custom-call | flops 100000000 | bytes 2000000 | tf_op jit(solution)/shard_map/pallas_call | solution.py:30
  41.1 11.0 %all-to-all-start = ((f32[8,48,128]{2,1,0:T(8,128)}), f32[8,48,128]{2,1,0:T(8,128)S(1)}, u32[]{:S(2)}, u32[]{:S(2)}) async-start(f32[8,48,128]{2,1,0:T(8,128)} %get-tuple-element.26), calls=%async_computation | async-start | bytes 393216 | tf_op jit(solution)/shard_map/all_to_all | solution.py:325
  52.1 5.9 %all-to-all-done.after.got = f32[8,48,128]{2,1,0:T(8,128)S(1)} async-done(((f32[8,48,128]{2,1,0:T(8,128)}), f32[8,48,128]{2,1,0:T(8,128)S(1)}, u32[]{:S(2)}, u32[]{:S(2)}) %all-to-all-start) | async-done | bytes 196640 | tf_op jit(solution)/shard_map/all_to_all | solution.py:325
  58.0 0.7 shard_map.96
  58.7 6.7 %all-to-all-start.1 = ((f32[8,48,128]{2,1,0:T(8,128)}), f32[8,48,128]{2,1,0:T(8,128)S(1)}, u32[]{:S(2)}, u32[]{:S(2)}) async-start(f32[8,48,128]{2,1,0:T(8,128)} %shard_map.96), calls=%async_computation.1 | async-start | bytes 393216 | tf_op jit(solution)/shard_map/all_to_all | solution.py:325
  66.0 8.0 %all-to-all-done.1.got = f32[8,48,128]{2,1,0:T(8,128)S(1)} async-done(((f32[8,48,128]{2,1,0:T(8,128)}), f32[8,48,128]{2,1,0:T(8,128)S(1)}, u32[]{:S(2)}, u32[]{:S(2)}) %all-to-all-start.1) | async-done | bytes 196640 | tf_op jit(solution)/shard_map/all_to_all | solution.py:325
  74.0 0.7 shard_map.97
  74.7 4.9 %all-to-all-start.2 = ((f32[8,48,128]{2,1,0:T(8,128)}), f32[8,48,128]{2,1,0:T(8,128)S(1)}, u32[]{:S(2)}, u32[]{:S(2)}) async-start(f32[8,48,128]{2,1,0:T(8,128)} %shard_map.97), calls=%async_computation.2 | async-start | bytes 393216 | tf_op jit(solution)/shard_map/all_to_all | solution.py:325
  79.6 4.3 %collective-permute-start.5 = (bf16[19,32,128]{2,1,0:T(8,128)(2,1)S(1)}, bf16[19,32,128]{2,1,0:T(8,128)(2,1)S(1)}, u32[]{:S(2)}, u32[]{:S(2)}) collective-permute-start(bf16[19,32,128]{2,1,0:T(8,128)(2,1)S(1)} %get-tuple-element.28), channel_id=1, source_target_pairs={{0,496},{16,0},{32,16},{48,32},{64,48},{80,64},{96,80},{112,96},{1... | collective-permute-start | bytes 466952 | tf_op jit(solution)/shard_map/ppermute | solution.py:25
  83.9 0.1 concatenate.77
  84.0 1.9 %collective-permute-start.4 = (bf16[7,32,128]{2,1,0:T(8,128)(2,1)S(1)}, bf16[7,32,128]{2,1,0:T(8,128)(2,1)S(1)}, u32[]{:S(2)}, u32[]{:S(2)}) collective-permute-start(bf16[7,32,128]{2,1,0:T(8,128)(2,1)S(1)} %get-tuple-element.27), channel_id=1, source_target_pairs={{0,16},{16,32},{32,48},{48,64},{64,80},{80,96},{96,112},{112,128},... | collective-permute-start | bytes 172040 | tf_op jit(solution)/shard_map/ppermute | solution.py:25
  85.9 0.4 all-to-all-done.2.got
  86.4 0.7 shard_map.98
  87.0 9.2 %all-to-all-start.3 = ((bf16[8,48,128]{2,1,0:T(8,128)(2,1)}), bf16[8,48,128]{2,1,0:T(8,128)(2,1)S(1)}, u32[]{:S(2)}, u32[]{:S(2)}) async-start(bf16[8,48,128]{2,1,0:T(8,128)(2,1)} %shard_map.98), calls=%async_computation.3 | async-start | bytes 196608 | tf_op jit(solution)/shard_map/all_to_all | solution.py:325
  96.2 2.8 %shard_map.95 = (bf16[256,256]{1,0:T(8,128)(2,1)}, bf16[256,256]{1,0:T(8,128)(2,1)}) custom-call(bf16[4,8,16,128]{3,2,1,0:T(8,128)(2,1)S(1)} %get-tuple-element.20.f_ref, bf16[4,8,16,128]{3,2,1,0:T(8,128)(2,1)S(1)} %get-tuple-element.21.g_ref, bf16[32,1792]{1,0:T(8,128)(2,1)S(1)} %get-tuple-element.24.h2, bf16[32,1792]{1,0:T(8,128)(2,1)S(1)} %get-tuple-element.25.d2, ...), custom_call_target="tpu_custom_call" | custom-call | flops 10000000000 | bytes 2000000 | tf_op jit(solution)/shard_map/pallas_call | solution.py:30
  99.0 2.2 %all-to-all-done.3.total = bf16[8,48,128]{2,1,0:T(8,128)(2,1)S(1)} async-done(((bf16[8,48,128]{2,1,0:T(8,128)(2,1)}), bf16[8,48,128]{2,1,0:T(8,128)(2,1)S(1)}, u32[]{:S(2)}, u32[]{:S(2)}) %all-to-all-start.3) | async-done | bytes 98336 | tf_op jit(solution)/shard_map/all_to_all | solution.py:325
  101.2 1.0 shard_map.99
  (86 shorter events, 1.9 us)
Async XLA Ops:
  0.6 0.9 copy-start.2
  1.5 0.9 copy-start.3
  2.4 11.6 %copy-start.5 = (bf16[3,3,3,8,32]{4,3,2,1,0:T(8,128)(2,1)S(1)}, bf16[3,3,3,8,32]{4,3,2,1,0:T(8,128)(2,1)}, u32[]{:S(2)}) copy-start(bf16[3,3,3,8,32]{4,3,2,1,0:T(8,128)(2,1)} %param.9) | copy-start | bytes 41476
  2.4 11.7 %copy-start.6 = (bf16[3,3,3,32,8]{3,4,2,1,0:T(8,128)(2,1)S(1)}, bf16[3,3,3,32,8]{3,4,2,1,0:T(8,128)(2,1)}, u32[]{:S(2)}) copy-start(bf16[3,3,3,32,8]{3,4,2,1,0:T(8,128)(2,1)} %param.7) | copy-start | bytes 41476
  3.2 11.2 %copy-start.4 = (bf16[3,3,3,32,32]{4,3,2,1,0:T(8,128)(2,1)S(1)}, bf16[3,3,3,32,32]{4,3,2,1,0:T(8,128)(2,1)}, u32[]{:S(2)}) copy-start(bf16[3,3,3,32,32]{4,3,2,1,0:T(8,128)(2,1)} %param.8) | copy-start | bytes 165892
  3.2 16.2 %collective-permute-start.1 = (bf16[4,10,16,128]{3,2,1,0:T(8,128)(2,1)S(1)}, bf16[4,10,16,128]{3,2,1,0:T(8,128)(2,1)S(1)}, u32[]{:S(2)}, u32[]{:S(2)}) collective-permute-start(bf16[4,10,16,128]{3,2,1,0:T(8,128)(2,1)S(1)} %get-tuple-element.23), channel_id=1, source_target_pairs={{0,15},{1,0},{2,1},{3,2},{4,3},{5,4},{6,5},{7,6},{8,7},{9,8},{10,9... | collective-permute-start | bytes 491528 | tf_op jit(solution)/shard_map/ppermute | solution.py:25
  12.1 6.6 %collective-permute-start = (bf16[4,8,16,128]{3,2,1,0:T(8,128)(2,1)S(1)}, bf16[4,8,16,128]{3,2,1,0:T(8,128)(2,1)S(1)}, u32[]{:S(2)}, u32[]{:S(2)}) collective-permute-start(bf16[4,8,16,128]{3,2,1,0:T(8,128)(2,1)S(1)} %get-tuple-element.22), channel_id=1, source_target_pairs={{0,1},{1,2},{2,3},{3,4},{4,5},{5,6},{6,7},{7,8},{8,9},{9,10},{10,1... | collective-permute-start | bytes 393224 | tf_op jit(solution)/shard_map/ppermute | solution.py:25
  14.7 0.7 copy-start.7
  18.7 0.7 copy-start
  19.4 0.9 slice-start
  20.4 16.4 %collective-permute-start.2 = (bf16[72,16,128]{2,1,0:T(8,128)(2,1)S(1)}, bf16[72,16,128]{2,1,0:T(8,128)(2,1)S(1)}, u32[]{:S(2)}, u32[]{:S(2)}) collective-permute-start(bf16[72,16,128]{2,1,0:T(8,128)(2,1)S(1)} %pad_maximum_fusion.1), channel_id=1, source_target_pairs={{0,16},{16,32},{32,48},{48,64},{64,80},{80,96},{96,112},{112,128},... | collective-permute-start | bytes 884744 | tf_op jit(solution)/shard_map/ppermute | solution.py:25
  25.2 11.7 %collective-permute-start.3 = (bf16[38,16,128]{2,1,0:T(8,128)(2,1)S(1)}, bf16[38,16,128]{2,1,0:T(8,128)(2,1)S(1)}, u32[]{:S(2)}, u32[]{:S(2)}) collective-permute-start(bf16[38,16,128]{2,1,0:T(8,128)(2,1)S(1)} %bitcast.249), channel_id=1, source_target_pairs={{0,496},{16,0},{32,16},{48,32},{64,48},{80,64},{96,80},{112,96},{1... | collective-permute-start | bytes 466952 | tf_op jit(solution)/shard_map/ppermute | solution.py:25
  33.8 3.0 %copy-start.1 = (bf16[4,8,16,128]{3,2,1,0:T(8,128)(2,1)S(1)}, bf16[4,8,16,128]{3,2,1,0:T(8,128)(2,1)}, u32[]{:S(2)}) copy-start(bf16[4,8,16,128]{3,2,1,0:T(8,128)(2,1)} %copy-done) | copy-start | bytes 393220
  41.1 16.9 %all-to-all-start = ((f32[8,48,128]{2,1,0:T(8,128)}), f32[8,48,128]{2,1,0:T(8,128)S(1)}, u32[]{:S(2)}, u32[]{:S(2)}) async-start(f32[8,48,128]{2,1,0:T(8,128)} %get-tuple-element.26), calls=%async_computation | async-start | bytes 393216 | tf_op jit(solution)/shard_map/all_to_all | solution.py:325
  58.7 15.2 %all-to-all-start.1 = ((f32[8,48,128]{2,1,0:T(8,128)}), f32[8,48,128]{2,1,0:T(8,128)S(1)}, u32[]{:S(2)}, u32[]{:S(2)}) async-start(f32[8,48,128]{2,1,0:T(8,128)} %shard_map.96), calls=%async_computation.1 | async-start | bytes 393216 | tf_op jit(solution)/shard_map/all_to_all | solution.py:325
  74.7 11.7 %all-to-all-start.2 = ((f32[8,48,128]{2,1,0:T(8,128)}), f32[8,48,128]{2,1,0:T(8,128)S(1)}, u32[]{:S(2)}, u32[]{:S(2)}) async-start(f32[8,48,128]{2,1,0:T(8,128)} %shard_map.97), calls=%async_computation.2 | async-start | bytes 393216 | tf_op jit(solution)/shard_map/all_to_all | solution.py:325
  79.6 16.6 %collective-permute-start.5 = (bf16[19,32,128]{2,1,0:T(8,128)(2,1)S(1)}, bf16[19,32,128]{2,1,0:T(8,128)(2,1)S(1)}, u32[]{:S(2)}, u32[]{:S(2)}) collective-permute-start(bf16[19,32,128]{2,1,0:T(8,128)(2,1)S(1)} %get-tuple-element.28), channel_id=1, source_target_pairs={{0,496},{16,0},{32,16},{48,32},{64,48},{80,64},{96,80},{112,96},{1... | collective-permute-start | bytes 466952 | tf_op jit(solution)/shard_map/ppermute | solution.py:25
  84.0 12.2 %collective-permute-start.4 = (bf16[7,32,128]{2,1,0:T(8,128)(2,1)S(1)}, bf16[7,32,128]{2,1,0:T(8,128)(2,1)S(1)}, u32[]{:S(2)}, u32[]{:S(2)}) collective-permute-start(bf16[7,32,128]{2,1,0:T(8,128)(2,1)S(1)} %get-tuple-element.27), channel_id=1, source_target_pairs={{0,16},{16,32},{32,48},{48,64},{64,80},{80,96},{96,112},{112,128},... | collective-permute-start | bytes 172040 | tf_op jit(solution)/shard_map/ppermute | solution.py:25
  87.0 14.2 %all-to-all-start.3 = ((bf16[8,48,128]{2,1,0:T(8,128)(2,1)}), bf16[8,48,128]{2,1,0:T(8,128)(2,1)S(1)}, u32[]{:S(2)}, u32[]{:S(2)}) async-start(bf16[8,48,128]{2,1,0:T(8,128)(2,1)} %shard_map.98), calls=%async_computation.3 | async-start | bytes 196608 | tf_op jit(solution)/shard_map/all_to_all | solution.py:325

commit v5 on v2

--- a/solution.py
+++ b/solution.py
@@ -16,6 +16,7 @@
 ROWS = 384
 GX = ("z", "yl")
 GY = ("x", "yh", "core")
+XC, Y, Z = ("x", "core"), ("yl", "yh"), ("z",)
 
 
 def shift(x, axis, by):
@@ -23,17 +24,17 @@
     return lax.ppermute(x, axis, [(i, (i + by) % devices) for i in range(devices)])
 
 
-def call(body, outs, args, scratch=(), flops=10**8, space=pltpu.VMEM):
+def call(body, outs, args, scratch=(), after=(), flops=10**8):
     moved = 2 * 10**6
     return pl.pallas_call(
         body,
         out_shape=[jax.ShapeDtypeStruct(s, d) for s, d in outs],
-        in_specs=[pl.BlockSpec(memory_space=space)] * len(args),
+        in_specs=[pl.BlockSpec(memory_space=pltpu.VMEM)] * len(args) + [pl.BlockSpec(memory_space=pl.ANY)] * len(after),
         out_specs=[pl.BlockSpec(memory_space=pltpu.VMEM)] * len(outs),
-        scratch_shapes=[pltpu.VMEM(*s) if isinstance(s, tuple) else s for s in scratch],
+        scratch_shapes=[pltpu.VMEM(*s) for s in scratch],
         compiler_params=pltpu.CompilerParams(vmem_limit_bytes=32 * 2**20),
         cost_estimate=pl.CostEstimate(flops=flops, bytes_accessed=moved, transcendentals=0),
-    )(*args)
+    )(*args, *after)
 
 
 def dot(a, b):
@@ -63,15 +64,11 @@
     return (s == source).astype(F32).astype(BF)
 
 
-def to_slabs_kernel(f_any, g_any, f_out, g_out, up_out, down_out, raw, sems):
-    copies = [pltpu.make_async_copy(ref, raw.at[k], sems.at[k]) for k, ref in enumerate((f_any, g_any))]
-    for copy in copies:
-        copy.start()
+def to_slabs_kernel(f_ref, g_ref, f_out, g_out, up_out, down_out):
     halves = split_z()
     order = slab_order(0)
-    for k, out in enumerate((f_out, g_out)):
-        copies[k].wait()
-        z = dot(raw[k], halves).astype(BF)
+    for ref, out in ((f_ref, f_out), (g_ref, g_out)):
+        z = dot(ref[...], halves).astype(BF)
         z = jnp.concatenate([z[:, :LANES], z[:, LANES:]], 0)
         out[...] = dot(order, z).astype(BF).reshape(4, 8, 16, LANES)
     up_out[:, 0:3] = f_out[:, 5:8]
@@ -84,8 +81,9 @@
 
 
 def act_and_slope(v):
-    s = jax.nn.sigmoid(v)
-    return 0.2 * v + 0.8 * v * s, 0.2 + 0.8 * (s + v * s * (1.0 - s))
+    t = jnp.tanh(0.5 * v)
+    gain = 0.6 + 0.4 * t
+    return v * gain, gain + 0.2 * v * (1.0 - t * t)
 
 
 def three(v):
@@ -115,7 +113,7 @@
 
 def forward_kernel(
     f_ref, g_ref, ylo, yhi, xlo, xhi, wd, wm, wg, wb,
-    grads_out, slope_out, h2_out, d2_out, up_out, down_out,
+    grads_out, slope_out, h2_out, d2_out,
     fpair, gpair, h1_three, d2_three, slope, xcol, mcol, gcol, zcol,
 ):
     def f(x, y):
@@ -172,12 +170,6 @@
         v, s = act_and_slope(dot(wm[...], mcol[:, lanes]))
         h2_out[:, lanes] = v.astype(BF)
         d2_out[:, lanes] = (dot(wg[...], gcol[:, lanes]) * s).astype(BF)
-    for i in range(2):
-        at = 4 * i * LANES
-        up_out[i] = d2_out[:, at + 3 * LANES : at + 4 * LANES]
-        down_out[i] = d2_out[:, at : at + LANES]
-        down_out[2 + i] = d2_out[:, at + LANES : at + 2 * LANES]
-        down_out[4 + i] = h2_out[:, at : at + LANES]
     for n, (i, j) in enumerate(LOCAL):
         d2_three[i, j] = three(d2_out[:, n * LANES : (n + 1) * LANES].astype(F32))
 
@@ -209,6 +201,30 @@
     grads_out[...] = rows.reshape(grads_out.shape)
 
 
+def y_rows_kernel(h2, d2, after, up_out, down_out):
+    for i in range(2):
+        at = 4 * i * LANES
+        up_out[i] = d2[:, at + 3 * LANES : at + 4 * LANES]
+        down_out[i] = d2[:, at : at + LANES]
+        down_out[2 + i] = d2[:, at + LANES : at + 2 * LANES]
+        down_out[4 + i] = h2[:, at : at + LANES]
+
+
+def x_rows_kernel(h2, d2, ylo, yhi, up_out, down_out):
+    for i in range(2):
+        down_out[7 * i] = ylo[i]
+        for j in range(4):
+            at = (4 * i + j) * LANES
+            down_out[7 * i + 1 + j] = d2[:, at : at + LANES]
+        down_out[7 * i + 5] = yhi[i]
+        down_out[7 * i + 6] = yhi[2 + i]
+    for j in range(4):
+        down_out[14 + j] = h2[:, j * LANES : (j + 1) * LANES]
+    down_out[18] = yhi[4]
+    for j in range(7):
+        up_out[j] = down_out[7 + j]
+
+
 def outputs_kernel(
     f_ref, g_ref, h2, d2, ylo, yhi, xlo, xhi, slope, wb, wu, wv,
     mapped_out, grad_out, d2_three, mcol, d1, ucol, slabs,
@@ -284,7 +300,7 @@
 
 
 def unpack_kernel(total, down_out, mid_out, up_out):
-    total = total[...].reshape(ROWS, LANES)
+    total = total[...].astype(F32).reshape(ROWS, LANES)
     flipped = jnp.concatenate([total[0:224], jnp.zeros((32, LANES), F32)], 0).T
     for tap in range(27):
         k, m = tap // 7, tap % 7
@@ -322,14 +338,17 @@
     return jnp.concatenate(rows, 0)
 
 
-def all_sum(part):
-    def spread(x, axes):
-        return jnp.broadcast_to(x[None], (lax.axis_size(axes),) + x.shape)
-
-    part = lax.all_to_all(part, ("x", "core"), 0, 0, tiled=True).sum(0)
-    for axes in (("z",), ("yl", "yh")):
-        part = lax.all_to_all(spread(part, axes), axes, 0, 0, tiled=True).sum(0)
-    return lax.all_to_all(spread(part, ("x", "core")), ("x", "core"), 0, 0, tiled=True)
+def exchange(part, axes):
+    return lax.all_to_all(part, axes, 0, 0, tiled=True)
+
+
+def sum_kernel(got, out):
+    total = jnp.sum(got[...], 0, keepdims=True).astype(out.dtype)
+    out[...] = jnp.broadcast_to(total, out.shape)
+
+
+def sum_spread(got, axes, dtype=F32):
+    return call(sum_kernel, [((lax.axis_size(axes),) + got.shape[1:], dtype)], [got])[0]
 
 
 def local(fields, cotangent, w_down, w_mid, w_up):
@@ -347,8 +366,6 @@
         to_slabs_kernel,
         [((4, 8, 16, LANES), BF)] * 2 + [((4, 4, 16, LANES), BF), ((4, 2, 16, LANES), BF)],
         [fields.reshape(256, 256), cotangent.reshape(256, 256)],
-        [((2, 256, 256), BF), pltpu.SemaphoreType.DMA((2,))],
-        space=pl.ANY,
     )
     ylo, yhi = shift(up, GY, 1), shift(down, GY, -1)
     f_ext = jnp.concatenate([ylo[:, :3], f, yhi], 1)
@@ -356,35 +373,35 @@
     xlo = shift(last, GX, 1)
     xhi = shift(f_ext[:2].reshape(26, 16, LANES), GX, -1)
 
-    parts = lax.axis_size(("x", "core"))
-    grads, slope, h2, d2, up, down = call(
+    parts = lax.axis_size(XC)
+    grads, slope, h2, d2 = call(
         forward_kernel,
-        [((parts, ROWS // parts, LANES), F32), ((15, 32, LANES), F32), ((32, 8 * LANES), BF), ((32, 8 * LANES), BF),
-         ((2, 32, LANES), BF), ((6, 32, LANES), BF)],
+        [((parts, ROWS // parts, LANES), F32), ((15, 32, LANES), F32), ((32, 8 * LANES), BF), ((32, 8 * LANES), BF)],
         [f, g, ylo, yhi, xlo, xhi, wd, wm, wg, wb_rows],
         [((9, 7, 16, LANES), BF), ((5, 5, 16, LANES), BF), ((4, 6, 96, LANES), BF), ((2, 4, 96, LANES), BF),
          ((32, 4 * ROW), F32), ((240, 4 * ROW), BF), ((864, 8 * LANES), BF), ((240, 8 * LANES), BF), ((576, ROW), BF)],
     )
+
+    got = exchange(grads, XC)
+    up, down = call(y_rows_kernel, [((2, 32, LANES), BF), ((6, 32, LANES), BF)], [h2, d2], after=[got])
     ylo, yhi = shift(up, GY, 1), shift(down, GY, -1)
-    cells = jnp.transpose(d2.reshape(32, 8, LANES), (1, 0, 2))
-    last = jnp.concatenate([ylo[1:2], cells[4:8], yhi[1:2], yhi[3:4]], 0)
-    first = jnp.concatenate(
-        [ylo[0:1], cells[0:4], yhi[0:1], yhi[2:3], last]
-        + [h2[None, :, j * LANES : (j + 1) * LANES] for j in range(4)] + [yhi[4:5]], 0
-    )
-    xlo = shift(last, GX, 1)
-    xhi = shift(first, GX, -1)
-
+    got = exchange(sum_spread(got, Z), Z)
+    last, first = call(
+        x_rows_kernel, [((7, 32, LANES), BF), ((19, 32, LANES), BF)], [h2, d2, ylo, yhi], flops=10**10
+    )
+    xlo, xhi = shift(last, GX, 1), shift(first, GX, -1)
+    got = exchange(sum_spread(got, Y), Y)
     mapped, grad_fields = call(
         outputs_kernel,
         [((256, 256), BF)] * 2,
         [f, g, h2, d2, ylo, yhi, xlo, xhi, slope, wb, wu, wv],
         [((5, 7, 96, LANES), BF), ((864, 15 * LANES), BF), ((32, 15 * LANES), BF), ((256, 8 * LANES), BF), ((512, LANES), BF)],
+        flops=10**10,
     )
     grad_down, grad_mid, grad_up = call(
         unpack_kernel,
         [((27, 8, 32), F32), ((27, 32, 32), F32), ((27, 8, 32), F32)],
-        [all_sum(grads)],
+        [exchange(sum_spread(got, XC, dtype=BF), XC)],
     )
     return (
         mapped.reshape(fields.shape),

time: 113 us -> 95.2 us (0.84)
  waiting for transfers between devices: 29.3 us -> 15.4 us
  starting transfers between devices: 65.8 us -> 63 us
  local copies, waits for them, and re-layouts: 6.56 us -> 4.34 us
    all_to_all x4, waiting for transfers between devices: 16.8 us -> 6.02 us  [exchange(): return lax.all_to_all(part, axes, 0, 0, tiled=True)]
    all_to_all x4, starting transfers between devices: 28.2 us -> 20.3 us  [exchange(): return lax.all_to_all(part, axes, 0, 0, tiled=True)]
    ppermute x8, starting transfers between devices: 37.6 us -> 42.7 us  [shift(): lax.ppermute(x, axis, [(i, (i + by) % devices) for i in range(devices)])]
    ppermute x8, waiting for transfers between devices: 12.5 us -> 9.41 us  [shift(): lax.ppermute(x, axis, [(i, (i + by) % devices) for i in range(devices)])]
    broadcast_in_dim x3 -> x0, local copies, waits for them, and re-layouts: 2.07 us -> none  [spread(): return jnp.broadcast_to(x[None], (lax.axis_size(axes),) + x.shape)]
    pallas_call x4 -> x9, Pallas kernels: 9.22 us -> 10.2 us  [call(): pl.pallas_call(body, out_shape=[jax.ShapeDtypeStruct(s, d) for s, d in ou...]
    unnamed x49 -> x37, local copies, waits for them, and re-layouts: 2.71 us -> 2.58 us
  transfers between devices with their start and end apart: 12 -> 12, of which waited for: 7 -> 6; matrix products, arithmetic and copies ran while one was open for 3% -> 2% of each run, Pallas kernels for 2% -> 4%
where the time goes in v5:
time: 95.2 us; the launch traced here: 94.5 us
  starting transfers between devices  63 us (66%)
  waiting for transfers between devices  15.4 us (16%)
  Pallas kernels  10.2 us (11%)
  local copies, waits for them, and re-layouts  4.34 us (5%)
  between operations  1.06 us (1%)
    ppermute x8, starting transfers between devices, shift(): lax.ppermute(x, axis, [(i, (i + by) % devices) for i in range(devices)])  42.7 us
    all_to_all x4, starting transfers between devices, exchange(): return lax.all_to_all(part, axes, 0, 0, tiled=True)  20.3 us
    pallas_call x9, Pallas kernels, call(): pl.pallas_call(body, out_shape=[jax.ShapeDtypeStruct(s, d) for s, d in ou...  10.2 us
    ppermute x8, waiting for transfers between devices, shift(): lax.ppermute(x, axis, [(i, (i + by) % devices) for i in range(devices)])  9.41 us
    all_to_all x4, waiting for transfers between devices, exchange(): return lax.all_to_all(part, axes, 0, 0, tiled=True)  6.02 us
    unnamed x37, local copies, waits for them, and re-layouts  2.58 us
  transfers between devices with their start and end apart: 12, of which 6 were waited for; matrix products, arithmetic and copies ran while one was open for 2% of the time, Pallas kernels for 4%

profile of v5, /device:TPU:1, one launch (start us, length us, event | category | flops | bytes accessed | tf_op | source)
XLA Modules:
  0.0 94.5 jit_solution(10307381920900150038)
XLA Ops:
  0.6 0.9 copy-done
  1.5 0.9 copy-done.1
  2.4 0.7 shard_map.92
  3.2 9.0 %collective-permute-start = (bf16[4,4,16,128]{3,2,1,0:T(8,128)(2,1)S(1)}, bf16[4,4,16,128]{3,2,1,0:T(8,128)(2,1)S(1)}, u32[]{:S(2)}, u32[]{:S(2)}) collective-permute-start(bf16[4,4,16,128]{3,2,1,0:T(8,128)(2,1)S(1)} %get-tuple-element.24), channel_id=1, source_target_pairs={{0,1},{1,2},{2,3},{3,4},{4,5},{5,6},{6,7},{7,8},{8,9},{9,10},{10,1... | collective-permute-start | bytes 196616 | tf_op jit(solution)/shard_map/ppermute | solution.py:24
  12.1 1.9 %collective-permute-start.1 = (bf16[4,2,16,128]{3,2,1,0:T(8,128)(2,1)S(1)}, bf16[4,2,16,128]{3,2,1,0:T(8,128)(2,1)S(1)}, u32[]{:S(2)}, u32[]{:S(2)}) collective-permute-start(bf16[4,2,16,128]{3,2,1,0:T(8,128)(2,1)S(1)} %get-tuple-element.25), channel_id=1, source_target_pairs={{0,15},{1,0},{2,1},{3,2},{4,3},{5,4},{6,5},{7,6},{8,7},{9,8},{10,9... | collective-permute-start | bytes 98312 | tf_op jit(solution)/shard_map/ppermute | solution.py:24
  14.3 0.1 copy.54.wb
  14.5 0.6 copy-done.5
  15.9 0.2 copy.41
  16.1 0.2 reshape.54.wm
  16.8 4.5 %collective-permute-done.1.yhi = bf16[4,2,16,128]{3,2,1,0:T(8,128)(2,1)S(1)} collective-permute-done((bf16[4,2,16,128]{3,2,1,0:T(8,128)(2,1)S(1)}, bf16[4,2,16,128]{3,2,1,0:T(8,128)(2,1)S(1)}, u32[]{:S(2)}, u32[]{:S(2)}) %collective-permute-start.1) | collective-permute-done | bytes 32800 | tf_op jit(solution)/shard_map/ppermute | solution.py:24
  21.5 2.5 %collective-permute-start.2 = (bf16[48,16,128]{2,1,0:T(8,128)(2,1)S(1)}, bf16[48,16,128]{2,1,0:T(8,128)(2,1)S(1)}, u32[]{:S(2)}, u32[]{:S(2)}) collective-permute-start(bf16[48,16,128]{2,1,0:T(8,128)(2,1)S(1)} %pad_maximum_fusion.1), channel_id=1, source_target_pairs={{0,16},{16,32},{32,48},{48,64},{64,80},{80,96},{96,112},{112,128},... | collective-permute-start | bytes 589832 | tf_op jit(solution)/shard_map/ppermute | solution.py:24
  24.1 10.4 %collective-permute-start.3 = (bf16[26,16,128]{2,1,0:T(8,128)(2,1)S(1)}, bf16[26,16,128]{2,1,0:T(8,128)(2,1)S(1)}, u32[]{:S(2)}, u32[]{:S(2)}) collective-permute-start(bf16[26,16,128]{2,1,0:T(8,128)(2,1)S(1)} %bitcast.247), channel_id=1, source_target_pairs={{0,496},{16,0},{32,16},{48,32},{64,48},{80,64},{96,80},{112,96},{1... | collective-permute-start | bytes 319496 | tf_op jit(solution)/shard_map/ppermute | solution.py:24
  34.5 1.7 %collective-permute-done.3.xhi = bf16[26,16,128]{2,1,0:T(8,128)(2,1)S(1)} collective-permute-done((bf16[26,16,128]{2,1,0:T(8,128)(2,1)S(1)}, bf16[26,16,128]{2,1,0:T(8,128)(2,1)S(1)}, u32[]{:S(2)}, u32[]{:S(2)}) %collective-permute-start.3) | collective-permute-done | bytes 106528 | tf_op jit(solution)/shard_map/ppermute | solution.py:24
  36.2 1.1 %collective-permute-done.2.xlo = bf16[48,16,128]{2,1,0:T(8,128)(2,1)S(1)} collective-permute-done((bf16[48,16,128]{2,1,0:T(8,128)(2,1)S(1)}, bf16[48,16,128]{2,1,0:T(8,128)(2,1)S(1)}, u32[]{:S(2)}, u32[]{:S(2)}) %collective-permute-start.2) | collective-permute-done | bytes 196640 | tf_op jit(solution)/shard_map/ppermute | solution.py:24
  37.3 3.6 %shard_map.93 = (f32[8,48,128]{2,1,0:T(8,128)}, f32[15,32,128]{2,1,0:T(8,128)S(1)}, bf16[32,1024]{1,0:T(8,128)(2,1)S(1)}, bf16[32,1024]{1,0:T(8,128)(2,1)S(1)}) custom-call(bf16[4,8,16,128]{3,2,1,0:T(8,128)(2,1)S(1)} %get-tuple-element.22.f_ref, bf16[4,8,16,128]{3,2,1,0:T(8,128)(2,1)S(1)} %get-tuple-element.23.g_ref, ...), custom_call_target="tpu_custom_call" | custom-call | flops 100000000 | bytes 2000000 | tf_op jit(solution)/shard_map/pallas_call | solution.py:29
  40.9 5.0 %all-to-all-start = ((f32[8,48,128]{2,1,0:T(8,128)}), f32[8,48,128]{2,1,0:T(8,128)S(1)}, u32[]{:S(2)}, u32[]{:S(2)}) async-start(f32[8,48,128]{2,1,0:T(8,128)} %get-tuple-element.28), calls=%async_computation | async-start | bytes 393216 | tf_op jit(solution)/shard_map/all_to_all | solution.py:342
  46.0 5.8 %all-to-all-done.after.got = f32[8,48,128]{2,1,0:T(8,128)S(1)} async-done(((f32[8,48,128]{2,1,0:T(8,128)}), f32[8,48,128]{2,1,0:T(8,128)S(1)}, u32[]{:S(2)}, u32[]{:S(2)}) %all-to-all-start) | async-done | bytes 196640 | tf_op jit(solution)/shard_map/all_to_all | solution.py:342
  51.8 0.7 shard_map.97
  52.5 4.9 %all-to-all-start.1 = ((f32[8,48,128]{2,1,0:T(8,128)}), f32[8,48,128]{2,1,0:T(8,128)S(1)}, u32[]{:S(2)}, u32[]{:S(2)}) async-start(f32[8,48,128]{2,1,0:T(8,128)} %shard_map.97), calls=%async_computation.1 | async-start | bytes 393216 | tf_op jit(solution)/shard_map/all_to_all | solution.py:342
  57.4 3.1 %collective-permute-start.5 = (bf16[6,32,128]{2,1,0:T(8,128)(2,1)S(1)}, bf16[6,32,128]{2,1,0:T(8,128)(2,1)S(1)}, u32[]{:S(2)}, u32[]{:S(2)}) collective-permute-start(bf16[6,32,128]{2,1,0:T(8,128)(2,1)S(1)} %get-tuple-element.30), channel_id=1, source_target_pairs={{0,15},{1,0},{2,1},{3,2},{4,3},{5,4},{6,5},{7,6},{8,7},{9,8},{10,9... | collective-permute-start | bytes 147464 | tf_op jit(solution)/shard_map/ppermute | solution.py:24
  60.6 6.3 %collective-permute-start.4 = (bf16[2,32,128]{2,1,0:T(8,128)(2,1)S(1)}, bf16[2,32,128]{2,1,0:T(8,128)(2,1)S(1)}, u32[]{:S(2)}, u32[]{:S(2)}) collective-permute-start(bf16[2,32,128]{2,1,0:T(8,128)(2,1)S(1)} %get-tuple-element.29), channel_id=1, source_target_pairs={{0,1},{1,2},{2,3},{3,4},{4,5},{5,6},{6,7},{7,8},{8,9},{9,10},{10,1... | collective-permute-start | bytes 49160 | tf_op jit(solution)/shard_map/ppermute | solution.py:24
  66.9 0.1 concatenate.76
  67.0 0.7 shard_map.98
  67.7 6.2 %all-to-all-start.2 = ((f32[8,48,128]{2,1,0:T(8,128)}), f32[8,48,128]{2,1,0:T(8,128)S(1)}, u32[]{:S(2)}, u32[]{:S(2)}) async-start(f32[8,48,128]{2,1,0:T(8,128)} %shard_map.98), calls=%async_computation.2 | async-start | bytes 393216 | tf_op jit(solution)/shard_map/all_to_all | solution.py:342
  74.0 7.5 %collective-permute-start.7 = (bf16[19,32,128]{2,1,0:T(8,128)(2,1)S(1)}, bf16[19,32,128]{2,1,0:T(8,128)(2,1)S(1)}, u32[]{:S(2)}, u32[]{:S(2)}) collective-permute-start(bf16[19,32,128]{2,1,0:T(8,128)(2,1)S(1)} %get-tuple-element.32), channel_id=1, source_target_pairs={{0,496},{16,0},{32,16},{48,32},{64,48},{80,64},{96,80},{112,96},{1... | collective-permute-start | bytes 466952 | tf_op jit(solution)/shard_map/ppermute | solution.py:24
  81.7 1.9 %collective-permute-start.6 = (bf16[7,32,128]{2,1,0:T(8,128)(2,1)S(1)}, bf16[7,32,128]{2,1,0:T(8,128)(2,1)S(1)}, u32[]{:S(2)}, u32[]{:S(2)}) collective-permute-start(bf16[7,32,128]{2,1,0:T(8,128)(2,1)S(1)} %get-tuple-element.31), channel_id=1, source_target_pairs={{0,16},{16,32},{32,48},{48,64},{64,80},{80,96},{96,112},{112,128},... | collective-permute-start | bytes 172040 | tf_op jit(solution)/shard_map/ppermute | solution.py:24
  83.6 0.7 shard_map.99
  84.3 4.2 %all-to-all-start.3 = ((bf16[8,48,128]{2,1,0:T(8,128)(2,1)}), bf16[8,48,128]{2,1,0:T(8,128)(2,1)S(1)}, u32[]{:S(2)}, u32[]{:S(2)}) async-start(bf16[8,48,128]{2,1,0:T(8,128)(2,1)} %shard_map.99), calls=%async_computation.3 | async-start | bytes 196608 | tf_op jit(solution)/shard_map/all_to_all | solution.py:342
  88.4 2.0 %collective-permute-done.6.xlo = bf16[7,32,128]{2,1,0:T(8,128)(2,1)S(1)} collective-permute-done((bf16[7,32,128]{2,1,0:T(8,128)(2,1)S(1)}, bf16[7,32,128]{2,1,0:T(8,128)(2,1)S(1)}, u32[]{:S(2)}, u32[]{:S(2)}) %collective-permute-start.6) | collective-permute-done | bytes 57376 | tf_op jit(solution)/shard_map/ppermute | solution.py:24
  90.5 2.8 %shard_map.96 = (bf16[256,256]{1,0:T(8,128)(2,1)}, bf16[256,256]{1,0:T(8,128)(2,1)}) custom-call(bf16[4,8,16,128]{3,2,1,0:T(8,128)(2,1)S(1)} %get-tuple-element.22.f_ref, bf16[4,8,16,128]{3,2,1,0:T(8,128)(2,1)S(1)} %get-tuple-element.23.g_ref, bf16[32,1024]{1,0:T(8,128)(2,1)S(1)} %get-tuple-element.26.h2, bf16[32,1024]{1,0:T(8,128)(2,1)S(1)} %get-tuple-element.27.d2, ...), custom_call_target="tpu_custom_call" | custom-call | flops 10000000000 | bytes 2000000 | tf_op jit(solution)/shard_map/pallas_call | solution.py:29
  93.3 0.2 all-to-all-done.3.total
  93.4 1.0 %shard_map.100 = (f32[27,8,32]{2,1,0:T(8,128)}, f32[27,32,32]{2,1,0:T(8,128)}, f32[27,8,32]{2,1,0:T(8,128)}) custom-call(bf16[8,48,128]{2,1,0:T(8,128)(2,1)S(1)} %all-to-all-done.3.total), custom_call_target="tpu_custom_call" | custom-call | flops 100000000 | bytes 2000000 | tf_op jit(solution)/shard_map/pallas_call | solution.py:29
  (84 shorter events, 1.8 us)
Async XLA Ops:
  0.6 0.9 copy-start
  1.5 0.9 copy-start.1
  2.4 11.6 %copy-start.3 = (bf16[3,3,3,8,32]{4,3,2,1,0:T(8,128)(2,1)S(1)}, bf16[3,3,3,8,32]{4,3,2,1,0:T(8,128)(2,1)}, u32[]{:S(2)}) copy-start(bf16[3,3,3,8,32]{4,3,2,1,0:T(8,128)(2,1)} %param.9) | copy-start | bytes 41476
  2.4 11.7 %copy-start.4 = (bf16[3,3,3,32,8]{3,4,2,1,0:T(8,128)(2,1)S(1)}, bf16[3,3,3,32,8]{3,4,2,1,0:T(8,128)(2,1)}, u32[]{:S(2)}) copy-start(bf16[3,3,3,32,8]{3,4,2,1,0:T(8,128)(2,1)} %param.7) | copy-start | bytes 41476
  3.1 11.2 %copy-start.2 = (bf16[3,3,3,32,32]{4,3,2,1,0:T(8,128)(2,1)S(1)}, bf16[3,3,3,32,32]{4,3,2,1,0:T(8,128)(2,1)}, u32[]{:S(2)}) copy-start(bf16[3,3,3,32,32]{4,3,2,1,0:T(8,128)(2,1)} %param.8) | copy-start | bytes 165892
  3.2 13.7 %collective-permute-start = (bf16[4,4,16,128]{3,2,1,0:T(8,128)(2,1)S(1)}, bf16[4,4,16,128]{3,2,1,0:T(8,128)(2,1)S(1)}, u32[]{:S(2)}, u32[]{:S(2)}) collective-permute-start(bf16[4,4,16,128]{3,2,1,0:T(8,128)(2,1)S(1)} %get-tuple-element.24), channel_id=1, source_target_pairs={{0,1},{1,2},{2,3},{3,4},{4,5},{5,6},{6,7},{7,8},{8,9},{9,10},{10,1... | collective-permute-start | bytes 196616 | tf_op jit(solution)/shard_map/ppermute | solution.py:24
  12.1 9.3 %collective-permute-start.1 = (bf16[4,2,16,128]{3,2,1,0:T(8,128)(2,1)S(1)}, bf16[4,2,16,128]{3,2,1,0:T(8,128)(2,1)S(1)}, u32[]{:S(2)}, u32[]{:S(2)}) collective-permute-start(bf16[4,2,16,128]{3,2,1,0:T(8,128)(2,1)S(1)} %get-tuple-element.25), channel_id=1, source_target_pairs={{0,15},{1,0},{2,1},{3,2},{4,3},{5,4},{6,5},{7,6},{8,7},{9,8},{10,9... | collective-permute-start | bytes 98312 | tf_op jit(solution)/shard_map/ppermute | solution.py:24
  14.5 0.7 copy-start.5
  21.5 15.8 %collective-permute-start.2 = (bf16[48,16,128]{2,1,0:T(8,128)(2,1)S(1)}, bf16[48,16,128]{2,1,0:T(8,128)(2,1)S(1)}, u32[]{:S(2)}, u32[]{:S(2)}) collective-permute-start(bf16[48,16,128]{2,1,0:T(8,128)(2,1)S(1)} %pad_maximum_fusion.1), channel_id=1, source_target_pairs={{0,16},{16,32},{32,48},{48,64},{64,80},{80,96},{96,112},{112,128},... | collective-permute-start | bytes 589832 | tf_op jit(solution)/shard_map/ppermute | solution.py:24
  24.1 12.1 %collective-permute-start.3 = (bf16[26,16,128]{2,1,0:T(8,128)(2,1)S(1)}, bf16[26,16,128]{2,1,0:T(8,128)(2,1)S(1)}, u32[]{:S(2)}, u32[]{:S(2)}) collective-permute-start(bf16[26,16,128]{2,1,0:T(8,128)(2,1)S(1)} %bitcast.247), channel_id=1, source_target_pairs={{0,496},{16,0},{32,16},{48,32},{64,48},{80,64},{96,80},{112,96},{1... | collective-permute-start | bytes 319496 | tf_op jit(solution)/shard_map/ppermute | solution.py:24
  40.9 10.9 %all-to-all-start = ((f32[8,48,128]{2,1,0:T(8,128)}), f32[8,48,128]{2,1,0:T(8,128)S(1)}, u32[]{:S(2)}, u32[]{:S(2)}) async-start(f32[8,48,128]{2,1,0:T(8,128)} %get-tuple-element.28), calls=%async_computation | async-start | bytes 393216 | tf_op jit(solution)/shard_map/all_to_all | solution.py:342
  52.5 14.5 %all-to-all-start.1 = ((f32[8,48,128]{2,1,0:T(8,128)}), f32[8,48,128]{2,1,0:T(8,128)S(1)}, u32[]{:S(2)}, u32[]{:S(2)}) async-start(f32[8,48,128]{2,1,0:T(8,128)} %shard_map.97), calls=%async_computation.1 | async-start | bytes 393216 | tf_op jit(solution)/shard_map/all_to_all | solution.py:342
  57.4 16.5 %collective-permute-start.5 = (bf16[6,32,128]{2,1,0:T(8,128)(2,1)S(1)}, bf16[6,32,128]{2,1,0:T(8,128)(2,1)S(1)}, u32[]{:S(2)}, u32[]{:S(2)}) collective-permute-start(bf16[6,32,128]{2,1,0:T(8,128)(2,1)S(1)} %get-tuple-element.30), channel_id=1, source_target_pairs={{0,15},{1,0},{2,1},{3,2},{4,3},{5,4},{6,5},{7,6},{8,7},{9,8},{10,9... | collective-permute-start | bytes 147464 | tf_op jit(solution)/shard_map/ppermute | solution.py:24
  60.6 13.4 %collective-permute-start.4 = (bf16[2,32,128]{2,1,0:T(8,128)(2,1)S(1)}, bf16[2,32,128]{2,1,0:T(8,128)(2,1)S(1)}, u32[]{:S(2)}, u32[]{:S(2)}) collective-permute-start(bf16[2,32,128]{2,1,0:T(8,128)(2,1)S(1)} %get-tuple-element.29), channel_id=1, source_target_pairs={{0,1},{1,2},{2,3},{3,4},{4,5},{5,6},{6,7},{7,8},{8,9},{9,10},{10,1... | collective-permute-start | bytes 49160 | tf_op jit(solution)/shard_map/ppermute | solution.py:24
  67.7 15.9 %all-to-all-start.2 = ((f32[8,48,128]{2,1,0:T(8,128)}), f32[8,48,128]{2,1,0:T(8,128)S(1)}, u32[]{:S(2)}, u32[]{:S(2)}) async-start(f32[8,48,128]{2,1,0:T(8,128)} %shard_map.98), calls=%async_computation.2 | async-start | bytes 393216 | tf_op jit(solution)/shard_map/all_to_all | solution.py:342
  74.0 16.5 %collective-permute-start.7 = (bf16[19,32,128]{2,1,0:T(8,128)(2,1)S(1)}, bf16[19,32,128]{2,1,0:T(8,128)(2,1)S(1)}, u32[]{:S(2)}, u32[]{:S(2)}) collective-permute-start(bf16[19,32,128]{2,1,0:T(8,128)(2,1)S(1)} %get-tuple-element.32), channel_id=1, source_target_pairs={{0,496},{16,0},{32,16},{48,32},{64,48},{80,64},{96,80},{112,96},{1... | collective-permute-start | bytes 466952 | tf_op jit(solution)/shard_map/ppermute | solution.py:24
  81.7 8.8 %collective-permute-start.6 = (bf16[7,32,128]{2,1,0:T(8,128)(2,1)S(1)}, bf16[7,32,128]{2,1,0:T(8,128)(2,1)S(1)}, u32[]{:S(2)}, u32[]{:S(2)}) collective-permute-start(bf16[7,32,128]{2,1,0:T(8,128)(2,1)S(1)} %get-tuple-element.31), channel_id=1, source_target_pairs={{0,16},{16,32},{32,48},{48,64},{64,80},{80,96},{96,112},{112,128},... | collective-permute-start | bytes 172040 | tf_op jit(solution)/shard_map/ppermute | solution.py:24
  84.3 9.2 %all-to-all-start.3 = ((bf16[8,48,128]{2,1,0:T(8,128)(2,1)}), bf16[8,48,128]{2,1,0:T(8,128)(2,1)S(1)}, u32[]{:S(2)}, u32[]{:S(2)}) async-start(bf16[8,48,128]{2,1,0:T(8,128)(2,1)} %shard_map.99), calls=%async_computation.3 | async-start | bytes 196608 | tf_op jit(solution)/shard_map/all_to_all | solution.py:342

commit v6 on v5

--- a/solution.py
+++ b/solution.py
@@ -64,16 +64,21 @@
     return (s == source).astype(F32).astype(BF)
 
 
-def to_slabs_kernel(f_ref, g_ref, f_out, g_out, up_out, down_out):
-    halves = split_z()
-    order = slab_order(0)
-    for ref, out in ((f_ref, f_out), (g_ref, g_out)):
-        z = dot(ref[...], halves).astype(BF)
-        z = jnp.concatenate([z[:, :LANES], z[:, LANES:]], 0)
-        out[...] = dot(order, z).astype(BF).reshape(4, 8, 16, LANES)
-    up_out[:, 0:3] = f_out[:, 5:8]
+def to_slabs(ref):
+    z = dot(ref[...], split_z()).astype(BF)
+    z = jnp.concatenate([z[:, :LANES], z[:, LANES:]], 0)
+    return dot(slab_order(0), z).astype(BF).reshape(4, 8, 16, LANES)
+
+
+def fields_kernel(f_ref, f_out, down_out):
+    f_out[...] = to_slabs(f_ref)
+    down_out[...] = f_out[:, 0:2]
+
+
+def cotangent_kernel(g_ref, f_ref, g_out, up_out):
+    g_out[...] = to_slabs(g_ref)
+    up_out[:, 0:3] = f_ref[:, 5:8]
     up_out[:, 3:4] = g_out[:, 7:8]
-    down_out[...] = f_out[:, 0:2]
 
 
 def rolled_odd(slab):
@@ -362,12 +367,11 @@
     wu = up_weights(w_up)
     wv = up_weights(w_down_swapped)
 
-    f, g, up, down = call(
-        to_slabs_kernel,
-        [((4, 8, 16, LANES), BF)] * 2 + [((4, 4, 16, LANES), BF), ((4, 2, 16, LANES), BF)],
-        [fields.reshape(256, 256), cotangent.reshape(256, 256)],
-    )
-    ylo, yhi = shift(up, GY, 1), shift(down, GY, -1)
+    slabs = ((4, 8, 16, LANES), BF)
+    f, down = call(fields_kernel, [slabs, ((4, 2, 16, LANES), BF)], [fields.reshape(256, 256)])
+    yhi = shift(down, GY, -1)
+    g, up = call(cotangent_kernel, [slabs, ((4, 4, 16, LANES), BF)], [cotangent.reshape(256, 256), f], flops=10**10)
+    ylo = shift(up, GY, 1)
     f_ext = jnp.concatenate([ylo[:, :3], f, yhi], 1)
     last = jnp.concatenate([f_ext[1:].reshape(39, 16, LANES), ylo[3, 3:4], g[3]], 0)
     xlo = shift(last, GX, 1)

time: 95.2 us -> 95.1 us (level)
    pallas_call x9 -> x10, Pallas kernels: 10.2 us -> 10.6 us  [call(): pl.pallas_call(body, out_shape=[jax.ShapeDtypeStruct(s, d) for s, d in ou...]
where the time goes in v6:
time: 95.1 us; the launch traced here: 94.3 us
  starting transfers between devices  63.1 us (66%)
  waiting for transfers between devices  15.4 us (16%)
  Pallas kernels  10.6 us (11%)
  local copies, waits for them, and re-layouts  3.75 us (4%)
  between operations  1.07 us (1%)
    ppermute x8, starting transfers between devices, shift(): lax.ppermute(x, axis, [(i, (i + by) % devices) for i in range(devices)])  42.7 us
    all_to_all x4, starting transfers between devices, exchange(): return lax.all_to_all(part, axes, 0, 0, tiled=True)  20.3 us
    pallas_call x10, Pallas kernels, call(): pl.pallas_call(body, out_shape=[jax.ShapeDtypeStruct(s, d) for s, d in ou...  10.6 us
    ppermute x8, waiting for transfers between devices, shift(): lax.ppermute(x, axis, [(i, (i + by) % devices) for i in range(devices)])  9.36 us
    all_to_all x4, waiting for transfers between devices, exchange(): return lax.all_to_all(part, axes, 0, 0, tiled=True)  6.04 us
    unnamed x37, local copies, waits for them, and re-layouts  2 us
  transfers between devices with their start and end apart: 12, of which 6 were waited for; matrix products, arithmetic and copies ran while one was open for 2% of the time, Pallas kernels for 4%

profile of v6, /device:TPU:1, one launch (start us, length us, event | category | flops | bytes accessed | tf_op | source)
XLA Modules:
  0.0 94.3 jit_solution(9218731082325902826)
XLA Ops:
  0.6 0.9 copy-done
  1.5 0.6 shard_map.92
  2.1 0.3 copy-done.1
  2.4 0.6 shard_map.93
  3.0 9.0 %collective-permute-start = (bf16[4,4,16,128]{3,2,1,0:T(8,128)(2,1)S(1)}, bf16[4,4,16,128]{3,2,1,0:T(8,128)(2,1)S(1)}, u32[]{:S(2)}, u32[]{:S(2)}) collective-permute-start(bf16[4,4,16,128]{3,2,1,0:T(8,128)(2,1)S(1)} %get-tuple-element.24), channel_id=1, source_target_pairs={{0,1},{1,2},{2,3},{3,4},{4,5},{5,6},{6,7},{7,8},{8,9},{9,10},{10,1... | collective-permute-start | bytes 196616 | tf_op jit(solution)/shard_map/ppermute | solution.py:24
  12.0 1.9 %collective-permute-start.1 = (bf16[4,2,16,128]{3,2,1,0:T(8,128)(2,1)S(1)}, bf16[4,2,16,128]{3,2,1,0:T(8,128)(2,1)S(1)}, u32[]{:S(2)}, u32[]{:S(2)}) collective-permute-start(bf16[4,2,16,128]{3,2,1,0:T(8,128)(2,1)S(1)} %get-tuple-element.25), channel_id=1, source_target_pairs={{0,15},{1,0},{2,1},{3,2},{4,3},{5,4},{6,5},{7,6},{8,7},{9,8},{10,9... | collective-permute-start | bytes 98312 | tf_op jit(solution)/shard_map/ppermute | solution.py:24
  14.2 0.1 copy.54.wb
  14.4 0.6 copy-done.5
  15.8 0.2 copy.41
  16.0 0.2 reshape.54.wm
  16.7 4.5 %collective-permute-done.1.yhi = bf16[4,2,16,128]{3,2,1,0:T(8,128)(2,1)S(1)} collective-permute-done((bf16[4,2,16,128]{3,2,1,0:T(8,128)(2,1)S(1)}, bf16[4,2,16,128]{3,2,1,0:T(8,128)(2,1)S(1)}, u32[]{:S(2)}, u32[]{:S(2)}) %collective-permute-start.1) | collective-permute-done | bytes 32800 | tf_op jit(solution)/shard_map/ppermute | solution.py:24
  21.3 2.6 %collective-permute-start.2 = (bf16[48,16,128]{2,1,0:T(8,128)(2,1)S(1)}, bf16[48,16,128]{2,1,0:T(8,128)(2,1)S(1)}, u32[]{:S(2)}, u32[]{:S(2)}) collective-permute-start(bf16[48,16,128]{2,1,0:T(8,128)(2,1)S(1)} %pad_maximum_fusion.1), channel_id=1, source_target_pairs={{0,16},{16,32},{32,48},{48,64},{64,80},{80,96},{96,112},{112,128},... | collective-permute-start | bytes 589832 | tf_op jit(solution)/shard_map/ppermute | solution.py:24
  23.9 10.4 %collective-permute-start.3 = (bf16[26,16,128]{2,1,0:T(8,128)(2,1)S(1)}, bf16[26,16,128]{2,1,0:T(8,128)(2,1)S(1)}, u32[]{:S(2)}, u32[]{:S(2)}) collective-permute-start(bf16[26,16,128]{2,1,0:T(8,128)(2,1)S(1)} %bitcast.247), channel_id=1, source_target_pairs={{0,496},{16,0},{32,16},{48,32},{64,48},{80,64},{96,80},{112,96},{1... | collective-permute-start | bytes 319496 | tf_op jit(solution)/shard_map/ppermute | solution.py:24
  34.3 1.7 %collective-permute-done.3.xhi = bf16[26,16,128]{2,1,0:T(8,128)(2,1)S(1)} collective-permute-done((bf16[26,16,128]{2,1,0:T(8,128)(2,1)S(1)}, bf16[26,16,128]{2,1,0:T(8,128)(2,1)S(1)}, u32[]{:S(2)}, u32[]{:S(2)}) %collective-permute-start.3) | collective-permute-done | bytes 106528 | tf_op jit(solution)/shard_map/ppermute | solution.py:24
  36.0 1.1 %collective-permute-done.2.xlo = bf16[48,16,128]{2,1,0:T(8,128)(2,1)S(1)} collective-permute-done((bf16[48,16,128]{2,1,0:T(8,128)(2,1)S(1)}, bf16[48,16,128]{2,1,0:T(8,128)(2,1)S(1)}, u32[]{:S(2)}, u32[]{:S(2)}) %collective-permute-start.2) | collective-permute-done | bytes 196640 | tf_op jit(solution)/shard_map/ppermute | solution.py:24
  37.2 3.6 %shard_map.94 = (f32[8,48,128]{2,1,0:T(8,128)}, f32[15,32,128]{2,1,0:T(8,128)S(1)}, bf16[32,1024]{1,0:T(8,128)(2,1)S(1)}, bf16[32,1024]{1,0:T(8,128)(2,1)S(1)}) custom-call(bf16[4,8,16,128]{3,2,1,0:T(8,128)(2,1)S(1)} %get-tuple-element.22.f_ref, bf16[4,8,16,128]{3,2,1,0:T(8,128)(2,1)S(1)} %get-tuple-element.23.g_ref, ...), custom_call_target="tpu_custom_call" | custom-call | flops 100000000 | bytes 2000000 | tf_op jit(solution)/shard_map/pallas_call | solution.py:29
  40.8 5.0 %all-to-all-start = ((f32[8,48,128]{2,1,0:T(8,128)}), f32[8,48,128]{2,1,0:T(8,128)S(1)}, u32[]{:S(2)}, u32[]{:S(2)}) async-start(f32[8,48,128]{2,1,0:T(8,128)} %get-tuple-element.28), calls=%async_computation | async-start | bytes 393216 | tf_op jit(solution)/shard_map/all_to_all | solution.py:347
  45.8 5.8 %all-to-all-done.after.got = f32[8,48,128]{2,1,0:T(8,128)S(1)} async-done(((f32[8,48,128]{2,1,0:T(8,128)}), f32[8,48,128]{2,1,0:T(8,128)S(1)}, u32[]{:S(2)}, u32[]{:S(2)}) %all-to-all-start) | async-done | bytes 196640 | tf_op jit(solution)/shard_map/all_to_all | solution.py:347
  51.7 0.7 shard_map.98
  52.4 4.9 %all-to-all-start.1 = ((f32[8,48,128]{2,1,0:T(8,128)}), f32[8,48,128]{2,1,0:T(8,128)S(1)}, u32[]{:S(2)}, u32[]{:S(2)}) async-start(f32[8,48,128]{2,1,0:T(8,128)} %shard_map.98), calls=%async_computation.1 | async-start | bytes 393216 | tf_op jit(solution)/shard_map/all_to_all | solution.py:347
  57.3 3.1 %collective-permute-start.5 = (bf16[6,32,128]{2,1,0:T(8,128)(2,1)S(1)}, bf16[6,32,128]{2,1,0:T(8,128)(2,1)S(1)}, u32[]{:S(2)}, u32[]{:S(2)}) collective-permute-start(bf16[6,32,128]{2,1,0:T(8,128)(2,1)S(1)} %get-tuple-element.30), channel_id=1, source_target_pairs={{0,15},{1,0},{2,1},{3,2},{4,3},{5,4},{6,5},{7,6},{8,7},{9,8},{10,9... | collective-permute-start | bytes 147464 | tf_op jit(solution)/shard_map/ppermute | solution.py:24
  60.5 6.3 %collective-permute-start.4 = (bf16[2,32,128]{2,1,0:T(8,128)(2,1)S(1)}, bf16[2,32,128]{2,1,0:T(8,128)(2,1)S(1)}, u32[]{:S(2)}, u32[]{:S(2)}) collective-permute-start(bf16[2,32,128]{2,1,0:T(8,128)(2,1)S(1)} %get-tuple-element.29), channel_id=1, source_target_pairs={{0,1},{1,2},{2,3},{3,4},{4,5},{5,6},{6,7},{7,8},{8,9},{9,10},{10,1... | collective-permute-start | bytes 49160 | tf_op jit(solution)/shard_map/ppermute | solution.py:24
  66.9 0.7 shard_map.99
  67.6 6.2 %all-to-all-start.2 = ((f32[8,48,128]{2,1,0:T(8,128)}), f32[8,48,128]{2,1,0:T(8,128)S(1)}, u32[]{:S(2)}, u32[]{:S(2)}) async-start(f32[8,48,128]{2,1,0:T(8,128)} %shard_map.99), calls=%async_computation.2 | async-start | bytes 393216 | tf_op jit(solution)/shard_map/all_to_all | solution.py:347
  73.9 7.5 %collective-permute-start.7 = (bf16[19,32,128]{2,1,0:T(8,128)(2,1)S(1)}, bf16[19,32,128]{2,1,0:T(8,128)(2,1)S(1)}, u32[]{:S(2)}, u32[]{:S(2)}) collective-permute-start(bf16[19,32,128]{2,1,0:T(8,128)(2,1)S(1)} %get-tuple-element.32), channel_id=1, source_target_pairs={{0,496},{16,0},{32,16},{48,32},{64,48},{80,64},{96,80},{112,96},{1... | collective-permute-start | bytes 466952 | tf_op jit(solution)/shard_map/ppermute | solution.py:24
  81.5 1.9 %collective-permute-start.6 = (bf16[7,32,128]{2,1,0:T(8,128)(2,1)S(1)}, bf16[7,32,128]{2,1,0:T(8,128)(2,1)S(1)}, u32[]{:S(2)}, u32[]{:S(2)}) collective-permute-start(bf16[7,32,128]{2,1,0:T(8,128)(2,1)S(1)} %get-tuple-element.31), channel_id=1, source_target_pairs={{0,16},{16,32},{32,48},{48,64},{64,80},{80,96},{96,112},{112,128},... | collective-permute-start | bytes 172040 | tf_op jit(solution)/shard_map/ppermute | solution.py:24
  83.5 0.7 shard_map.100
  84.1 4.2 %all-to-all-start.3 = ((bf16[8,48,128]{2,1,0:T(8,128)(2,1)}), bf16[8,48,128]{2,1,0:T(8,128)(2,1)S(1)}, u32[]{:S(2)}, u32[]{:S(2)}) async-start(bf16[8,48,128]{2,1,0:T(8,128)(2,1)} %shard_map.100), calls=%async_computation.3 | async-start | bytes 196608 | tf_op jit(solution)/shard_map/all_to_all | solution.py:347
  88.3 2.0 %collective-permute-done.6.xlo = bf16[7,32,128]{2,1,0:T(8,128)(2,1)S(1)} collective-permute-done((bf16[7,32,128]{2,1,0:T(8,128)(2,1)S(1)}, bf16[7,32,128]{2,1,0:T(8,128)(2,1)S(1)}, u32[]{:S(2)}, u32[]{:S(2)}) %collective-permute-start.6) | collective-permute-done | bytes 57376 | tf_op jit(solution)/shard_map/ppermute | solution.py:24
  90.4 2.8 %shard_map.97 = (bf16[256,256]{1,0:T(8,128)(2,1)}, bf16[256,256]{1,0:T(8,128)(2,1)}) custom-call(bf16[4,8,16,128]{3,2,1,0:T(8,128)(2,1)S(1)} %get-tuple-element.22.f_ref, bf16[4,8,16,128]{3,2,1,0:T(8,128)(2,1)S(1)} %get-tuple-element.23.g_ref, bf16[32,1024]{1,0:T(8,128)(2,1)S(1)} %get-tuple-element.26.h2, bf16[32,1024]{1,0:T(8,128)(2,1)S(1)} %get-tuple-element.27.d2, ...), custom_call_target="tpu_custom_call" | custom-call | flops 10000000000 | bytes 2000000 | tf_op jit(solution)/shard_map/pallas_call | solution.py:29
  93.1 0.2 all-to-all-done.3.total
  93.3 1.0 %shard_map.101 = (f32[27,8,32]{2,1,0:T(8,128)}, f32[27,32,32]{2,1,0:T(8,128)}, f32[27,8,32]{2,1,0:T(8,128)}) custom-call(bf16[8,48,128]{2,1,0:T(8,128)(2,1)S(1)} %all-to-all-done.3.total), custom_call_target="tpu_custom_call" | custom-call | flops 100000000 | bytes 2000000 | tf_op jit(solution)/shard_map/pallas_call | solution.py:29
  (85 shorter events, 1.9 us)
Async XLA Ops:
  0.6 0.9 copy-start
  1.5 0.9 copy-start.1
  2.4 11.5 %copy-start.3 = (bf16[3,3,3,8,32]{4,3,2,1,0:T(8,128)(2,1)S(1)}, bf16[3,3,3,8,32]{4,3,2,1,0:T(8,128)(2,1)}, u32[]{:S(2)}) copy-start(bf16[3,3,3,8,32]{4,3,2,1,0:T(8,128)(2,1)} %param.9) | copy-start | bytes 41476
  2.4 11.5 %copy-start.4 = (bf16[3,3,3,32,8]{3,4,2,1,0:T(8,128)(2,1)S(1)}, bf16[3,3,3,32,8]{3,4,2,1,0:T(8,128)(2,1)}, u32[]{:S(2)}) copy-start(bf16[3,3,3,32,8]{3,4,2,1,0:T(8,128)(2,1)} %param.7) | copy-start | bytes 41476
  3.0 11.2 %copy-start.2 = (bf16[3,3,3,32,32]{4,3,2,1,0:T(8,128)(2,1)S(1)}, bf16[3,3,3,32,32]{4,3,2,1,0:T(8,128)(2,1)}, u32[]{:S(2)}) copy-start(bf16[3,3,3,32,32]{4,3,2,1,0:T(8,128)(2,1)} %param.8) | copy-start | bytes 165892
  3.0 13.7 %collective-permute-start = (bf16[4,4,16,128]{3,2,1,0:T(8,128)(2,1)S(1)}, bf16[4,4,16,128]{3,2,1,0:T(8,128)(2,1)S(1)}, u32[]{:S(2)}, u32[]{:S(2)}) collective-permute-start(bf16[4,4,16,128]{3,2,1,0:T(8,128)(2,1)S(1)} %get-tuple-element.24), channel_id=1, source_target_pairs={{0,1},{1,2},{2,3},{3,4},{4,5},{5,6},{6,7},{7,8},{8,9},{9,10},{10,1... | collective-permute-start | bytes 196616 | tf_op jit(solution)/shard_map/ppermute | solution.py:24
  12.0 9.2 %collective-permute-start.1 = (bf16[4,2,16,128]{3,2,1,0:T(8,128)(2,1)S(1)}, bf16[4,2,16,128]{3,2,1,0:T(8,128)(2,1)S(1)}, u32[]{:S(2)}, u32[]{:S(2)}) collective-permute-start(bf16[4,2,16,128]{3,2,1,0:T(8,128)(2,1)S(1)} %get-tuple-element.25), channel_id=1, source_target_pairs={{0,15},{1,0},{2,1},{3,2},{4,3},{5,4},{6,5},{7,6},{8,7},{9,8},{10,9... | collective-permute-start | bytes 98312 | tf_op jit(solution)/shard_map/ppermute | solution.py:24
  14.3 0.7 copy-start.5
  21.3 15.8 %collective-permute-start.2 = (bf16[48,16,128]{2,1,0:T(8,128)(2,1)S(1)}, bf16[48,16,128]{2,1,0:T(8,128)(2,1)S(1)}, u32[]{:S(2)}, u32[]{:S(2)}) collective-permute-start(bf16[48,16,128]{2,1,0:T(8,128)(2,1)S(1)} %pad_maximum_fusion.1), channel_id=1, source_target_pairs={{0,16},{16,32},{32,48},{48,64},{64,80},{80,96},{96,112},{112,128},... | collective-permute-start | bytes 589832 | tf_op jit(solution)/shard_map/ppermute | solution.py:24
  23.9 12.1 %collective-permute-start.3 = (bf16[26,16,128]{2,1,0:T(8,128)(2,1)S(1)}, bf16[26,16,128]{2,1,0:T(8,128)(2,1)S(1)}, u32[]{:S(2)}, u32[]{:S(2)}) collective-permute-start(bf16[26,16,128]{2,1,0:T(8,128)(2,1)S(1)} %bitcast.247), channel_id=1, source_target_pairs={{0,496},{16,0},{32,16},{48,32},{64,48},{80,64},{96,80},{112,96},{1... | collective-permute-start | bytes 319496 | tf_op jit(solution)/shard_map/ppermute | solution.py:24
  40.8 10.9 %all-to-all-start = ((f32[8,48,128]{2,1,0:T(8,128)}), f32[8,48,128]{2,1,0:T(8,128)S(1)}, u32[]{:S(2)}, u32[]{:S(2)}) async-start(f32[8,48,128]{2,1,0:T(8,128)} %get-tuple-element.28), calls=%async_computation | async-start | bytes 393216 | tf_op jit(solution)/shard_map/all_to_all | solution.py:347
  52.4 14.6 %all-to-all-start.1 = ((f32[8,48,128]{2,1,0:T(8,128)}), f32[8,48,128]{2,1,0:T(8,128)S(1)}, u32[]{:S(2)}, u32[]{:S(2)}) async-start(f32[8,48,128]{2,1,0:T(8,128)} %shard_map.98), calls=%async_computation.1 | async-start | bytes 393216 | tf_op jit(solution)/shard_map/all_to_all | solution.py:347
  57.3 16.5 %collective-permute-start.5 = (bf16[6,32,128]{2,1,0:T(8,128)(2,1)S(1)}, bf16[6,32,128]{2,1,0:T(8,128)(2,1)S(1)}, u32[]{:S(2)}, u32[]{:S(2)}) collective-permute-start(bf16[6,32,128]{2,1,0:T(8,128)(2,1)S(1)} %get-tuple-element.30), channel_id=1, source_target_pairs={{0,15},{1,0},{2,1},{3,2},{4,3},{5,4},{6,5},{7,6},{8,7},{9,8},{10,9... | collective-permute-start | bytes 147464 | tf_op jit(solution)/shard_map/ppermute | solution.py:24
  60.5 13.4 %collective-permute-start.4 = (bf16[2,32,128]{2,1,0:T(8,128)(2,1)S(1)}, bf16[2,32,128]{2,1,0:T(8,128)(2,1)S(1)}, u32[]{:S(2)}, u32[]{:S(2)}) collective-permute-start(bf16[2,32,128]{2,1,0:T(8,128)(2,1)S(1)} %get-tuple-element.29), channel_id=1, source_target_pairs={{0,1},{1,2},{2,3},{3,4},{4,5},{5,6},{6,7},{7,8},{8,9},{9,10},{10,1... | collective-permute-start | bytes 49160 | tf_op jit(solution)/shard_map/ppermute | solution.py:24
  67.6 15.8 %all-to-all-start.2 = ((f32[8,48,128]{2,1,0:T(8,128)}), f32[8,48,128]{2,1,0:T(8,128)S(1)}, u32[]{:S(2)}, u32[]{:S(2)}) async-start(f32[8,48,128]{2,1,0:T(8,128)} %shard_map.99), calls=%async_computation.2 | async-start | bytes 393216 | tf_op jit(solution)/shard_map/all_to_all | solution.py:347
  73.9 16.5 %collective-permute-start.7 = (bf16[19,32,128]{2,1,0:T(8,128)(2,1)S(1)}, bf16[19,32,128]{2,1,0:T(8,128)(2,1)S(1)}, u32[]{:S(2)}, u32[]{:S(2)}) collective-permute-start(bf16[19,32,128]{2,1,0:T(8,128)(2,1)S(1)} %get-tuple-element.32), channel_id=1, source_target_pairs={{0,496},{16,0},{32,16},{48,32},{64,48},{80,64},{96,80},{112,96},{1... | collective-permute-start | bytes 466952 | tf_op jit(solution)/shard_map/ppermute | solution.py:24
  81.5 8.8 %collective-permute-start.6 = (bf16[7,32,128]{2,1,0:T(8,128)(2,1)S(1)}, bf16[7,32,128]{2,1,0:T(8,128)(2,1)S(1)}, u32[]{:S(2)}, u32[]{:S(2)}) collective-permute-start(bf16[7,32,128]{2,1,0:T(8,128)(2,1)S(1)} %get-tuple-element.31), channel_id=1, source_target_pairs={{0,16},{16,32},{32,48},{48,64},{64,80},{80,96},{96,112},{112,128},... | collective-permute-start | bytes 172040 | tf_op jit(solution)/shard_map/ppermute | solution.py:24
  84.1 9.2 %all-to-all-start.3 = ((bf16[8,48,128]{2,1,0:T(8,128)(2,1)}), bf16[8,48,128]{2,1,0:T(8,128)(2,1)S(1)}, u32[]{:S(2)}, u32[]{:S(2)}) async-start(bf16[8,48,128]{2,1,0:T(8,128)(2,1)} %shard_map.100), calls=%async_computation.3 | async-start | bytes 196608 | tf_op jit(solution)/shard_map/all_to_all | solution.py:347
